TPU v7x, 1024 devices: a whole 8x8x8 slice. The times are simulated.
1024 devices in a mesh: blk: 256 (over z_lo, y, x, core), head: 4 (over z_hi).
Axes of the slice: x: 8, y: 8, z: 8 (z_hi: 4, z_lo: 2; z = z_hi * 2 + z_lo), core: 2. Of those that a mesh axis runs over, the one named last changes fastest.
Arguments:
- image_feats: bfloat16 [81920, 768], P('blk'), may hold values from -6 to 6
- text_feats: bfloat16 [81920, 768], P('blk'), may hold values from -6 to 6
- image_head: bfloat16 [768, 768], P(None, 'head'), may hold values from -0.21875 to 0.21875
- text_head: bfloat16 [768, 768], P(None, 'head'), may hold values from -0.21875 to 0.21875
Outputs:
- image_grad: bfloat16 [81920, 768], P('blk', 'head')
- text_grad: bfloat16 [81920, 768], P('blk', 'head')
- row_loss: float32 [81920], P(('blk', 'head'))
All inputs are finite; a program needn't handle non-finite values.
Results may differ from a plain program's by a relative error of at most 0.024.
Values may be sent and summed in bfloat16 or wider, within the bound.
No kernel may reach another device: no remote copies, remote signals or barrier semaphores. Data moves between devices by JAX's collectives and lax.ppermute only.
A program may use at most 32 MiB of HBM per device.

v0:
```python
import jax
import jax.numpy as jnp
from jax import lax
from jax.sharding import PartitionSpec as P

STEPS = 4


logit_scale = 10.0
logit_bias = -2.0
epsilon = 1e-06


def passed_along(block, axis, distance):
    devices = range(lax.axis_size(axis))
    route = [((i - distance) % len(devices), i) for i in devices]
    return lax.ppermute(block, axis, route)


def inner(left, right):
    return lax.dot_general(
        left, right, (((1,), (1,)), ((), ())), preferred_element_type=jnp.float32
    )


def outer_sum(left, right):
    return lax.dot_general(
        left, right, (((0,), (0,)), ((), ())), preferred_element_type=jnp.float32
    )


def sign_table(row_ids, columns, step):
    if step == 0:
        return jnp.where(row_ids[:, None] == columns[None, :], 1.0, -1.0).astype(jnp.float32)
    return -jnp.ones((row_ids.shape[0], columns.shape[0]), jnp.float32)


def body(image_feats, text_feats, image_head, text_head):
    rows = image_feats.shape[0]
    part_width = image_head.shape[1]
    groups = lax.axis_size("head")
    group = lax.axis_index("head")
    quarter = rows // groups
    z_image = jnp.dot(image_feats, image_head, preferred_element_type=jnp.float32)
    z_text = jnp.dot(text_feats, text_head, preferred_element_type=jnp.float32)
    sq_image, sq_text = lax.psum(
        (jnp.sum(z_image * z_image, axis=1), jnp.sum(z_text * z_text, axis=1)), "head"
    )
    n_image = jnp.sqrt(sq_image + epsilon)[:, None]
    n_text = jnp.sqrt(sq_text + epsilon)[:, None]
    u_image = (z_image / n_image).astype(jnp.bfloat16)
    u_text = (z_text / n_text).astype(jnp.bfloat16)
    moving = u_text
    columns = jnp.arange(rows, dtype=jnp.int32)
    g_image = jnp.zeros((rows, part_width), jnp.float32)
    losses = jnp.zeros((rows,), jnp.float32)
    carried = jnp.zeros((rows, part_width), jnp.float32)
    for step in range(STEPS):
        if step > 0:
            moving, carried = (
                passed_along(moving, "blk", -1),
                passed_along(carried.astype(jnp.bfloat16), "blk", -1).astype(carried.dtype),
            )
        summed = lax.psum(inner(u_image, moving).astype(jnp.bfloat16), "head").astype(jnp.float32)
        logits = logit_scale * summed + logit_bias
        signs = sign_table(columns, columns, step)
        losses = losses + jnp.sum(jax.nn.softplus(-signs * logits), axis=1)
        weights = (-signs * jax.nn.sigmoid(-signs * logits) * logit_scale).astype(jnp.bfloat16)
        g_image = g_image + jnp.dot(weights, moving, preferred_element_type=jnp.float32)
        share = outer_sum(weights, u_image)
        carried = carried + share
    g_text = passed_along(carried.astype(jnp.bfloat16), "blk", STEPS - 1).astype(carried.dtype)
    row_loss = lax.dynamic_slice_in_dim(losses, group * quarter, quarter, 0)
    dot_image, dot_text = lax.psum(
        (jnp.sum(g_image * z_image, axis=1), jnp.sum(g_text * z_text, axis=1)), "head"
    )
    dz_image = (g_image / n_image - z_image * (dot_image[:, None] / n_image**3)).astype(
        jnp.bfloat16
    )
    dz_text = (g_text / n_text - z_text * (dot_text[:, None] / n_text**3)).astype(jnp.bfloat16)
    image_grad, text_grad = (
        lax.psum_scatter(
            inner(dz_image, image_head).astype(jnp.bfloat16),
            "head",
            scatter_dimension=1,
            tiled=True,
        ).astype(jnp.float32),
        lax.psum_scatter(
            inner(dz_text, text_head).astype(jnp.bfloat16), "head", scatter_dimension=1, tiled=True
        ).astype(jnp.float32),
    )
    return (image_grad.astype(jnp.bfloat16), text_grad.astype(jnp.bfloat16), row_loss)


def solution(mesh):
    in_specs = (P("blk", None), P("blk", None), P(None, "head"), P(None, "head"))
    out_specs = (P("blk", "head"), P("blk", "head"), P(("blk", "head")))
    return jax.shard_map(body, mesh=mesh, in_specs=in_specs, out_specs=out_specs, check_vma=False)
```

profile of v0, /device:TPU:1, one launch (start us, length us, event | category | flops | bytes accessed | tf_op | source)
XLA Modules:
  0.0 262.9 jit_solution(13373890174411547436)
XLA Ops:
  7.2 0.0 copy-start
  7.2 0.0 copy-start.1
  7.2 0.0 copy-start.2
  7.2 0.0 all-reduce.5.cloned.1.call-start
  7.2 1.0 copy-done
  8.2 1.4 multiply_reduce_fusion.2
  9.6 0.0 copy-done.1
  9.6 0.0 copy-done.2
  9.6 0.4 multiply_reduce_fusion.1
  10.0 21.9 %all-reduce.1 = (f32[320]{0:T(512)S(1)}, f32[320]{0:T(512)S(1)}) all-reduce(f32[320]{0:T(512)S(1)} %get-tuple-element.13, f32[320]{0:T(512)S(1)} %get-tuple-element.15), channel_id=1, replica_groups=mesh['blk'=256,'head'=4] {'head'}, use_global_device_ids=true, to_apply=%region_1.0 | all-reduce | flops 640 | bytes 5120 | tf_op jit(solution)/shard_map/psum | solution.py:46
  31.9 4.6 %collective-permute-start = (bf16[320,192]{0,1:T(8,128)(2,1)S(1)}, bf16[320,192]{0,1:T(8,128)(2,1)S(1)}, u32[]{:S(2)}, u32[]{:S(2)}) collective-permute-start(bf16[320,192]{0,1:T(8,128)(2,1)S(1)} %divide_convert_fusion), channel_id=1, source_target_pairs={{4,0},{8,4},{12,8},{16,12},{20,16},{24,20},{28,24},{32,28},{36,32}... | collective-permute-start | bytes 368648 | tf_op jit(solution)/shard_map/ppermute | solution.py:17
  36.6 1.0 convolution_convert_fusion.5
  37.6 2.9 %collective-permute-done = bf16[320,192]{0,1:T(8,128)(2,1)S(1)} collective-permute-done((bf16[320,192]{0,1:T(8,128)(2,1)S(1)}, bf16[320,192]{0,1:T(8,128)(2,1)S(1)}, u32[]{:S(2)}, u32[]{:S(2)}) %collective-permute-start) | collective-permute-done | bytes 122912 | tf_op jit(solution)/shard_map/ppermute | solution.py:17
  40.5 6.5 %collective-permute-start.1 = (bf16[320,192]{0,1:T(8,128)(2,1)S(1)}, bf16[320,192]{0,1:T(8,128)(2,1)S(1)}, u32[]{:S(2)}, u32[]{:S(2)}) collective-permute-start(bf16[320,192]{0,1:T(8,128)(2,1)S(1)} %collective-permute-done), channel_id=1, source_target_pairs={{4,0},{8,4},{12,8},{16,12},{20,16},{24,20},{28,24},{32,28},{36,32}... | collective-permute-start | bytes 368648 | tf_op jit(solution)/shard_map/ppermute | solution.py:17
  46.9 1.0 convolution_convert_fusion.4
  47.9 0.0 collective-permute-done.1
  47.9 9.7 %collective-permute-start.2 = (bf16[320,192]{0,1:T(8,128)(2,1)S(1)}, bf16[320,192]{0,1:T(8,128)(2,1)S(1)}, u32[]{:S(2)}, u32[]{:S(2)}) collective-permute-start(bf16[320,192]{0,1:T(8,128)(2,1)S(1)} %collective-permute-done.1), channel_id=1, source_target_pairs={{4,0},{8,4},{12,8},{16,12},{20,16},{24,20},{28,24},{32,28},{36,32}... | collective-permute-start | bytes 368648 | tf_op jit(solution)/shard_map/ppermute | solution.py:17
  57.6 1.0 convolution_convert_fusion.3
  58.6 0.0 collective-permute-done.2
  58.6 1.0 convolution_convert_fusion.2
  59.5 0.0 all-reduce.5.cloned.1.call-update
  59.6 0.0 reduce-scatter.5.cloned.1.call-start
  59.6 78.2 %all-reduce.5.cloned.1.call-done = (bf16[320,320]{1,0:T(8,128)(2,1)}, bf16[320,320]{1,0:T(8,128)(2,1)}, bf16[320,320]{1,0:T(8,128)(2,1)}, bf16[320,320]{1,0:T(8,128)(2,1)}) async-done(((bf16[320,320]{1,0:T(8,128)(2,1)}, bf16[320,320]{1,0:T(8,128)(2,1)}, bf16[320,320]{1,0:T(8,128)(2,1)}, bf16[320,320]{1,0:T(8,128)(2,1)}), (bf16[320,320]{1,0:T(8,128)(2,1)}, bf16[320,320]{1,0:T(8,128)(2,1)}, ...) | async-done | bytes 819216 | tf_op jit(solution)/shard_map/psum | solution.py:64
  137.8 1.5 fusion
  139.3 0.0 copy-start.4
  139.3 0.2 convolution_convert_fusion.6
  139.6 0.3 fusion.17
  139.8 3.1 %collective-permute-start.3 = (bf16[320,192]{0,1:T(8,128)(2,1)S(1)}, bf16[320,192]{0,1:T(8,128)(2,1)S(1)}, u32[]{:S(2)}, u32[]{:S(2)}) collective-permute-start(bf16[320,192]{0,1:T(8,128)(2,1)S(1)} %convolution_convert_fusion.6), channel_id=1, source_target_pairs={{4,0},{8,4},{12,8},{16,12},{20,16},{24,20},{28,24},{32,28},{36,32}... | collective-permute-start | bytes 368648 | tf_op jit(solution)/shard_map/ppermute | solution.py:17
  143.0 0.0 copy-done.4
  143.0 0.0 copy-start.5
  143.0 0.3 convolution_add_fusion.2
  143.3 0.6 copy-done.5
  143.9 0.3 convolution_add_fusion.1
  144.3 2.7 %collective-permute-done.3 = bf16[320,192]{0,1:T(8,128)(2,1)S(1)} collective-permute-done((bf16[320,192]{0,1:T(8,128)(2,1)S(1)}, bf16[320,192]{0,1:T(8,128)(2,1)S(1)}, u32[]{:S(2)}, u32[]{:S(2)}) %collective-permute-start.3) | collective-permute-done | bytes 122912 | tf_op jit(solution)/shard_map/ppermute | solution.py:17
  147.0 0.3 add_convert_fusion.2
  147.3 4.6 %collective-permute-start.4 = (bf16[320,192]{0,1:T(8,128)(2,1)S(1)}, bf16[320,192]{0,1:T(8,128)(2,1)S(1)}, u32[]{:S(2)}, u32[]{:S(2)}) collective-permute-start(bf16[320,192]{0,1:T(8,128)(2,1)S(1)} %add_convert_fusion.2), channel_id=1, source_target_pairs={{4,0},{8,4},{12,8},{16,12},{20,16},{24,20},{28,24},{32,28},{36,32}... | collective-permute-start | bytes 368648 | tf_op jit(solution)/shard_map/ppermute | solution.py:17
  152.0 0.3 fusion.15
  152.3 0.0 copy-start.6
  152.4 1.4 collective-permute-done.4
  153.8 8.9 %collective-permute-start.5 = (bf16[320,192]{0,1:T(8,128)(2,1)S(1)}, bf16[320,192]{0,1:T(8,128)(2,1)S(1)}, u32[]{:S(2)}, u32[]{:S(2)}) collective-permute-start(bf16[320,192]{0,1:T(8,128)(2,1)S(1)} %add_convert_fusion.1), channel_id=1, source_target_pairs={{4,0},{8,4},{12,8},{16,12},{20,16},{24,20},{28,24},{32,28},{36,32}... | collective-permute-start | bytes 368648 | tf_op jit(solution)/shard_map/ppermute | solution.py:17
  162.7 0.0 copy-done.6
  162.7 0.3 fusion.16
  163.1 0.6 collective-permute-done.5
  163.7 1.9 collective-permute-start.6
  165.7 0.4 multiply_reduce_fusion
  166.0 8.4 %collective-permute-done.6 = bf16[320,192]{0,1:T(8,128)(2,1)S(1)} collective-permute-done((bf16[320,192]{0,1:T(8,128)(2,1)S(1)}, bf16[320,192]{0,1:T(8,128)(2,1)S(1)}, u32[]{:S(2)}, u32[]{:S(2)}) %collective-permute-start.6) | collective-permute-done | bytes 122912 | tf_op jit(solution)/shard_map/ppermute | solution.py:17
  174.4 0.1 fusion.6
  174.5 7.7 %all-reduce = (f32[320]{0:T(512)S(1)}, f32[320]{0:T(512)S(1)}) all-reduce(f32[320]{0:T(512)S(1)} %get-tuple-element.17, f32[320]{0:T(512)S(1)} %fusion.6), channel_id=1, replica_groups=mesh['blk'=256,'head'=4] {'head'}, use_global_device_ids=true, to_apply=%region_9.10 | all-reduce | flops 640 | bytes 5120 | tf_op jit(solution)/shard_map/psum | solution.py:74
  182.2 1.2 convolution_convert_fusion
  183.5 0.0 copy-start.3
  183.5 0.0 reduce-scatter.5.cloned.1.call-update
  183.5 0.0 reduce-scatter.3.cloned.1.call-start
  183.6 0.9 copy-done.3
  184.4 1.2 convolution_convert_fusion.1
  185.7 0.0 reduce-scatter.3.cloned.1.call-update
  185.7 0.4 fusion.3
  186.1 0.7 fusion.1
  186.9 0.6 dynamic_slice.3
  187.5 31.4 %reduce-scatter.5.cloned.1.call-done = bf16[320,192]{0,1:T(8,128)(2,1)} async-done(((bf16[320,768]{0,1:T(8,128)(2,1)}), bf16[320,192]{0,1:T(8,128)(2,1)}) %reduce-scatter.5.cloned.1.call-update) | async-done | bytes 122896 | tf_op jit(solution)/shard_map/reduce_scatter | solution.py:88
  218.9 37.5 %reduce-scatter.3.cloned.1.call-done = bf16[320,192]{0,1:T(8,128)(2,1)} async-done(((bf16[320,768]{0,1:T(8,128)(2,1)}), bf16[320,192]{0,1:T(8,128)(2,1)}) %reduce-scatter.3.cloned.1.call-update) | async-done | bytes 122896 | tf_op jit(solution)/shard_map/reduce_scatter | solution.py:82
  (9 shorter events, 0.2 us)
Async XLA Ops:
  7.2 1.0 copy-start
  7.2 2.4 copy-start.1
  7.2 2.4 copy-start.2
  7.2 130.6 %all-reduce.5.cloned.1.call-start = ((), (), s32[]{:S(2)}) async-start(), calls=%async_computation.4 | async-start | bytes 1966080 | tf_op jit(solution)/shard_map/psum | solution.py:64
  31.9 8.5 %collective-permute-start = (bf16[320,192]{0,1:T(8,128)(2,1)S(1)}, bf16[320,192]{0,1:T(8,128)(2,1)S(1)}, u32[]{:S(2)}, u32[]{:S(2)}) collective-permute-start(bf16[320,192]{0,1:T(8,128)(2,1)S(1)} %divide_convert_fusion), channel_id=1, source_target_pairs={{4,0},{8,4},{12,8},{16,12},{20,16},{24,20},{28,24},{32,28},{36,32}... | collective-permute-start | bytes 368648 | tf_op jit(solution)/shard_map/ppermute | solution.py:17
  40.5 7.4 %collective-permute-start.1 = (bf16[320,192]{0,1:T(8,128)(2,1)S(1)}, bf16[320,192]{0,1:T(8,128)(2,1)S(1)}, u32[]{:S(2)}, u32[]{:S(2)}) collective-permute-start(bf16[320,192]{0,1:T(8,128)(2,1)S(1)} %collective-permute-done), channel_id=1, source_target_pairs={{4,0},{8,4},{12,8},{16,12},{20,16},{24,20},{28,24},{32,28},{36,32}... | collective-permute-start | bytes 368648 | tf_op jit(solution)/shard_map/ppermute | solution.py:17
  47.9 10.7 %collective-permute-start.2 = (bf16[320,192]{0,1:T(8,128)(2,1)S(1)}, bf16[320,192]{0,1:T(8,128)(2,1)S(1)}, u32[]{:S(2)}, u32[]{:S(2)}) collective-permute-start(bf16[320,192]{0,1:T(8,128)(2,1)S(1)} %collective-permute-done.1), channel_id=1, source_target_pairs={{4,0},{8,4},{12,8},{16,12},{20,16},{24,20},{28,24},{32,28},{36,32}... | collective-permute-start | bytes 368648 | tf_op jit(solution)/shard_map/ppermute | solution.py:17
  59.6 159.3 %reduce-scatter.5.cloned.1.call-start = ((), (), s32[]{:S(2)}) async-start(), calls=%async_computation.3 | async-start | bytes 737280 | tf_op jit(solution)/shard_map/reduce_scatter | solution.py:88
  139.3 3.6 %copy-start.4 = (bf16[320,320]{1,0:T(8,128)(2,1)S(1)}, bf16[320,320]{1,0:T(8,128)(2,1)}, u32[]{:S(2)}) copy-start(bf16[320,320]{1,0:T(8,128)(2,1)} %get-tuple-element.8) | copy-start | bytes 614404
  139.8 7.2 %collective-permute-start.3 = (bf16[320,192]{0,1:T(8,128)(2,1)S(1)}, bf16[320,192]{0,1:T(8,128)(2,1)S(1)}, u32[]{:S(2)}, u32[]{:S(2)}) collective-permute-start(bf16[320,192]{0,1:T(8,128)(2,1)S(1)} %convolution_convert_fusion.6), channel_id=1, source_target_pairs={{4,0},{8,4},{12,8},{16,12},{20,16},{24,20},{28,24},{32,28},{36,32}... | collective-permute-start | bytes 368648 | tf_op jit(solution)/shard_map/ppermute | solution.py:17
  143.0 0.9 copy-start.5
  147.3 6.5 %collective-permute-start.4 = (bf16[320,192]{0,1:T(8,128)(2,1)S(1)}, bf16[320,192]{0,1:T(8,128)(2,1)S(1)}, u32[]{:S(2)}, u32[]{:S(2)}) collective-permute-start(bf16[320,192]{0,1:T(8,128)(2,1)S(1)} %add_convert_fusion.2), channel_id=1, source_target_pairs={{4,0},{8,4},{12,8},{16,12},{20,16},{24,20},{28,24},{32,28},{36,32}... | collective-permute-start | bytes 368648 | tf_op jit(solution)/shard_map/ppermute | solution.py:17
  152.3 10.4 %copy-start.6 = (bf16[320,320]{1,0:T(8,128)(2,1)S(1)}, bf16[320,320]{1,0:T(8,128)(2,1)}, u32[]{:S(2)}) copy-start(bf16[320,320]{1,0:T(8,128)(2,1)} %get-tuple-element.10) | copy-start | bytes 614404
  153.8 9.9 %collective-permute-start.5 = (bf16[320,192]{0,1:T(8,128)(2,1)S(1)}, bf16[320,192]{0,1:T(8,128)(2,1)S(1)}, u32[]{:S(2)}, u32[]{:S(2)}) collective-permute-start(bf16[320,192]{0,1:T(8,128)(2,1)S(1)} %add_convert_fusion.1), channel_id=1, source_target_pairs={{4,0},{8,4},{12,8},{16,12},{20,16},{24,20},{28,24},{32,28},{36,32}... | collective-permute-start | bytes 368648 | tf_op jit(solution)/shard_map/ppermute | solution.py:17
  163.7 10.7 %collective-permute-start.6 = (bf16[320,192]{0,1:T(8,128)(2,1)S(1)}, bf16[320,192]{0,1:T(8,128)(2,1)S(1)}, u32[]{:S(2)}, u32[]{:S(2)}) collective-permute-start(bf16[320,192]{0,1:T(8,128)(2,1)S(1)} %add_convert_fusion), channel_id=1, source_target_pairs={{1012,0},{1016,4},{1020,8},{0,12},{4,16},{8,20},{12,24},{16,28},{2... | collective-permute-start | bytes 368648 | tf_op jit(solution)/shard_map/ppermute | solution.py:17
  183.5 1.0 copy-start.3
  183.5 72.9 %reduce-scatter.3.cloned.1.call-start = ((), (), s32[]{:S(2)}) async-start(), calls=%async_computation.2 | async-start | bytes 737280 | tf_op jit(solution)/shard_map/reduce_scatter | solution.py:82
Sparse Core Ops, SparseCore 0:
  59.7 78.0 all-reduce.4
  183.6 35.2 reduce-scatter.4
  223.3 33.1 reduce-scatter.2
where the time goes:
time: 265 us; the launch traced here: 263 us
  waiting for transfers between devices  163 us (62%)
  starting transfers between devices  39.4 us (15%)
  blocking collectives  29.7 us (11%)
  between operations  14 us (5%)
  matrix products  10.7 us (4%)
  local copies, waits for them, and re-layouts  3.03 us (1%)
  other arithmetic  2.88 us (1%)
    psum x1, waiting for transfers between devices, body(): lax.psum(inner(u_image, moving).astype(jnp.bfloat16), 'head')  78.2 us
    ppermute x7, starting transfers between devices, passed_along(): return lax.ppermute(block, axis, route)  39.3 us
    reduce_scatter x1, waiting for transfers between devices, body(): lax.psum_scatter(inner(dz_image, image_head).astype(jnp.bfloat16), 'head'...  37.5 us
    reduce_scatter x1, waiting for transfers between devices, body(): lax.psum_scatter(inner(dz_text, text_head).astype(jnp.bfloat16), 'head',...  31.4 us
    psum x1, blocking collectives, body(): lax.psum((jnp.sum(z_image * z_image, axis=1), jnp.sum(z_text * z_text, ax...  21.9 us
    ppermute x7, waiting for transfers between devices, passed_along(): return lax.ppermute(block, axis, route)  16.1 us
    psum x1, blocking collectives, body(): lax.psum((jnp.sum(g_image * z_image, axis=1), jnp.sum(g_text * z_text, ax...  7.72 us
    dot_general x6, matrix products, inner(): lax.dot_general(left, right, (((1,), (1,)), ((), ())), preferred_element_...  6.34 us
  transfers between devices with their start and end apart: 10, of which 8 were waited for; matrix products, arithmetic and copies ran while one was open for 3% of the time, Pallas kernels for 0%

commit v1 on v0

v1 whole, which is shorter than its diff:
```python
import jax
import jax.numpy as jnp
from jax import lax
from jax.sharding import PartitionSpec as P

LOGIT_SCALE = 10.0
LOGIT_BIAS = -2.0
EPSILON = 1e-06
AXES = ("blk", "head")


class Grid:
    def __init__(self, n_blk, n_head):
        self.n_blk, self.n_head = n_blk, n_head
        self.half = n_blk // 2
        self.depth = 2 * n_head

    def at(self, device):
        blk, head = divmod(device, self.n_head)
        return blk, 2 * head + blk // self.half

    def device(self, blk, z):
        z %= self.depth
        blk = blk % self.half + self.half * (z % 2)
        return blk * self.n_head + z // 2

    def route(self, source):
        return [(source(d), d) for d in range(self.n_blk * self.n_head)]

    def along_blk(self, distance):
        def source(d):
            blk, head = divmod(d, self.n_head)
            step = distance(blk) if callable(distance) else distance
            return (blk + step) % self.n_blk * self.n_head + head

        return self.route(source)

    def along_z(self, odd, even):
        def source(d):
            blk, z = self.at(d)
            return self.device(blk, z + (odd if z % 2 else even))

        return self.route(source)


def project(feats, shards):
    head = jnp.concatenate(shards, axis=1)
    z = jnp.dot(feats, head, preferred_element_type=jnp.float32)
    n = jnp.sqrt(jnp.sum(z * z, axis=1, keepdims=True) + EPSILON)
    return z, n, (z / n).astype(jnp.bfloat16), head


def inner(left, right):
    return lax.dot_general(left, right, (((1,), (1,)), ((), ())), preferred_element_type=jnp.float32)


def weights_of(logits):
    rows, columns = logits.shape
    own = lax.broadcasted_iota(jnp.int32, logits.shape, 0) == lax.broadcasted_iota(
        jnp.int32, logits.shape, 1
    )
    signs = jnp.where(own, 1.0, -1.0)
    return (-signs * jax.nn.sigmoid(-signs * logits) * LOGIT_SCALE).astype(jnp.bfloat16)


def gradient(g, z, n, head, group):
    rows = z.shape[0]
    g, z, n = g, z[:rows], n[:rows]
    dot = jnp.sum(g * z, axis=1, keepdims=True)
    dz = (g / n - z * (dot / n**3)).astype(jnp.bfloat16)
    width = head.shape[0] // lax.axis_size("head")
    part = lax.dynamic_slice_in_dim(head, group * width, width, 0)
    return inner(dz, part).astype(jnp.bfloat16)


def body(image_feats, text_feats, image_head, text_head):
    rows = image_feats.shape[0]
    grid = Grid(lax.axis_size("blk"), lax.axis_size("head"))
    group = lax.axis_index("head")
    first = lax.axis_index("blk") % 2 == 0

    def permute(block, route):
        return lax.ppermute(block, AXES, route)

    swap = grid.along_blk(lambda blk: 1 - 2 * (blk % 2))
    mine = jnp.where(first, image_head, text_head)
    taken = [permute(mine, grid.along_z(*way)) for way in ((1, -1), (-2, 2), (3, -3))]
    text_2 = permute(text_feats, grid.along_blk(2))
    image_2 = permute(image_feats, grid.along_blk(-2))
    far = permute(
        jnp.where(first, text_feats, image_feats),
        grid.along_blk(lambda blk: 3 if blk % 2 else -3),
    )
    near = permute(jnp.where(first, image_feats, text_feats), swap)
    text_x = permute(text_2, swap)
    image_x = permute(image_2, swap)
    others = permute(jnp.concatenate(taken, axis=1), swap)
    others = jnp.split(others, 3, axis=1)
    image_shards = [image_head] + [jnp.where(first, t, o) for t, o in zip(taken, others)]
    text_shards = [text_head] + [jnp.where(first, o, t) for t, o in zip(taken, others)]
    texts = jnp.concatenate([text_feats, text_2, text_x, jnp.where(first, near, far)], axis=0)
    images = jnp.concatenate([image_feats, image_2, image_x, jnp.where(first, far, near)], axis=0)

    z_text, n_text, u_text, text_whole = project(texts, text_shards)
    z_image, n_image, u_image, image_whole = project(images, image_shards)

    logits = LOGIT_SCALE * inner(u_image[:rows], u_text) + LOGIT_BIAS
    logits_t = LOGIT_SCALE * inner(u_text[:rows], u_image) + LOGIT_BIAS
    g_image = jnp.dot(weights_of(logits), u_text, preferred_element_type=jnp.float32)
    g_text = jnp.dot(weights_of(logits_t), u_image, preferred_element_type=jnp.float32)
    image_grad = gradient(g_image, z_image[:rows], n_image[:rows], image_whole, group)
    text_grad = gradient(g_text, z_text[:rows], n_text[:rows], text_whole, group)

    quarter = rows // lax.axis_size("head")
    own = lax.dynamic_slice_in_dim(logits, group * quarter, quarter, 0)
    row_ids = group * quarter + lax.broadcasted_iota(jnp.int32, own.shape, 0)
    signs = jnp.where(row_ids == lax.broadcasted_iota(jnp.int32, own.shape, 1), 1.0, -1.0)
    row_loss = jnp.sum(jax.nn.softplus(-signs * own), axis=1)
    return image_grad, text_grad, row_loss


def solution(mesh):
    in_specs = (P("blk", None), P("blk", None), P(None, "head"), P(None, "head"))
    out_specs = (P("blk", "head"), P("blk", "head"), P(("blk", "head")))
    return jax.shard_map(body, mesh=mesh, in_specs=in_specs, out_specs=out_specs, check_vma=False)
```

time: 265 us -> 97.5 us (0.37)
  the two profiles are of different devices: /device:TPU:1 before, /device:TPU:2 now
where the time goes in v1:
time: 97.5 us; the launch traced here: 96.9 us
  starting transfers between devices  46.4 us (48%)
  matrix products  19.6 us (20%)
  waiting for transfers between devices  19.4 us (20%)
  other arithmetic  7.73 us (8%)
  local copies, waits for them, and re-layouts  2.79 us (3%)
    ppermute x10, starting transfers between devices, permute(): return lax.ppermute(block, AXES, route)  46.4 us
    ppermute x10, waiting for transfers between devices, permute(): return lax.ppermute(block, AXES, route)  19.4 us
    dot_general x3, matrix products, inner(): lax.dot_general(left, right, (((1,), (1,)), ((), ())), preferred_element_...  7.36 us
    dot_general x2, matrix products, project(): z = jnp.dot(feats, head, preferred_element_type=jnp.float32)  6.12 us
    dot_general x1, matrix products, body(): jnp.dot(weights_of(logits_t), u_image, preferred_element_type=jnp.float32)  4.99 us
    unnamed x18, local copies, waits for them, and re-layouts  2.79 us
    convert_element_type x2, other arithmetic, project(): return (z, n, (z / n).astype(jnp.bfloat16), head)  1.98 us
  transfers between devices with their start and end apart: 10, of which 4 were waited for; matrix products, arithmetic and copies ran while one was open for 7% of the time, Pallas kernels for 0%

profile of v1, /device:TPU:2, one launch (start us, length us, event | category | flops | bytes accessed | tf_op | source)
XLA Modules:
  0.0 96.9 jit_solution(6747340407793317899)
XLA Ops:
  0.6 0.0 copy-start.5
  0.7 0.0 copy-start.6
  0.7 1.1 %broadcast_select_fusion.10 = bf16[768,192]{0,1:T(8,128)(2,1)S(1)} fusion(bf16[768,192]{0,1:T(8,128)(2,1)} %param.6, bf16[768,192]{0,1:T(8,128)(2,1)} %param.7, pred[]{:T(512)S(6)} %eq.19), kind=kLoop, calls=%fused_computation.67 | loop fusion | flops 147456 | bytes 884737 | tf_op jit(solution)/shard_map/jit(_where)/select_n | solution.py:86
  1.8 15.5 %collective-permute-start.6 = (bf16[768,192]{0,1:T(8,128)(2,1)S(1)}, bf16[768,192]{0,1:T(8,128)(2,1)S(1)}, u32[]{:S(2)}, u32[]{:S(2)}) collective-permute-start(bf16[768,192]{0,1:T(8,128)(2,1)S(1)} %broadcast_select_fusion.10), channel_id=1, source_target_pairs={{514,0},{515,1},{512,2},{513,3},{518,4},{519,5},{516,6},{517,7},{5... | collective-permute-start | bytes 884744 | tf_op jit(solution)/shard_map/ppermute | solution.py:83
  17.2 2.8 %collective-permute-start.5 = (bf16[768,192]{0,1:T(8,128)(2,1)S(1)}, bf16[768,192]{0,1:T(8,128)(2,1)S(1)}, u32[]{:S(2)}, u32[]{:S(2)}) collective-permute-start(bf16[768,192]{0,1:T(8,128)(2,1)S(1)} %broadcast_select_fusion.10), channel_id=1, source_target_pairs={{1,0},{2,1},{3,2},{0,3},{5,4},{6,5},{7,6},{4,7},{9,8},{10,9},{11,1... | collective-permute-start | bytes 884744 | tf_op jit(solution)/shard_map/ppermute | solution.py:83
  20.1 3.3 %collective-permute-start.4 = (bf16[768,192]{0,1:T(8,128)(2,1)S(1)}, bf16[768,192]{0,1:T(8,128)(2,1)S(1)}, u32[]{:S(2)}, u32[]{:S(2)}) collective-permute-start(bf16[768,192]{0,1:T(8,128)(2,1)S(1)} %broadcast_select_fusion.10), channel_id=1, source_target_pairs={{515,0},{512,1},{513,2},{514,3},{519,4},{516,5},{517,6},{518,7},{5... | collective-permute-start | bytes 884744 | tf_op jit(solution)/shard_map/ppermute | solution.py:83
  23.4 3.4 %collective-permute-start = (bf16[320,768]{1,0:T(8,128)(2,1)}, bf16[320,768]{1,0:T(8,128)(2,1)}, u32[]{:S(2)}, u32[]{:S(2)}) collective-permute-start(bf16[320,768]{1,0:T(8,128)(2,1)} %param.4), channel_id=1, source_target_pairs={{1016,0},{1017,1},{1018,2},{1019,3},{1020,4},{1021,5},{1022,6},{10... | collective-permute-start | bytes 1474568 | tf_op jit(solution)/shard_map/ppermute | solution.py:83
  26.8 2.4 %collective-permute-start.8 = (bf16[320,768]{1,0:T(8,128)(2,1)}, bf16[320,768]{1,0:T(8,128)(2,1)}, u32[]{:S(2)}, u32[]{:S(2)}) collective-permute-start(bf16[320,768]{1,0:T(8,128)(2,1)} %param.5), channel_id=1, source_target_pairs={{8,0},{9,1},{10,2},{11,3},{12,4},{13,5},{14,6},{15,7},{16,8},{17,9... | collective-permute-start | bytes 1474568 | tf_op jit(solution)/shard_map/ppermute | solution.py:83
  29.2 1.3 %collective-permute-done.6 = bf16[768,192]{0,1:T(8,128)(2,1)S(1)} collective-permute-done((bf16[768,192]{0,1:T(8,128)(2,1)S(1)}, bf16[768,192]{0,1:T(8,128)(2,1)S(1)}, u32[]{:S(2)}, u32[]{:S(2)}) %collective-permute-start.6) | collective-permute-done | bytes 294944 | tf_op jit(solution)/shard_map/ppermute | solution.py:83
  30.5 7.7 %collective-permute-done.5 = bf16[768,192]{0,1:T(8,128)(2,1)S(1)} collective-permute-done((bf16[768,192]{0,1:T(8,128)(2,1)S(1)}, bf16[768,192]{0,1:T(8,128)(2,1)S(1)}, u32[]{:S(2)}, u32[]{:S(2)}) %collective-permute-start.5) | collective-permute-done | bytes 294944 | tf_op jit(solution)/shard_map/ppermute | solution.py:83
  38.2 5.0 %collective-permute-done.4 = bf16[768,192]{0,1:T(8,128)(2,1)S(1)} collective-permute-done((bf16[768,192]{0,1:T(8,128)(2,1)S(1)}, bf16[768,192]{0,1:T(8,128)(2,1)S(1)}, u32[]{:S(2)}, u32[]{:S(2)}) %collective-permute-start.4) | collective-permute-done | bytes 294944 | tf_op jit(solution)/shard_map/ppermute | solution.py:83
  43.2 0.1 pad_maximum_fusion.2
  43.2 1.9 %collective-permute-start.7 = (bf16[768,576]{0,1:T(8,128)(2,1)S(1)}, bf16[768,576]{0,1:T(8,128)(2,1)S(1)}, u32[]{:S(2)}, u32[]{:S(2)}) collective-permute-start(bf16[768,576]{0,1:T(8,128)(2,1)S(1)} %pad_maximum_fusion.2), channel_id=1, source_target_pairs={{4,0},{5,1},{6,2},{7,3},{0,4},{1,5},{2,6},{3,7},{12,8},{13,9},{14,... | collective-permute-start | bytes 2654216 | tf_op jit(solution)/shard_map/ppermute | solution.py:83
  45.2 0.0 copy-done.5
  45.2 0.0 copy-done.6
  45.2 1.0 %broadcast_select_fusion.3 = (bf16[320,768]{1,0:T(8,128)(2,1)}, bf16[320,768]{1,0:T(8,128)(2,1)}) fusion(bf16[320,768]{1,0:T(8,128)(2,1)S(1)} %copy-done.5, bf16[320,768]{1,0:T(8,128)(2,1)S(1)} %copy-done.6, pred[]{:T(512)S(6)} %eq.19), kind=kLoop, calls=%fused_computation.56 | loop fusion | flops 491520 | bytes 1966081 | tf_op jit(solution)/shard_map/jit(_where)/select_n | solution.py:91
  46.2 10.7 %collective-permute-start.2 = (bf16[320,768]{1,0:T(8,128)(2,1)}, bf16[320,768]{1,0:T(8,128)(2,1)}, u32[]{:S(2)}, u32[]{:S(2)}) collective-permute-start(bf16[320,768]{1,0:T(8,128)(2,1)} %get-tuple-element.11), channel_id=1, source_target_pairs={{1012,0},{1013,1},{1014,2},{1015,3},{16,4},{17,5},{18,6},{19,7},{1... | collective-permute-start | bytes 1474568 | tf_op jit(solution)/shard_map/ppermute | solution.py:83
  57.0 1.9 %collective-permute-start.3 = (bf16[320,768]{1,0:T(8,128)(2,1)}, bf16[320,768]{1,0:T(8,128)(2,1)}, u32[]{:S(2)}, u32[]{:S(2)}) collective-permute-start(bf16[320,768]{1,0:T(8,128)(2,1)} %get-tuple-element.12), channel_id=1, source_target_pairs={{4,0},{5,1},{6,2},{7,3},{0,4},{1,5},{2,6},{3,7},{12,8},{13,9},{14,... | collective-permute-start | bytes 1474568 | tf_op jit(solution)/shard_map/ppermute | solution.py:83
  58.9 0.0 collective-permute-done
  59.0 2.4 %collective-permute-start.1 = (bf16[320,768]{1,0:T(8,128)(2,1)}, bf16[320,768]{1,0:T(8,128)(2,1)S(1)}, u32[]{:S(2)}, u32[]{:S(2)}) collective-permute-start(bf16[320,768]{1,0:T(8,128)(2,1)} %collective-permute-done), channel_id=1, source_target_pairs={{4,0},{5,1},{6,2},{7,3},{0,4},{1,5},{2,6},{3,7},{12,8},{13,9},{14,... | collective-permute-start | bytes 1474568 | tf_op jit(solution)/shard_map/ppermute | solution.py:83
  61.4 0.0 collective-permute-done.8
  61.4 1.9 %collective-permute-start.9 = (bf16[320,768]{1,0:T(8,128)(2,1)}, bf16[320,768]{1,0:T(8,128)(2,1)S(1)}, u32[]{:S(2)}, u32[]{:S(2)}) collective-permute-start(bf16[320,768]{1,0:T(8,128)(2,1)} %collective-permute-done.8), channel_id=1, source_target_pairs={{4,0},{5,1},{6,2},{7,3},{0,4},{1,5},{2,6},{3,7},{12,8},{13,9},{14,... | collective-permute-start | bytes 1474568 | tf_op jit(solution)/shard_map/ppermute | solution.py:83
  63.3 5.5 %collective-permute-done.2 = bf16[320,768]{1,0:T(8,128)(2,1)} collective-permute-done((bf16[320,768]{1,0:T(8,128)(2,1)}, bf16[320,768]{1,0:T(8,128)(2,1)}, u32[]{:S(2)}, u32[]{:S(2)}) %collective-permute-start.2) | collective-permute-done | bytes 491552 | tf_op jit(solution)/shard_map/ppermute | solution.py:83
  68.8 0.0 collective-permute-done.3
  68.8 1.2 %broadcast_select_fusion.1 = (bf16[320,768]{1,0:T(8,128)(2,1)S(1)}, bf16[320,768]{1,0:T(8,128)(2,1)S(1)}) fusion(bf16[320,768]{1,0:T(8,128)(2,1)} %collective-permute-done.2, bf16[320,768]{1,0:T(8,128)(2,1)} %collective-permute-done.3, pred[]{:T(512)S(6)} %eq.19), kind=kLoop, calls=%fused_computation.54 | loop fusion | flops 491520 | bytes 1966081 | tf_op jit(solution)/shard_map/jit(_where)/select_n | solution.py:102
  70.0 0.0 copy-start.3
  70.0 0.0 collective-permute-done.7
  70.0 0.1 broadcast_select_fusion.9
  70.2 0.0 collective-permute-done.9
  70.2 0.8 copy-done.3
  71.0 0.0 copy-start.4
  71.0 2.9 %multiply_reduce_fusion = (f32[1280]{0:T(1024)S(1)}, f32[1280,768]{1,0:T(8,128)S(1)}) fusion(bf16[768,192]{0,1:T(8,128)(2,1)S(1)} %get-tuple-element.15, bf16[768,192]{0,1:T(8,128)(2,1)S(1)} %get-tuple-element.13, bf16[768,192]{0,1:T(8,128)(2,1)S(1)} %get-tuple-element.4, bf16[768,192]{0,1:T(8,128)(2,1)S(1)} %copy-done.3, ...), kind=kOutput, calls=%fused_computation.1 | convolution fusion | flops 1524497152 | bytes 7083008 | tf_op jit(solution)/shard_map/dot_general | solution.py:48
  73.9 0.0 copy-start
  73.9 0.0 copy-done.4
  73.9 0.0 copy-start.7
  74.0 1.2 %pad_maximum_fusion = (bf16[768,768]{0,1:T(8,128)(2,1)}, bf16[768,768]{0,1:T(8,128)(2,1)S(1)}) fusion(bf16[768,192]{0,1:T(8,128)(2,1)S(1)} %get-tuple-element.16, bf16[768,192]{0,1:T(8,128)(2,1)S(1)} %get-tuple-element.14, bf16[768,192]{0,1:T(8,128)(2,1)S(1)} %get-tuple-element.3, bf16[768,192]{0,1:T(8,128)(2,1)S(1)} %copy-done.4, ...), kind=kLoop, calls=%fused_computation.36 | loop fusion | flops 9437184 | bytes 4718592 | tf_op jit(solution)/shard_map/concatenate | solution.py:47
  75.1 0.0 collective-permute-done.1
  75.1 0.2 copy-done.7
  75.3 3.2 %multiply_reduce_fusion.1 = (f32[1280]{0:T(1024)S(1)}, f32[1280,768]{1,0:T(8,128)S(1)}) fusion(bf16[768,192]{0,1:T(8,128)(2,1)S(1)} %get-tuple-element.16, bf16[768,192]{0,1:T(8,128)(2,1)S(1)} %get-tuple-element.14, bf16[768,192]{0,1:T(8,128)(2,1)S(1)} %get-tuple-element.3, bf16[768,192]{0,1:T(8,128)(2,1)S(1)} %copy-done.4, ...), kind=kOutput, calls=%fused_computation.3 | convolution fusion | flops 1524497152 | bytes 7083008 | tf_op jit(solution)/shard_map/dot_general | solution.py:48
  78.5 0.0 copy-start.1
  78.6 0.0 copy-done
  78.6 0.3 divide_convert_fusion
  78.9 1.5 %copy-done.1 = f32[1280,768]{1,0:T(8,128)} copy-done((f32[1280,768]{1,0:T(8,128)}, f32[1280,768]{1,0:T(8,128)S(1)}, u32[]{:S(2)}) %copy-start.1) | copy-done | bytes 3932184
  80.4 1.7 %divide_convert_fusion.1 = bf16[1280,768]{1,0:T(8,128)(2,1)} fusion(f32[1280,768]{1,0:T(8,128)S(1)} %get-tuple-element.20, f32[1280]{0:T(1024)S(1)} %add_sqrt_fusion.1), kind=kLoop, calls=%fused_computation.2 | loop fusion | flops 1966080 | bytes 5903360 | tf_op jit(solution)/shard_map/convert_element_type | solution.py:50
  82.1 5.0 %multiply_reduce_fusion.2 = (f32[320]{0:T(512)S(1)}, f32[320,768]{1,0:T(8,128)}) fusion(f32[1280,768]{1,0:T(8,128)} %copy-done, bf16[1280,768]{1,0:T(8,128)(2,1)} %divide_convert_fusion.1, bf16[1280,768]{1,0:T(8,128)(2,1)S(1)} %divide_convert_fusion), kind=kOutput, calls=%fused_computation.42 | convolution fusion | flops 1263697664 | bytes 6391040 | tf_op jit(solution)/shard_map/dot_general | solution.py:110
  87.1 0.0 copy-start.2
  87.1 2.0 %fusion = f32[320,1280]{1,0:T(8,128)S(1)} fusion(bf16[1280,768]{1,0:T(8,128)(2,1)S(1)} %divide_convert_fusion, bf16[1280,768]{1,0:T(8,128)(2,1)} %divide_convert_fusion.1), kind=kOutput, calls=%fused_computation.6 | convolution fusion | flops 629964800 | bytes 4096000 | tf_op jit(solution)/shard_map/dot_general | solution.py:54
  89.1 0.2 copy-done.2
  89.4 1.1 %multiply_reduce_fusion.3 = (f32[320]{0:T(512)S(1)}, f32[320,768]{1,0:T(8,128)S(1)}) fusion(f32[1280,768]{1,0:T(8,128)S(1)} %copy-done.2, bf16[1280,768]{1,0:T(8,128)(2,1)S(1)} %divide_convert_fusion, f32[320,1280]{1,0:T(8,128)S(1)} %fusion), kind=kOutput, calls=%fused_computation.44 | convolution fusion | flops 633732800 | bytes 5571840 | tf_op jit(solution)/shard_map/dot_general | solution.py:109
  90.5 1.0 fusion.35
  91.5 0.0 copy-start.8
  91.5 2.7 %convolution_convert_fusion.1 = bf16[320,192]{0,1:T(8,128)(2,1)} fusion(f32[320,768]{1,0:T(8,128)S(1)} %get-tuple-element.22, f32[1280,768]{1,0:T(8,128)S(1)} %copy-done.2, f32[320]{0:T(512)S(1)} %fusion.41, f32[320]{0:T(512)S(1)} %slice.33, bf16[768,768]{0,1:T(8,128)(2,1)} %get-tuple-element.25, s32[]{:T(128)S(6)} %select_n.100), kind=kOutput, calls=%fused_computation.39 | convolution fusion | flops 95416320 | bytes 2486276 | tf_op jit(solution)/shard_map/dot_general | solution.py:54
  94.2 0.0 copy-done.8
  94.2 2.7 %convolution_convert_fusion = bf16[320,192]{0,1:T(8,128)(2,1)} fusion(f32[320,768]{1,0:T(8,128)S(1)} %copy-done.8, f32[1280,768]{1,0:T(8,128)} %copy-done, f32[320]{0:T(512)S(1)} %fusion.40, f32[320]{0:T(512)S(1)} %slice.36, bf16[768,768]{0,1:T(8,128)(2,1)S(1)} %get-tuple-element.26, s32[]{:T(128)S(6)} %select_n.100), kind=kOutput, calls=%fused_computation.38 | convolution fusion | flops 95416320 | bytes 2486276 | tf_op jit(solution)/shard_map/dot_general | solution.py:54
  (7 shorter events, 0.1 us)
Async XLA Ops:
  0.6 44.6 %copy-start.5 = (bf16[320,768]{1,0:T(8,128)(2,1)S(1)}, bf16[320,768]{1,0:T(8,128)(2,1)}, u32[]{:S(2)}) copy-start(bf16[320,768]{1,0:T(8,128)(2,1)} %param.5) | copy-start | bytes 1474564
  0.7 44.6 %copy-start.6 = (bf16[320,768]{1,0:T(8,128)(2,1)S(1)}, bf16[320,768]{1,0:T(8,128)(2,1)}, u32[]{:S(2)}) copy-start(bf16[320,768]{1,0:T(8,128)(2,1)} %param.4) | copy-start | bytes 1474564
  1.8 28.8 %collective-permute-start.6 = (bf16[768,192]{0,1:T(8,128)(2,1)S(1)}, bf16[768,192]{0,1:T(8,128)(2,1)S(1)}, u32[]{:S(2)}, u32[]{:S(2)}) collective-permute-start(bf16[768,192]{0,1:T(8,128)(2,1)S(1)} %broadcast_select_fusion.10), channel_id=1, source_target_pairs={{514,0},{515,1},{512,2},{513,3},{518,4},{519,5},{516,6},{517,7},{5... | collective-permute-start | bytes 884744 | tf_op jit(solution)/shard_map/ppermute | solution.py:83
  17.2 20.9 %collective-permute-start.5 = (bf16[768,192]{0,1:T(8,128)(2,1)S(1)}, bf16[768,192]{0,1:T(8,128)(2,1)S(1)}, u32[]{:S(2)}, u32[]{:S(2)}) collective-permute-start(bf16[768,192]{0,1:T(8,128)(2,1)S(1)} %broadcast_select_fusion.10), channel_id=1, source_target_pairs={{1,0},{2,1},{3,2},{0,3},{5,4},{6,5},{7,6},{4,7},{9,8},{10,9},{11,1... | collective-permute-start | bytes 884744 | tf_op jit(solution)/shard_map/ppermute | solution.py:83
  20.1 23.1 %collective-permute-start.4 = (bf16[768,192]{0,1:T(8,128)(2,1)S(1)}, bf16[768,192]{0,1:T(8,128)(2,1)S(1)}, u32[]{:S(2)}, u32[]{:S(2)}) collective-permute-start(bf16[768,192]{0,1:T(8,128)(2,1)S(1)} %broadcast_select_fusion.10), channel_id=1, source_target_pairs={{515,0},{512,1},{513,2},{514,3},{519,4},{516,5},{517,6},{518,7},{5... | collective-permute-start | bytes 884744 | tf_op jit(solution)/shard_map/ppermute | solution.py:83
  23.4 35.6 %collective-permute-start = (bf16[320,768]{1,0:T(8,128)(2,1)}, bf16[320,768]{1,0:T(8,128)(2,1)}, u32[]{:S(2)}, u32[]{:S(2)}) collective-permute-start(bf16[320,768]{1,0:T(8,128)(2,1)} %param.4), channel_id=1, source_target_pairs={{1016,0},{1017,1},{1018,2},{1019,3},{1020,4},{1021,5},{1022,6},{10... | collective-permute-start | bytes 1474568 | tf_op jit(solution)/shard_map/ppermute | solution.py:83
  26.8 34.6 %collective-permute-start.8 = (bf16[320,768]{1,0:T(8,128)(2,1)}, bf16[320,768]{1,0:T(8,128)(2,1)}, u32[]{:S(2)}, u32[]{:S(2)}) collective-permute-start(bf16[320,768]{1,0:T(8,128)(2,1)} %param.5), channel_id=1, source_target_pairs={{8,0},{9,1},{10,2},{11,3},{12,4},{13,5},{14,6},{15,7},{16,8},{17,9... | collective-permute-start | bytes 1474568 | tf_op jit(solution)/shard_map/ppermute | solution.py:83
  43.2 26.8 %collective-permute-start.7 = (bf16[768,576]{0,1:T(8,128)(2,1)S(1)}, bf16[768,576]{0,1:T(8,128)(2,1)S(1)}, u32[]{:S(2)}, u32[]{:S(2)}) collective-permute-start(bf16[768,576]{0,1:T(8,128)(2,1)S(1)} %pad_maximum_fusion.2), channel_id=1, source_target_pairs={{4,0},{5,1},{6,2},{7,3},{0,4},{1,5},{2,6},{3,7},{12,8},{13,9},{14,... | collective-permute-start | bytes 2654216 | tf_op jit(solution)/shard_map/ppermute | solution.py:83
  46.2 22.5 %collective-permute-start.2 = (bf16[320,768]{1,0:T(8,128)(2,1)}, bf16[320,768]{1,0:T(8,128)(2,1)}, u32[]{:S(2)}, u32[]{:S(2)}) collective-permute-start(bf16[320,768]{1,0:T(8,128)(2,1)} %get-tuple-element.11), channel_id=1, source_target_pairs={{1012,0},{1013,1},{1014,2},{1015,3},{16,4},{17,5},{18,6},{19,7},{1... | collective-permute-start | bytes 1474568 | tf_op jit(solution)/shard_map/ppermute | solution.py:83
  57.0 11.8 %collective-permute-start.3 = (bf16[320,768]{1,0:T(8,128)(2,1)}, bf16[320,768]{1,0:T(8,128)(2,1)}, u32[]{:S(2)}, u32[]{:S(2)}) collective-permute-start(bf16[320,768]{1,0:T(8,128)(2,1)} %get-tuple-element.12), channel_id=1, source_target_pairs={{4,0},{5,1},{6,2},{7,3},{0,4},{1,5},{2,6},{3,7},{12,8},{13,9},{14,... | collective-permute-start | bytes 1474568 | tf_op jit(solution)/shard_map/ppermute | solution.py:83
  59.0 16.2 %collective-permute-start.1 = (bf16[320,768]{1,0:T(8,128)(2,1)}, bf16[320,768]{1,0:T(8,128)(2,1)S(1)}, u32[]{:S(2)}, u32[]{:S(2)}) collective-permute-start(bf16[320,768]{1,0:T(8,128)(2,1)} %collective-permute-done), channel_id=1, source_target_pairs={{4,0},{5,1},{6,2},{7,3},{0,4},{1,5},{2,6},{3,7},{12,8},{13,9},{14,... | collective-permute-start | bytes 1474568 | tf_op jit(solution)/shard_map/ppermute | solution.py:83
  61.4 8.8 %collective-permute-start.9 = (bf16[320,768]{1,0:T(8,128)(2,1)}, bf16[320,768]{1,0:T(8,128)(2,1)S(1)}, u32[]{:S(2)}, u32[]{:S(2)}) collective-permute-start(bf16[320,768]{1,0:T(8,128)(2,1)} %collective-permute-done.8), channel_id=1, source_target_pairs={{4,0},{5,1},{6,2},{7,3},{0,4},{1,5},{2,6},{3,7},{12,8},{13,9},{14,... | collective-permute-start | bytes 1474568 | tf_op jit(solution)/shard_map/ppermute | solution.py:83
  70.0 1.0 copy-start.3
  71.0 2.9 %copy-start.4 = (bf16[768,192]{0,1:T(8,128)(2,1)S(1)}, bf16[768,192]{0,1:T(8,128)(2,1)}, u32[]{:S(2)}) copy-start(bf16[768,192]{0,1:T(8,128)(2,1)} %param.6) | copy-start | bytes 884740
  73.9 4.7 %copy-start = (f32[1280,768]{1,0:T(8,128)}, f32[1280,768]{1,0:T(8,128)S(1)}, u32[]{:S(2)}) copy-start(f32[1280,768]{1,0:T(8,128)S(1)} %get-tuple-element.18) | copy-start | bytes 11796484
  73.9 1.4 %copy-start.7 = (bf16[320,768]{1,0:T(8,128)(2,1)S(1)}, bf16[320,768]{1,0:T(8,128)(2,1)}, u32[]{:S(2)}) copy-start(bf16[320,768]{1,0:T(8,128)(2,1)} %param.4) | copy-start | bytes 1474564
  78.5 1.9 %copy-start.1 = (f32[1280,768]{1,0:T(8,128)}, f32[1280,768]{1,0:T(8,128)S(1)}, u32[]{:S(2)}) copy-start(f32[1280,768]{1,0:T(8,128)S(1)} %get-tuple-element.20) | copy-start | bytes 11796484
  87.1 2.3 %copy-start.2 = (f32[1280,768]{1,0:T(8,128)S(1)}, f32[1280,768]{1,0:T(8,128)}, u32[]{:S(2)}) copy-start(f32[1280,768]{1,0:T(8,128)} %copy-done.1) | copy-start | bytes 11796484
  91.5 2.7 %copy-start.8 = (f32[320,768]{1,0:T(8,128)S(1)}, f32[320,768]{1,0:T(8,128)}, u32[]{:S(2)}) copy-start(f32[320,768]{1,0:T(8,128)} %get-tuple-element.24) | copy-start | bytes 2949124

commit v2 on v1

v2 whole, which is shorter than its diff:
```python
import jax
import jax.numpy as jnp
from jax import lax
from jax.experimental import pallas as pl
from jax.experimental.pallas import tpu as pltpu
from jax.sharding import PartitionSpec as P

LOGIT_SCALE = 10.0
LOGIT_BIAS = -2.0
EPSILON = 1e-06
AXES = ("blk", "head")
LANES = 128


class Grid:
    def __init__(self, n_blk, n_head):
        self.n_blk, self.n_head = n_blk, n_head
        self.half = n_blk // 2
        self.depth = 2 * n_head

    def route(self, source):
        return [(source(d), d) for d in range(self.n_blk * self.n_head)]

    def along_blk(self, even, odd):
        def source(d):
            blk, head = divmod(d, self.n_head)
            step = odd if blk % 2 else even
            return (blk + step) % self.n_blk * self.n_head + head

        return self.route(source)

    def along_z(self, even, odd):
        def source(d):
            blk, head = divmod(d, self.n_head)
            z = 2 * head + blk // self.half
            z = (z + (odd if z % 2 else even)) % self.depth
            return (blk % self.half + self.half * (z % 2)) * self.n_head + z // 2

        return self.route(source)


def dot(left, right, left_dim=1, right_dim=0):
    return lax.dot_general(
        left, right, (((left_dim,), (right_dim,)), ((), ())), preferred_element_type=jnp.float32
    )


def stack(shards, whole):
    at = 0
    for shard in shards:
        whole[at : at + shard.shape[0], :] = shard[...]
        at += shard.shape[0]


def project(feats, whole):
    z = dot(feats, whole[...], 1, 1)
    back = 1.0 / jnp.sqrt(jnp.sum(z * z, axis=1, keepdims=True) + EPSILON)
    return z, back, (z * back).astype(jnp.bfloat16)


def window(group, width):
    start = group * width // LANES * LANES
    return pl.multiple_of(start, LANES), pl.multiple_of(group * width - start, 64)


def primary_kernel(group, own, r1, r2, r3, w0, w1, w2, w3, u_out, z_out, back_out, cut_out, whole):
    rows = own.shape[0]
    stack((w0, w1, w2, w3), whole)
    start, _ = window(group[0], w0.shape[0])
    cut_out[...] = whole[:, pl.ds(start, cut_out.shape[1])]
    for k, block in enumerate((own, r1, r2, r3)):
        z, back, u = project(block[...], whole)
        u_out[k * rows : (k + 1) * rows, :] = u
        if k == 0:
            z_out[...] = z
            back_out[...] = back


def side(u_own, u_others, z, back, cut, logits_ref, at):
    rows = u_own.shape[0]
    logits = LOGIT_SCALE * dot(u_own, u_others[...], 1, 1) + LOGIT_BIAS
    logits_ref[at] = logits
    own = logits[:, :rows]
    turn = jnp.where(
        lax.broadcasted_iota(jnp.int32, own.shape, 0) == lax.broadcasted_iota(jnp.int32, own.shape, 1),
        -1.0,
        1.0,
    )
    w_own = (turn * LOGIT_SCALE / (1.0 + jnp.exp(-turn * own))).astype(jnp.bfloat16)
    w = (LOGIT_SCALE / (1.0 + jnp.exp(-logits[:, rows:]))).astype(jnp.bfloat16)
    g = dot(w_own, u_others[:rows, :]) + dot(w, u_others[rows:, :])
    inner = jnp.sum(g * z, axis=1, keepdims=True)
    dz = (g * back - z * (inner * back * back * back)).astype(jnp.bfloat16)
    return jnp.transpose(dot(dz, cut))


def main_kernel(
    place, own, s123, w0, w123, u_p, z_p, back_p, cut_p, image_out, text_out, loss_out,
    whole, u_q, logits_ref, grads,
):
    group, swapped = place[0], place[1]
    rows, width = own.shape[0], w0.shape[0]
    stack((w0, w123), whole)
    start, offset = window(group, width)
    z_q, back_q, u = project(own[...], whole)
    u_q[:rows, :] = u
    for k in range(3):
        _, _, u = project(s123[k * rows : (k + 1) * rows, :], whole)
        u_q[(k + 1) * rows : (k + 2) * rows, :] = u
    cut_q = whole[:, pl.ds(start, cut_p.shape[1])]
    grads[0] = side(u_p[:rows, :], u_q, z_p[...], back_p[...], cut_p[...], logits_ref, 0)
    grads[1] = side(u_q[:rows, :], u_p, z_q, back_q, cut_q, logits_ref, 1)
    image_out[...] = grads[swapped, pl.ds(offset, width), :].astype(image_out.dtype)
    text_out[...] = grads[1 - swapped, pl.ds(offset, width), :].astype(text_out.dtype)
    quarter = loss_out.shape[1]
    first = pl.multiple_of(group * quarter, 8)
    x = logits_ref[swapped, pl.ds(first, quarter), :]
    on = first + lax.broadcasted_iota(jnp.int32, x.shape, 0) == lax.broadcasted_iota(
        jnp.int32, x.shape, 1
    )
    x = jnp.where(on, -x, x)
    loss = jnp.sum(jnp.maximum(x, 0.0) + jnp.log1p(jnp.exp(-jnp.abs(x))), axis=1, keepdims=True)
    loss_out[...] = jnp.transpose(jnp.broadcast_to(loss, (quarter, LANES)))[:1, :]


VMEM = pl.BlockSpec(memory_space=pltpu.VMEM)
SMEM = pl.BlockSpec(memory_space=pltpu.SMEM)
PARAMS = pltpu.CompilerParams(vmem_limit_bytes=48 * 1024 * 1024)


def body(image_feats, text_feats, image_head, text_head):
    rows, depth = image_feats.shape
    groups = lax.axis_size("head")
    grid = Grid(lax.axis_size("blk"), groups)
    group = lax.axis_index("head")
    odd = lax.axis_index("blk") % 2
    even = odd == 0

    def permute(block, route):
        return lax.ppermute(block, AXES, route)

    swap = grid.along_blk(1, -1)
    image_head, text_head = image_head.T, text_head.T
    width, features = image_head.shape[0], image_head.shape[0] * groups
    own_p = jnp.where(even, image_feats, text_feats)
    own_q = jnp.where(even, text_feats, image_feats)
    head_p = jnp.where(even, image_head, text_head)
    head_q = jnp.where(even, text_head, image_head)
    r1 = permute(own_q, grid.along_blk(-1, 1))
    r2 = permute(own_p, grid.along_blk(-2, 2))
    r3 = permute(own_q, grid.along_blk(-3, 3))
    taken = [permute(head_p, grid.along_z(*way)) for way in ((-3, 3), (2, -2), (-1, 1))]
    s123 = permute(jnp.concatenate([own_p, r1, r2], axis=0), swap)
    w123 = permute(jnp.concatenate(taken, axis=0), swap)

    place = jnp.stack([group, odd]).astype(jnp.int32)
    cut = 2 * LANES
    whole = pltpu.VMEM((features, depth), jnp.bfloat16)
    u_p, z_p, back_p, cut_p = pl.pallas_call(
        primary_kernel,
        out_shape=(
            jax.ShapeDtypeStruct((4 * rows, features), jnp.bfloat16),
            jax.ShapeDtypeStruct((rows, features), jnp.float32),
            jax.ShapeDtypeStruct((rows, 1), jnp.float32),
            jax.ShapeDtypeStruct((features, cut), jnp.bfloat16),
        ),
        in_specs=[SMEM] + [VMEM] * 8,
        out_specs=(VMEM,) * 4,
        scratch_shapes=[whole],
        compiler_params=PARAMS,
        cost_estimate=pl.CostEstimate(
            flops=8 * rows * depth * features, bytes_accessed=8_000_000, transcendentals=0
        ),
    )(place, own_p, r1, r2, r3, head_p, *taken)
    image_grad, text_grad, loss = pl.pallas_call(
        main_kernel,
        out_shape=(
            jax.ShapeDtypeStruct((width, rows), jnp.bfloat16),
            jax.ShapeDtypeStruct((width, rows), jnp.bfloat16),
            jax.ShapeDtypeStruct((1, rows // groups), jnp.float32),
        ),
        in_specs=[SMEM] + [VMEM] * 8,
        out_specs=(VMEM,) * 3,
        scratch_shapes=[
            whole,
            pltpu.VMEM((4 * rows, features), jnp.bfloat16),
            pltpu.VMEM((2, rows, 4 * rows), jnp.float32),
            pltpu.VMEM((2, cut, rows), jnp.float32),
        ],
        compiler_params=PARAMS,
        cost_estimate=pl.CostEstimate(
            flops=24 * rows * depth * features, bytes_accessed=8_000_000, transcendentals=0
        ),
    )(place, own_q, s123, head_q, w123, u_p, z_p, back_p, cut_p)
    return image_grad.T, text_grad.T, loss.reshape(rows // groups)


def solution(mesh):
    in_specs = (P("blk", None), P("blk", None), P(None, "head"), P(None, "head"))
    out_specs = (P("blk", "head"), P("blk", "head"), P(("blk", "head")))
    return jax.shard_map(body, mesh=mesh, in_specs=in_specs, out_specs=out_specs, check_vma=False)
```

time: 97.5 us -> 104 us (1.067)
  the two profiles are of different devices: /device:TPU:2 before, /device:TPU:127 now
where the time goes in v2:
time: 104 us
  waiting for transfers between devices  53.1 us (51%)
  starting transfers between devices  33 us (32%)
  Pallas kernels  13.6 us (13%)
  other arithmetic  3.58 us (3%)
    ppermute x8, waiting for transfers between devices, permute(): return lax.ppermute(block, AXES, route)  53.1 us
    ppermute x8, starting transfers between devices, permute(): return lax.ppermute(block, AXES, route)  33 us
    pallas_call x1, Pallas kernels, body(): pl.pallas_call(main_kernel, out_shape=(jax.ShapeDtypeStruct((width, rows)...  9.36 us
    pallas_call x1, Pallas kernels, body(): pl.pallas_call(primary_kernel, out_shape=(jax.ShapeDtypeStruct((4 * rows,...  4.23 us
  transfers between devices with their start and end apart: 8, of which 6 were waited for; matrix products, arithmetic and copies ran while one was open for 1% of the time, Pallas kernels for 4%

profile of v2, /device:TPU:127, one launch (start us, length us, event | category | flops | bytes accessed | tf_op | source)
XLA Modules:
  0.0 104.0 jit_solution(14209806339512095600)
XLA Ops:
  0.6 1.2 %broadcast_select_fusion = (bf16[320,768]{1,0:T(8,128)(2,1)S(1)}, bf16[320,768]{1,0:T(8,128)(2,1)S(1)}) fusion(bf16[320,768]{1,0:T(8,128)(2,1)} %param.4, bf16[320,768]{1,0:T(8,128)(2,1)} %param.5, pred[]{:T(512)S(6)} %eq.5), kind=kLoop, calls=%fused_computation.2 | loop fusion | flops 491520 | bytes 1966081 | tf_op jit(solution)/shard_map/jit(_where)/select_n | solution.py:145
  1.9 0.0 copy-start
  1.9 0.0 copy-start.1
  1.9 3.8 %collective-permute-start = (bf16[320,768]{1,0:T(8,128)(2,1)S(1)}, bf16[320,768]{1,0:T(8,128)(2,1)S(1)}, u32[]{:S(2)}, u32[]{:S(2)}) collective-permute-start(bf16[320,768]{1,0:T(8,128)(2,1)S(1)} %get-tuple-element.18.own), channel_id=1, source_target_pairs={{1020,0},{1021,1},{1022,2},{1023,3},{8,4},{9,5},{10,6},{11,7},{4,8... | collective-permute-start | bytes 1474568 | tf_op jit(solution)/shard_map/ppermute | solution.py:140
  5.7 2.2 %collective-permute-start.1 = (bf16[320,768]{1,0:T(8,128)(2,1)S(1)}, bf16[320,768]{1,0:T(8,128)(2,1)S(1)}, u32[]{:S(2)}, u32[]{:S(2)}) collective-permute-start(bf16[320,768]{1,0:T(8,128)(2,1)S(1)} %get-tuple-element.17.own), channel_id=1, source_target_pairs={{1016,0},{1017,1},{1018,2},{1019,3},{12,4},{13,5},{14,6},{15,7},{0... | collective-permute-start | bytes 1474568 | tf_op jit(solution)/shard_map/ppermute | solution.py:140
  7.9 10.6 %collective-permute-done.r1 = bf16[320,768]{1,0:T(8,128)(2,1)S(1)} collective-permute-done((bf16[320,768]{1,0:T(8,128)(2,1)S(1)}, bf16[320,768]{1,0:T(8,128)(2,1)S(1)}, u32[]{:S(2)}, u32[]{:S(2)}) %collective-permute-start) | collective-permute-done | bytes 491552 | tf_op jit(solution)/shard_map/ppermute | solution.py:140
  18.5 3.2 %collective-permute-done.1.r2 = bf16[320,768]{1,0:T(8,128)(2,1)S(1)} collective-permute-done((bf16[320,768]{1,0:T(8,128)(2,1)S(1)}, bf16[320,768]{1,0:T(8,128)(2,1)S(1)}, u32[]{:S(2)}, u32[]{:S(2)}) %collective-permute-start.1) | collective-permute-done | bytes 491552 | tf_op jit(solution)/shard_map/ppermute | solution.py:140
  21.7 1.2 %pad_maximum_fusion = bf16[960,768]{1,0:T(8,128)(2,1)} fusion(bf16[320,768]{1,0:T(8,128)(2,1)S(1)} %collective-permute-done.1.r2, bf16[320,768]{1,0:T(8,128)(2,1)S(1)} %collective-permute-done.r1, bf16[320,768]{1,0:T(8,128)(2,1)S(1)} %get-tuple-element.17.own), kind=kLoop, calls=%fused_computation | loop fusion | flops 4423680 | bytes 2949120 | tf_op jit(solution)/shard_map/concatenate | solution.py:153
  22.9 1.9 %collective-permute-start.2 = (bf16[960,768]{1,0:T(8,128)(2,1)}, bf16[960,768]{1,0:T(8,128)(2,1)}, u32[]{:S(2)}, u32[]{:S(2)}) collective-permute-start(bf16[960,768]{1,0:T(8,128)(2,1)} %pad_maximum_fusion), channel_id=1, source_target_pairs={{4,0},{5,1},{6,2},{7,3},{0,4},{1,5},{2,6},{3,7},{12,8},{13,9},{14,... | collective-permute-start | bytes 4423688 | tf_op jit(solution)/shard_map/ppermute | solution.py:140
  24.8 0.0 copy-done
  24.8 0.0 copy-done.1
  24.9 15.2 %collective-permute-start.3 = (bf16[192,768]{1,0:T(8,128)(2,1)S(1)}, bf16[192,768]{1,0:T(8,128)(2,1)S(1)}, u32[]{:S(2)}, u32[]{:S(2)}) collective-permute-start(bf16[192,768]{1,0:T(8,128)(2,1)S(1)} %get-tuple-element.19.w0), channel_id=1, source_target_pairs={{514,0},{515,1},{512,2},{513,3},{518,4},{519,5},{516,6},{517,7},{5... | collective-permute-start | bytes 884744 | tf_op jit(solution)/shard_map/ppermute | solution.py:140
  40.1 2.8 %collective-permute-start.4 = (bf16[192,768]{1,0:T(8,128)(2,1)S(1)}, bf16[192,768]{1,0:T(8,128)(2,1)S(1)}, u32[]{:S(2)}, u32[]{:S(2)}) collective-permute-start(bf16[192,768]{1,0:T(8,128)(2,1)S(1)} %get-tuple-element.19.w0), channel_id=1, source_target_pairs={{1,0},{2,1},{3,2},{0,3},{5,4},{6,5},{7,6},{4,7},{9,8},{10,9},{11,1... | collective-permute-start | bytes 884744 | tf_op jit(solution)/shard_map/ppermute | solution.py:140
  42.9 2.8 %collective-permute-start.5 = (bf16[192,768]{1,0:T(8,128)(2,1)S(1)}, bf16[192,768]{1,0:T(8,128)(2,1)S(1)}, u32[]{:S(2)}, u32[]{:S(2)}) collective-permute-start(bf16[192,768]{1,0:T(8,128)(2,1)S(1)} %get-tuple-element.19.w0), channel_id=1, source_target_pairs={{515,0},{512,1},{513,2},{514,3},{519,4},{516,5},{517,6},{518,7},{5... | collective-permute-start | bytes 884744 | tf_op jit(solution)/shard_map/ppermute | solution.py:140
  45.8 1.6 %collective-permute-done.3.w1 = bf16[192,768]{1,0:T(8,128)(2,1)S(1)} collective-permute-done((bf16[192,768]{1,0:T(8,128)(2,1)S(1)}, bf16[192,768]{1,0:T(8,128)(2,1)S(1)}, u32[]{:S(2)}, u32[]{:S(2)}) %collective-permute-start.3) | collective-permute-done | bytes 294944 | tf_op jit(solution)/shard_map/ppermute | solution.py:140
  47.4 12.9 %collective-permute-done.4.w2 = bf16[192,768]{1,0:T(8,128)(2,1)S(1)} collective-permute-done((bf16[192,768]{1,0:T(8,128)(2,1)S(1)}, bf16[192,768]{1,0:T(8,128)(2,1)S(1)}, u32[]{:S(2)}, u32[]{:S(2)}) %collective-permute-start.4) | collective-permute-done | bytes 294944 | tf_op jit(solution)/shard_map/ppermute | solution.py:140
  60.3 6.3 %collective-permute-done.5.w3 = bf16[192,768]{1,0:T(8,128)(2,1)S(1)} collective-permute-done((bf16[192,768]{1,0:T(8,128)(2,1)S(1)}, bf16[192,768]{1,0:T(8,128)(2,1)S(1)}, u32[]{:S(2)}, u32[]{:S(2)}) %collective-permute-start.5) | collective-permute-done | bytes 294944 | tf_op jit(solution)/shard_map/ppermute | solution.py:140
  66.5 1.0 pad_maximum_fusion.1
  67.5 2.4 %collective-permute-start.6 = (bf16[576,768]{1,0:T(8,128)(2,1)}, bf16[576,768]{1,0:T(8,128)(2,1)}, u32[]{:S(2)}, u32[]{:S(2)}) collective-permute-start(bf16[576,768]{1,0:T(8,128)(2,1)} %pad_maximum_fusion.1), channel_id=1, source_target_pairs={{4,0},{5,1},{6,2},{7,3},{0,4},{1,5},{2,6},{3,7},{12,8},{13,9},{14,... | collective-permute-start | bytes 2654216 | tf_op jit(solution)/shard_map/ppermute | solution.py:140
  69.9 1.9 %collective-permute-start.7 = (bf16[320,768]{1,0:T(8,128)(2,1)S(1)}, bf16[320,768]{1,0:T(8,128)(2,1)}, u32[]{:S(2)}, u32[]{:S(2)}) collective-permute-start(bf16[320,768]{1,0:T(8,128)(2,1)S(1)} %get-tuple-element.18.own), channel_id=1, source_target_pairs={{1012,0},{1013,1},{1014,2},{1015,3},{16,4},{17,5},{18,6},{19,7},{1... | collective-permute-start | bytes 1474568 | tf_op jit(solution)/shard_map/ppermute | solution.py:140
  71.8 0.1 pad_add_fusion.group.place
  71.9 18.5 %collective-permute-done.7.r3 = bf16[320,768]{1,0:T(8,128)(2,1)} collective-permute-done((bf16[320,768]{1,0:T(8,128)(2,1)S(1)}, bf16[320,768]{1,0:T(8,128)(2,1)}, u32[]{:S(2)}, u32[]{:S(2)}) %collective-permute-start.7) | collective-permute-done | bytes 491552 | tf_op jit(solution)/shard_map/ppermute | solution.py:140
  90.4 4.2 %shard_map.67 = (bf16[1280,768]{1,0:T(8,128)(2,1)}, f32[320,768]{1,0:T(8,128)S(1)}, f32[320,1]{1,0:T(8,128)S(1)}, bf16[768,256]{1,0:T(8,128)(2,1)S(1)}) custom-call(s32[2]{0:T(128)S(1)} %pad_add_fusion.group.place, bf16[320,768]{1,0:T(8,128)(2,1)S(1)} %get-tuple-element.17.own, bf16[320,768]{1,0:T(8,128)(2,1)S(1)} %collective-permute-done.r1, ...), custom_call_target="tpu_custom_call" | custom-call | flops 1509949440 | bytes 8000000 | tf_op jit(solution)/shard_map/pallas_call | solution.py:159
  94.7 0.0 collective-permute-done.6.w123
  94.7 0.0 collective-permute-done.2.s123
  94.7 9.4 %shard_map.68 = (bf16[192,320]{1,0:T(8,128)(2,1)}, bf16[192,320]{1,0:T(8,128)(2,1)}, f32[1,80]{1,0:T(1,128)}) custom-call(s32[2]{0:T(128)S(1)} %pad_add_fusion.group.place, bf16[320,768]{1,0:T(8,128)(2,1)S(1)} %get-tuple-element.18.own, bf16[960,768]{1,0:T(8,128)(2,1)} %collective-permute-done.2.s123, bf16[192,768]{1,0:T(8,128)(2,1)S(1)} %get-tuple-element.20.w0, ...), custom_call_target="tpu_custom_call" | custom-call | flops 4529848320 | bytes 8000000 | tf_op jit(solution)/shard_map/pallas_call | solution.py:175
  (1 shorter events, 0.0 us)
Async XLA Ops:
  1.9 22.9 %copy-start = (bf16[768,192]{0,1:T(8,128)(2,1)S(1)}, bf16[768,192]{0,1:T(8,128)(2,1)}, u32[]{:S(2)}) copy-start(bf16[768,192]{0,1:T(8,128)(2,1)} %param.6) | copy-start | bytes 884740
  1.9 22.9 %copy-start.1 = (bf16[768,192]{0,1:T(8,128)(2,1)S(1)}, bf16[768,192]{0,1:T(8,128)(2,1)}, u32[]{:S(2)}) copy-start(bf16[768,192]{0,1:T(8,128)(2,1)} %param.7) | copy-start | bytes 884740
  1.9 16.6 %collective-permute-start = (bf16[320,768]{1,0:T(8,128)(2,1)S(1)}, bf16[320,768]{1,0:T(8,128)(2,1)S(1)}, u32[]{:S(2)}, u32[]{:S(2)}) collective-permute-start(bf16[320,768]{1,0:T(8,128)(2,1)S(1)} %get-tuple-element.18.own), channel_id=1, source_target_pairs={{1020,0},{1021,1},{1022,2},{1023,3},{8,4},{9,5},{10,6},{11,7},{4,8... | collective-permute-start | bytes 1474568 | tf_op jit(solution)/shard_map/ppermute | solution.py:140
  5.7 15.9 %collective-permute-start.1 = (bf16[320,768]{1,0:T(8,128)(2,1)S(1)}, bf16[320,768]{1,0:T(8,128)(2,1)S(1)}, u32[]{:S(2)}, u32[]{:S(2)}) collective-permute-start(bf16[320,768]{1,0:T(8,128)(2,1)S(1)} %get-tuple-element.17.own), channel_id=1, source_target_pairs={{1016,0},{1017,1},{1018,2},{1019,3},{12,4},{13,5},{14,6},{15,7},{0... | collective-permute-start | bytes 1474568 | tf_op jit(solution)/shard_map/ppermute | solution.py:140
  22.9 71.8 %collective-permute-start.2 = (bf16[960,768]{1,0:T(8,128)(2,1)}, bf16[960,768]{1,0:T(8,128)(2,1)}, u32[]{:S(2)}, u32[]{:S(2)}) collective-permute-start(bf16[960,768]{1,0:T(8,128)(2,1)} %pad_maximum_fusion), channel_id=1, source_target_pairs={{4,0},{5,1},{6,2},{7,3},{0,4},{1,5},{2,6},{3,7},{12,8},{13,9},{14,... | collective-permute-start | bytes 4423688 | tf_op jit(solution)/shard_map/ppermute | solution.py:140
  24.9 22.5 %collective-permute-start.3 = (bf16[192,768]{1,0:T(8,128)(2,1)S(1)}, bf16[192,768]{1,0:T(8,128)(2,1)S(1)}, u32[]{:S(2)}, u32[]{:S(2)}) collective-permute-start(bf16[192,768]{1,0:T(8,128)(2,1)S(1)} %get-tuple-element.19.w0), channel_id=1, source_target_pairs={{514,0},{515,1},{512,2},{513,3},{518,4},{519,5},{516,6},{517,7},{5... | collective-permute-start | bytes 884744 | tf_op jit(solution)/shard_map/ppermute | solution.py:140
  40.1 20.2 %collective-permute-start.4 = (bf16[192,768]{1,0:T(8,128)(2,1)S(1)}, bf16[192,768]{1,0:T(8,128)(2,1)S(1)}, u32[]{:S(2)}, u32[]{:S(2)}) collective-permute-start(bf16[192,768]{1,0:T(8,128)(2,1)S(1)} %get-tuple-element.19.w0), channel_id=1, source_target_pairs={{1,0},{2,1},{3,2},{0,3},{5,4},{6,5},{7,6},{4,7},{9,8},{10,9},{11,1... | collective-permute-start | bytes 884744 | tf_op jit(solution)/shard_map/ppermute | solution.py:140
  42.9 23.6 %collective-permute-start.5 = (bf16[192,768]{1,0:T(8,128)(2,1)S(1)}, bf16[192,768]{1,0:T(8,128)(2,1)S(1)}, u32[]{:S(2)}, u32[]{:S(2)}) collective-permute-start(bf16[192,768]{1,0:T(8,128)(2,1)S(1)} %get-tuple-element.19.w0), channel_id=1, source_target_pairs={{515,0},{512,1},{513,2},{514,3},{519,4},{516,5},{517,6},{518,7},{5... | collective-permute-start | bytes 884744 | tf_op jit(solution)/shard_map/ppermute | solution.py:140
  67.5 27.1 %collective-permute-start.6 = (bf16[576,768]{1,0:T(8,128)(2,1)}, bf16[576,768]{1,0:T(8,128)(2,1)}, u32[]{:S(2)}, u32[]{:S(2)}) collective-permute-start(bf16[576,768]{1,0:T(8,128)(2,1)} %pad_maximum_fusion.1), channel_id=1, source_target_pairs={{4,0},{5,1},{6,2},{7,3},{0,4},{1,5},{2,6},{3,7},{12,8},{13,9},{14,... | collective-permute-start | bytes 2654216 | tf_op jit(solution)/shard_map/ppermute | solution.py:140
  69.9 20.5 %collective-permute-start.7 = (bf16[320,768]{1,0:T(8,128)(2,1)S(1)}, bf16[320,768]{1,0:T(8,128)(2,1)}, u32[]{:S(2)}, u32[]{:S(2)}) collective-permute-start(bf16[320,768]{1,0:T(8,128)(2,1)S(1)} %get-tuple-element.18.own), channel_id=1, source_target_pairs={{1012,0},{1013,1},{1014,2},{1015,3},{16,4},{17,5},{18,6},{19,7},{1... | collective-permute-start | bytes 1474568 | tf_op jit(solution)/shard_map/ppermute | solution.py:140

commit v3 on v2

--- a/solution.py
+++ b/solution.py
@@ -8,6 +8,7 @@
 LOGIT_SCALE = 10.0
 LOGIT_BIAS = -2.0
 EPSILON = 1e-06
+PACK = 20_000_000_000
 AXES = ("blk", "head")
 LANES = 128
 
@@ -74,6 +75,11 @@
         if k == 0:
             z_out[...] = z
             back_out[...] = back
+
+
+def pack_kernel(*refs):
+    *blocks, out = refs
+    stack(blocks, out)
 
 
 def side(u_own, u_others, z, back, cut, logits_ref, at):
@@ -128,6 +134,18 @@
 PARAMS = pltpu.CompilerParams(vmem_limit_bytes=48 * 1024 * 1024)
 
 
+def pack(*blocks):
+    rows = sum(block.shape[0] for block in blocks)
+    return pl.pallas_call(
+        pack_kernel,
+        out_shape=jax.ShapeDtypeStruct((rows, blocks[0].shape[1]), blocks[0].dtype),
+        in_specs=[VMEM] * len(blocks),
+        out_specs=VMEM,
+        compiler_params=PARAMS,
+        cost_estimate=pl.CostEstimate(flops=PACK, bytes_accessed=4_000_000, transcendentals=0),
+    )(*blocks)
+
+
 def body(image_feats, text_feats, image_head, text_head):
     rows, depth = image_feats.shape
     groups = lax.axis_size("head")
@@ -146,12 +164,16 @@
     own_q = jnp.where(even, text_feats, image_feats)
     head_p = jnp.where(even, image_head, text_head)
     head_q = jnp.where(even, text_head, image_head)
+    near = grid.along_z(-1, 1)
+    w1 = permute(head_p, near)
+    w2 = permute(head_p, grid.along_z(2, -2))
     r1 = permute(own_q, grid.along_blk(-1, 1))
     r2 = permute(own_p, grid.along_blk(-2, 2))
-    r3 = permute(own_q, grid.along_blk(-3, 3))
-    taken = [permute(head_p, grid.along_z(*way)) for way in ((-3, 3), (2, -2), (-1, 1))]
-    s123 = permute(jnp.concatenate([own_p, r1, r2], axis=0), swap)
-    w123 = permute(jnp.concatenate(taken, axis=0), swap)
+    w3 = permute(w2, near)
+    r3 = permute(r1, grid.along_blk(-2, 2))
+    taken = [w1, w2, w3]
+    s123 = permute(pack(own_p, r1, r2), swap)
+    w123 = permute(pack(*taken), swap)
 
     place = jnp.stack([group, odd]).astype(jnp.int32)
     cut = 2 * LANES
@@ -169,7 +191,7 @@
         scratch_shapes=[whole],
         compiler_params=PARAMS,
         cost_estimate=pl.CostEstimate(
-            flops=8 * rows * depth * features, bytes_accessed=8_000_000, transcendentals=0
+            flops=80 * rows * depth * features, bytes_accessed=8_000_000, transcendentals=0
         ),
     )(place, own_p, r1, r2, r3, head_p, *taken)
     image_grad, text_grad, loss = pl.pallas_call(

time: 104 us -> 75 us (0.72)
  waiting for transfers between devices: 53.1 us -> 10.8 us
  starting transfers between devices: 33 us -> 48.8 us
  other arithmetic: 3.58 us -> 1.43 us
    ppermute x8, waiting for transfers between devices: 53.1 us -> 10.8 us  [permute(): return lax.ppermute(block, AXES, route)]
    ppermute x8, starting transfers between devices: 33 us -> 48.8 us  [permute(): return lax.ppermute(block, AXES, route)]
    concatenate x2 -> x0, other arithmetic: 2.21 us -> none  [the longest x1 1.22 us: body(): s123 = permute(jnp.concatenate([own_p, r1, r2], axis=0), swap)]
  transfers between devices with their start and end apart: 8 -> 8, of which waited for: 6 -> 2; matrix products, arithmetic and copies ran while one was open for 1% -> 0% of each run, Pallas kernels for 4% -> 5%
where the time goes in v3:
time: 75 us; the launch traced here: 74.6 us
  starting transfers between devices  48.8 us (65%)
  Pallas kernels  12.7 us (17%)
  waiting for transfers between devices  10.8 us (14%)
  other arithmetic  1.43 us (2%)
  between operations  0.81 us (1%)
    ppermute x8, starting transfers between devices, permute(): return lax.ppermute(block, AXES, route)  48.8 us
    ppermute x8, waiting for transfers between devices, permute(): return lax.ppermute(block, AXES, route)  10.8 us
    pallas_call x1, Pallas kernels, body(): pl.pallas_call(main_kernel, out_shape=(jax.ShapeDtypeStruct((width, rows)...  8.79 us
    pallas_call x1, Pallas kernels, body(): pl.pallas_call(primary_kernel, out_shape=(jax.ShapeDtypeStruct((4 * rows,...  3.75 us
  transfers between devices with their start and end apart: 8, of which 2 were waited for; matrix products, arithmetic and copies ran while one was open for 0% of the time, Pallas kernels for 5%

profile of v3, /device:TPU:127, one launch (start us, length us, event | category | flops | bytes accessed | tf_op | source)
XLA Modules:
  0.0 74.6 jit_solution(6000639843777289975)
XLA Ops:
  0.6 0.0 copy-start
  0.6 0.0 copy-start.1
  0.7 1.3 %broadcast_select_fusion = (bf16[320,768]{1,0:T(8,128)(2,1)S(1)}, bf16[320,768]{1,0:T(8,128)(2,1)S(1)}) fusion(bf16[320,768]{1,0:T(8,128)(2,1)} %param.4, bf16[320,768]{1,0:T(8,128)(2,1)} %param.5, pred[]{:T(512)S(6)} %eq.5), kind=kLoop, calls=%fused_computation | loop fusion | flops 491520 | bytes 1966081 | tf_op jit(solution)/shard_map/jit(_where)/select_n | solution.py:163
  2.0 3.7 %collective-permute-start = (bf16[320,768]{1,0:T(8,128)(2,1)S(1)}, bf16[320,768]{1,0:T(8,128)(2,1)S(1)}, u32[]{:S(2)}, u32[]{:S(2)}) collective-permute-start(bf16[320,768]{1,0:T(8,128)(2,1)S(1)} %get-tuple-element.18.own), channel_id=1, source_target_pairs={{1020,0},{1021,1},{1022,2},{1023,3},{8,4},{9,5},{10,6},{11,7},{4,8... | collective-permute-start | bytes 1474568 | tf_op jit(solution)/shard_map/ppermute | solution.py:158
  5.7 2.2 %collective-permute-start.1 = (bf16[320,768]{1,0:T(8,128)(2,1)S(1)}, bf16[320,768]{1,0:T(8,128)(2,1)S(1)}, u32[]{:S(2)}, u32[]{:S(2)}) collective-permute-start(bf16[320,768]{1,0:T(8,128)(2,1)S(1)} %get-tuple-element.17.refs_0_.own), channel_id=1, source_target_pairs={{1016,0},{1017,1},{1018,2},{1019,3},{12,4},{13,5},{14,6},{15,7},{0... | collective-permute-start | bytes 1474568 | tf_op jit(solution)/shard_map/ppermute | solution.py:158
  7.8 0.0 copy-done
  7.8 0.0 copy-done.1
  7.9 16.1 %collective-permute-start.4 = (bf16[192,768]{1,0:T(8,128)(2,1)S(1)}, bf16[192,768]{1,0:T(8,128)(2,1)S(1)}, u32[]{:S(2)}, u32[]{:S(2)}) collective-permute-start(bf16[192,768]{1,0:T(8,128)(2,1)S(1)} %get-tuple-element.19.w0), channel_id=1, source_target_pairs={{1,0},{2,1},{3,2},{0,3},{5,4},{6,5},{7,6},{4,7},{9,8},{10,9},{11,1... | collective-permute-start | bytes 884744 | tf_op jit(solution)/shard_map/ppermute | solution.py:158
  24.0 2.8 %collective-permute-start.3 = (bf16[192,768]{1,0:T(8,128)(2,1)S(1)}, bf16[192,768]{1,0:T(8,128)(2,1)S(1)}, u32[]{:S(2)}, u32[]{:S(2)}) collective-permute-start(bf16[192,768]{1,0:T(8,128)(2,1)S(1)} %get-tuple-element.19.w0), channel_id=1, source_target_pairs={{515,0},{512,1},{513,2},{514,3},{519,4},{516,5},{517,6},{518,7},{5... | collective-permute-start | bytes 884744 | tf_op jit(solution)/shard_map/ppermute | solution.py:158
  26.9 0.1 pad_add_fusion.group.place
  27.0 1.7 %collective-permute-done.4.refs_1_.w2 = bf16[192,768]{1,0:T(8,128)(2,1)S(1)} collective-permute-done((bf16[192,768]{1,0:T(8,128)(2,1)S(1)}, bf16[192,768]{1,0:T(8,128)(2,1)S(1)}, u32[]{:S(2)}, u32[]{:S(2)}) %collective-permute-start.4) | collective-permute-done | bytes 294944 | tf_op jit(solution)/shard_map/ppermute | solution.py:158
  28.6 11.2 %collective-permute-start.5 = (bf16[192,768]{1,0:T(8,128)(2,1)S(1)}, bf16[192,768]{1,0:T(8,128)(2,1)S(1)}, u32[]{:S(2)}, u32[]{:S(2)}) collective-permute-start(bf16[192,768]{1,0:T(8,128)(2,1)S(1)} %collective-permute-done.4.refs_1_.w2), channel_id=1, source_target_pairs={{515,0},{512,1},{513,2},{514,3},{519,4},{516,5},{517,6},{518,7},{5... | collective-permute-start | bytes 884744 | tf_op jit(solution)/shard_map/ppermute | solution.py:158
  39.8 0.0 collective-permute-done.refs_1_.r1
  39.9 0.0 collective-permute-done.1.refs_2_.r2
  39.9 0.1 shard_map.67
  40.0 8.3 %collective-permute-start.2 = (bf16[960,768]{1,0:T(8,128)(2,1)S(1)}, bf16[960,768]{1,0:T(8,128)(2,1)S(1)}, u32[]{:S(2)}, u32[]{:S(2)}) collective-permute-start(bf16[960,768]{1,0:T(8,128)(2,1)S(1)} %shard_map.67), channel_id=1, source_target_pairs={{4,0},{5,1},{6,2},{7,3},{0,4},{1,5},{2,6},{3,7},{12,8},{13,9},{14,... | collective-permute-start | bytes 4423688 | tf_op jit(solution)/shard_map/ppermute | solution.py:158
  48.3 1.9 %collective-permute-start.7 = (bf16[320,768]{1,0:T(8,128)(2,1)S(1)}, bf16[320,768]{1,0:T(8,128)(2,1)S(1)}, u32[]{:S(2)}, u32[]{:S(2)}) collective-permute-start(bf16[320,768]{1,0:T(8,128)(2,1)S(1)} %collective-permute-done.refs_1_.r1), channel_id=1, source_target_pairs={{1016,0},{1017,1},{1018,2},{1019,3},{12,4},{13,5},{14,6},{15,7},{0... | collective-permute-start | bytes 1474568 | tf_op jit(solution)/shard_map/ppermute | solution.py:158
  50.2 0.0 collective-permute-done.3.refs_0_.w1
  50.2 0.0 collective-permute-done.5.refs_2_.w3
  50.2 0.1 shard_map.68
  50.3 2.6 %collective-permute-start.6 = (bf16[576,768]{1,0:T(8,128)(2,1)S(1)}, bf16[576,768]{1,0:T(8,128)(2,1)S(1)}, u32[]{:S(2)}, u32[]{:S(2)}) collective-permute-start(bf16[576,768]{1,0:T(8,128)(2,1)S(1)} %shard_map.68), channel_id=1, source_target_pairs={{4,0},{5,1},{6,2},{7,3},{0,4},{1,5},{2,6},{3,7},{12,8},{13,9},{14,... | collective-permute-start | bytes 2654216 | tf_op jit(solution)/shard_map/ppermute | solution.py:158
  52.9 9.2 %collective-permute-done.7.r3 = bf16[320,768]{1,0:T(8,128)(2,1)S(1)} collective-permute-done((bf16[320,768]{1,0:T(8,128)(2,1)S(1)}, bf16[320,768]{1,0:T(8,128)(2,1)S(1)}, u32[]{:S(2)}, u32[]{:S(2)}) %collective-permute-start.7) | collective-permute-done | bytes 491552 | tf_op jit(solution)/shard_map/ppermute | solution.py:158
  62.1 3.8 %shard_map.69 = (bf16[1280,768]{1,0:T(8,128)(2,1)}, f32[320,768]{1,0:T(8,128)S(1)}, f32[320,1]{1,0:T(8,128)S(1)}, bf16[768,256]{1,0:T(8,128)(2,1)S(1)}) custom-call(s32[2]{0:T(128)S(1)} %pad_add_fusion.group.place, bf16[320,768]{1,0:T(8,128)(2,1)S(1)} %get-tuple-element.17.refs_0_.own, bf16[320,768]{1,0:T(8,128)(2,1)S(1)} %collective-permute-done.refs_1_.r1, ...), custom_call_target="tpu_custom_call" | custom-call | flops 15099494400 | bytes 8000000 | tf_op jit(solution)/shard_map/pallas_call | solution.py:181
  65.8 0.0 collective-permute-done.6.w123
  65.8 0.0 collective-permute-done.2.s123
  65.8 8.8 %shard_map.70 = (bf16[192,320]{1,0:T(8,128)(2,1)}, bf16[192,320]{1,0:T(8,128)(2,1)}, f32[1,80]{1,0:T(1,128)}) custom-call(s32[2]{0:T(128)S(1)} %pad_add_fusion.group.place, bf16[320,768]{1,0:T(8,128)(2,1)S(1)} %get-tuple-element.18.own, bf16[960,768]{1,0:T(8,128)(2,1)S(1)} %collective-permute-done.2.s123, bf16[192,768]{1,0:T(8,128)(2,1)S(1)} %get-tuple-element.20.w0, ...), custom_call_target="tpu_custom_call" | custom-call | flops 4529848320 | bytes 8000000 | tf_op jit(solution)/shard_map/pallas_call | solution.py:197
  (1 shorter events, 0.0 us)
Async XLA Ops:
  0.6 7.2 %copy-start = (bf16[768,192]{0,1:T(8,128)(2,1)S(1)}, bf16[768,192]{0,1:T(8,128)(2,1)}, u32[]{:S(2)}) copy-start(bf16[768,192]{0,1:T(8,128)(2,1)} %param.6) | copy-start | bytes 884740
  0.6 7.2 %copy-start.1 = (bf16[768,192]{0,1:T(8,128)(2,1)S(1)}, bf16[768,192]{0,1:T(8,128)(2,1)}, u32[]{:S(2)}) copy-start(bf16[768,192]{0,1:T(8,128)(2,1)} %param.7) | copy-start | bytes 884740
  2.0 37.9 %collective-permute-start = (bf16[320,768]{1,0:T(8,128)(2,1)S(1)}, bf16[320,768]{1,0:T(8,128)(2,1)S(1)}, u32[]{:S(2)}, u32[]{:S(2)}) collective-permute-start(bf16[320,768]{1,0:T(8,128)(2,1)S(1)} %get-tuple-element.18.own), channel_id=1, source_target_pairs={{1020,0},{1021,1},{1022,2},{1023,3},{8,4},{9,5},{10,6},{11,7},{4,8... | collective-permute-start | bytes 1474568 | tf_op jit(solution)/shard_map/ppermute | solution.py:158
  5.7 34.2 %collective-permute-start.1 = (bf16[320,768]{1,0:T(8,128)(2,1)S(1)}, bf16[320,768]{1,0:T(8,128)(2,1)S(1)}, u32[]{:S(2)}, u32[]{:S(2)}) collective-permute-start(bf16[320,768]{1,0:T(8,128)(2,1)S(1)} %get-tuple-element.17.refs_0_.own), channel_id=1, source_target_pairs={{1016,0},{1017,1},{1018,2},{1019,3},{12,4},{13,5},{14,6},{15,7},{0... | collective-permute-start | bytes 1474568 | tf_op jit(solution)/shard_map/ppermute | solution.py:158
  7.9 20.7 %collective-permute-start.4 = (bf16[192,768]{1,0:T(8,128)(2,1)S(1)}, bf16[192,768]{1,0:T(8,128)(2,1)S(1)}, u32[]{:S(2)}, u32[]{:S(2)}) collective-permute-start(bf16[192,768]{1,0:T(8,128)(2,1)S(1)} %get-tuple-element.19.w0), channel_id=1, source_target_pairs={{1,0},{2,1},{3,2},{0,3},{5,4},{6,5},{7,6},{4,7},{9,8},{10,9},{11,1... | collective-permute-start | bytes 884744 | tf_op jit(solution)/shard_map/ppermute | solution.py:158
  24.0 26.2 %collective-permute-start.3 = (bf16[192,768]{1,0:T(8,128)(2,1)S(1)}, bf16[192,768]{1,0:T(8,128)(2,1)S(1)}, u32[]{:S(2)}, u32[]{:S(2)}) collective-permute-start(bf16[192,768]{1,0:T(8,128)(2,1)S(1)} %get-tuple-element.19.w0), channel_id=1, source_target_pairs={{515,0},{512,1},{513,2},{514,3},{519,4},{516,5},{517,6},{518,7},{5... | collective-permute-start | bytes 884744 | tf_op jit(solution)/shard_map/ppermute | solution.py:158
  28.6 21.6 %collective-permute-start.5 = (bf16[192,768]{1,0:T(8,128)(2,1)S(1)}, bf16[192,768]{1,0:T(8,128)(2,1)S(1)}, u32[]{:S(2)}, u32[]{:S(2)}) collective-permute-start(bf16[192,768]{1,0:T(8,128)(2,1)S(1)} %collective-permute-done.4.refs_1_.w2), channel_id=1, source_target_pairs={{515,0},{512,1},{513,2},{514,3},{519,4},{516,5},{517,6},{518,7},{5... | collective-permute-start | bytes 884744 | tf_op jit(solution)/shard_map/ppermute | solution.py:158
  40.0 25.8 %collective-permute-start.2 = (bf16[960,768]{1,0:T(8,128)(2,1)S(1)}, bf16[960,768]{1,0:T(8,128)(2,1)S(1)}, u32[]{:S(2)}, u32[]{:S(2)}) collective-permute-start(bf16[960,768]{1,0:T(8,128)(2,1)S(1)} %shard_map.67), channel_id=1, source_target_pairs={{4,0},{5,1},{6,2},{7,3},{0,4},{1,5},{2,6},{3,7},{12,8},{13,9},{14,... | collective-permute-start | bytes 4423688 | tf_op jit(solution)/shard_map/ppermute | solution.py:158
  48.3 13.8 %collective-permute-start.7 = (bf16[320,768]{1,0:T(8,128)(2,1)S(1)}, bf16[320,768]{1,0:T(8,128)(2,1)S(1)}, u32[]{:S(2)}, u32[]{:S(2)}) collective-permute-start(bf16[320,768]{1,0:T(8,128)(2,1)S(1)} %collective-permute-done.refs_1_.r1), channel_id=1, source_target_pairs={{1016,0},{1017,1},{1018,2},{1019,3},{12,4},{13,5},{14,6},{15,7},{0... | collective-permute-start | bytes 1474568 | tf_op jit(solution)/shard_map/ppermute | solution.py:158
  50.3 15.5 %collective-permute-start.6 = (bf16[576,768]{1,0:T(8,128)(2,1)S(1)}, bf16[576,768]{1,0:T(8,128)(2,1)S(1)}, u32[]{:S(2)}, u32[]{:S(2)}) collective-permute-start(bf16[576,768]{1,0:T(8,128)(2,1)S(1)} %shard_map.68), channel_id=1, source_target_pairs={{4,0},{5,1},{6,2},{7,3},{0,4},{1,5},{2,6},{3,7},{12,8},{13,9},{14,... | collective-permute-start | bytes 2654216 | tf_op jit(solution)/shard_map/ppermute | solution.py:158

commit v4 on v3

--- a/solution.py
+++ b/solution.py
@@ -64,7 +64,7 @@
     return pl.multiple_of(start, LANES), pl.multiple_of(group * width - start, 64)
 
 
-def primary_kernel(group, own, r1, r2, r3, w0, w1, w2, w3, u_out, z_out, back_out, cut_out, whole):
+def primary_kernel(group, w0, w1, w2, w3, own, r1, r2, r3, u_out, z_out, back_out, cut_out, whole):
     rows = own.shape[0]
     stack((w0, w1, w2, w3), whole)
     start, _ = window(group[0], w0.shape[0])
@@ -78,7 +78,7 @@
 
 
 def pack_kernel(*refs):
-    *blocks, out = refs
+    _, *blocks, out = refs
     stack(blocks, out)
 
 
@@ -101,7 +101,7 @@
 
 
 def main_kernel(
-    place, own, s123, w0, w123, u_p, z_p, back_p, cut_p, image_out, text_out, loss_out,
+    place, w0, w123, own, s123, u_p, z_p, back_p, cut_p, image_out, text_out, loss_out,
     whole, u_q, logits_ref, grads,
 ):
     group, swapped = place[0], place[1]
@@ -134,16 +134,31 @@
 PARAMS = pltpu.CompilerParams(vmem_limit_bytes=48 * 1024 * 1024)
 
 
-def pack(*blocks):
+def pack(*blocks, after):
     rows = sum(block.shape[0] for block in blocks)
     return pl.pallas_call(
         pack_kernel,
         out_shape=jax.ShapeDtypeStruct((rows, blocks[0].shape[1]), blocks[0].dtype),
-        in_specs=[VMEM] * len(blocks),
+        in_specs=[pl.BlockSpec(memory_space=pl.ANY)] + [VMEM] * len(blocks),
         out_specs=VMEM,
         compiler_params=PARAMS,
         cost_estimate=pl.CostEstimate(flops=PACK, bytes_accessed=4_000_000, transcendentals=0),
-    )(*blocks)
+    )(after, *blocks)
+
+
+def gate_kernel(x, out):
+    pass
+
+
+def gate(x, cost=PACK):
+    return pl.pallas_call(
+        gate_kernel,
+        out_shape=jax.ShapeDtypeStruct(x.shape, x.dtype),
+        in_specs=[pl.BlockSpec(memory_space=pl.ANY)],
+        out_specs=pl.BlockSpec(memory_space=pl.ANY),
+        input_output_aliases={0: 0},
+        cost_estimate=pl.CostEstimate(flops=cost, bytes_accessed=0, transcendentals=0),
+    )(x)
 
 
 def body(image_feats, text_feats, image_head, text_head):
@@ -160,20 +175,22 @@
     swap = grid.along_blk(1, -1)
     image_head, text_head = image_head.T, text_head.T
     width, features = image_head.shape[0], image_head.shape[0] * groups
+    head_p = jnp.where(even, image_head, text_head)
+    head_q = jnp.where(even, text_head, image_head)
     own_p = jnp.where(even, image_feats, text_feats)
     own_q = jnp.where(even, text_feats, image_feats)
-    head_p = jnp.where(even, image_head, text_head)
-    head_q = jnp.where(even, text_head, image_head)
     near = grid.along_z(-1, 1)
     w1 = permute(head_p, near)
     w2 = permute(head_p, grid.along_z(2, -2))
     r1 = permute(own_q, grid.along_blk(-1, 1))
     r2 = permute(own_p, grid.along_blk(-2, 2))
+    w2 = gate(w2)
     w3 = permute(w2, near)
+    r1 = gate(r1)
     r3 = permute(r1, grid.along_blk(-2, 2))
     taken = [w1, w2, w3]
-    s123 = permute(pack(own_p, r1, r2), swap)
-    w123 = permute(pack(*taken), swap)
+    s123 = permute(pack(own_p, r1, r2, after=w2), swap)
+    w123 = permute(pack(*taken, after=w1), swap)
 
     place = jnp.stack([group, odd]).astype(jnp.int32)
     cut = 2 * LANES
@@ -193,7 +210,7 @@
         cost_estimate=pl.CostEstimate(
             flops=80 * rows * depth * features, bytes_accessed=8_000_000, transcendentals=0
         ),
-    )(place, own_p, r1, r2, r3, head_p, *taken)
+    )(place, head_p, *taken, own_p, r1, r2, r3)
     image_grad, text_grad, loss = pl.pallas_call(
         main_kernel,
         out_shape=(
@@ -213,7 +230,7 @@
         cost_estimate=pl.CostEstimate(
             flops=24 * rows * depth * features, bytes_accessed=8_000_000, transcendentals=0
         ),
-    )(place, own_q, s123, head_q, w123, u_p, z_p, back_p, cut_p)
+    )(place, head_q, w123, own_q, s123, u_p, z_p, back_p, cut_p)
     return image_grad.T, text_grad.T, loss.reshape(rows // groups)
 
 

time: 75 us -> 66.7 us (0.89)
  starting transfers between devices: 48.8 us -> 35.5 us
  waiting for transfers between devices: 10.8 us -> 13.6 us
  local copies, waits for them, and re-layouts: 0.01 us -> 2.57 us
    ppermute x8, starting transfers between devices: 48.8 us -> 35.5 us  [permute(): return lax.ppermute(block, AXES, route)]
    ppermute x8, waiting for transfers between devices: 10.8 us -> 13.6 us  [permute(): return lax.ppermute(block, AXES, route)]
    unnamed x4 -> x14, local copies, waits for them, and re-layouts: 0.01 us -> 2.57 us
    select_n x1, other arithmetic: 1.3 us -> 0.07 us  [body(): own_p = jnp.where(even, image_feats, text_feats)]
    select_n x1, other arithmetic: 0.05 us -> 1.17 us  [body(): head_p = jnp.where(even, image_head, text_head)]
  transfers between devices with their start and end apart: 8 -> 8, of which waited for: 2 -> 2; matrix products, arithmetic and copies ran while one was open for 0% -> 0% of each run, Pallas kernels for 5% -> 6%
where the time goes in v4:
time: 66.7 us; the launch traced here: 66.3 us
  starting transfers between devices  35.5 us (53%)
  waiting for transfers between devices  13.6 us (20%)
  Pallas kernels  12.5 us (19%)
  local copies, waits for them, and re-layouts  2.57 us (4%)
  other arithmetic  1.32 us (2%)
  between operations  0.82 us (1%)
    ppermute x8, starting transfers between devices, permute(): return lax.ppermute(block, AXES, route)  35.5 us
    ppermute x8, waiting for transfers between devices, permute(): return lax.ppermute(block, AXES, route)  13.6 us
    pallas_call x1, Pallas kernels, body(): pl.pallas_call(main_kernel, out_shape=(jax.ShapeDtypeStruct((width, rows)...  8.63 us
    pallas_call x1, Pallas kernels, body(): pl.pallas_call(primary_kernel, out_shape=(jax.ShapeDtypeStruct((4 * rows,...  3.72 us
    unnamed x14, local copies, waits for them, and re-layouts  2.57 us
  transfers between devices with their start and end apart: 8, of which 2 were waited for; matrix products, arithmetic and copies ran while one was open for 0% of the time, Pallas kernels for 6%

profile of v4, /device:TPU:127, one launch (start us, length us, event | category | flops | bytes accessed | tf_op | source)
XLA Modules:
  0.0 66.3 jit_solution(447301858478740342)
XLA Ops:
  0.6 0.0 copy-start.5
  0.6 0.0 copy-start.6
  0.7 1.2 %select_bitcast_fusion = (bf16[192,768]{1,0:T(8,128)(2,1)S(1)}, bf16[192,768]{1,0:T(8,128)(2,1)S(1)}) fusion(bf16[768,192]{0,1:T(8,128)(2,1)} %param.6, bf16[768,192]{0,1:T(8,128)(2,1)} %param.7, pred[]{:T(512)S(6)} %eq.5), kind=kLoop, calls=%fused_computation.2 | loop fusion | flops 294912 | bytes 1179649 | tf_op jit(solution)/shard_map/jit(_where)/select_n | solution.py:178
  1.8 16.1 %collective-permute-start.1 = (bf16[192,768]{1,0:T(8,128)(2,1)S(1)}, bf16[192,768]{1,0:T(8,128)(2,1)S(1)}, u32[]{:S(2)}, u32[]{:S(2)}) collective-permute-start(bf16[192,768]{1,0:T(8,128)(2,1)S(1)} %get-tuple-element.19.w0), channel_id=1, source_target_pairs={{1,0},{2,1},{3,2},{0,3},{5,4},{6,5},{7,6},{4,7},{9,8},{10,9},{11,1... | collective-permute-start | bytes 884744 | tf_op jit(solution)/shard_map/ppermute | solution.py:173
  18.0 2.8 %collective-permute-start = (bf16[192,768]{1,0:T(8,128)(2,1)S(1)}, bf16[192,768]{1,0:T(8,128)(2,1)S(1)}, u32[]{:S(2)}, u32[]{:S(2)}) collective-permute-start(bf16[192,768]{1,0:T(8,128)(2,1)S(1)} %get-tuple-element.19.w0), channel_id=1, source_target_pairs={{515,0},{512,1},{513,2},{514,3},{519,4},{516,5},{517,6},{518,7},{5... | collective-permute-start | bytes 884744 | tf_op jit(solution)/shard_map/ppermute | solution.py:173
  20.8 0.0 copy-done.5
  20.8 0.0 copy-done.6
  20.8 0.1 broadcast_select_fusion
  20.9 1.9 %collective-permute-start.4 = (bf16[320,768]{1,0:T(8,128)(2,1)S(1)}, bf16[320,768]{1,0:T(8,128)(2,1)S(1)}, u32[]{:S(2)}, u32[]{:S(2)}) collective-permute-start(bf16[320,768]{1,0:T(8,128)(2,1)S(1)} %get-tuple-element.18.own), channel_id=1, source_target_pairs={{1020,0},{1021,1},{1022,2},{1023,3},{8,4},{9,5},{10,6},{11,7},{4,8... | collective-permute-start | bytes 1474568 | tf_op jit(solution)/shard_map/ppermute | solution.py:173
  22.8 4.2 %collective-permute-start.5 = (bf16[320,768]{1,0:T(8,128)(2,1)S(1)}, bf16[320,768]{1,0:T(8,128)(2,1)S(1)}, u32[]{:S(2)}, u32[]{:S(2)}) collective-permute-start(bf16[320,768]{1,0:T(8,128)(2,1)S(1)} %get-tuple-element.17.refs_1_.own), channel_id=1, source_target_pairs={{1016,0},{1017,1},{1018,2},{1019,3},{12,4},{13,5},{14,6},{15,7},{0... | collective-permute-start | bytes 1474568 | tf_op jit(solution)/shard_map/ppermute | solution.py:173
  27.1 0.1 pad_add_fusion.group.place
  27.1 0.0 collective-permute-done.1.x
  27.1 0.0 copy-start.3
  27.1 0.7 %copy-done.3 = bf16[192,768]{1,0:T(8,128)(2,1)} copy-done((bf16[192,768]{1,0:T(8,128)(2,1)}, bf16[192,768]{1,0:T(8,128)(2,1)S(1)}, u32[]{:S(2)}) %copy-start.3) | copy-done | bytes 294936
  27.8 0.0 copy-start.4
  27.8 4.1 %collective-permute-start.2 = (bf16[192,768]{1,0:T(8,128)(2,1)}, bf16[192,768]{1,0:T(8,128)(2,1)S(1)}, u32[]{:S(2)}, u32[]{:S(2)}) collective-permute-start(bf16[192,768]{1,0:T(8,128)(2,1)} %shard_map.67.refs_2_.refs_0_.w2), channel_id=1, source_target_pairs={{515,0},{512,1},{513,2},{514,3},{519,4},{516,5},{517,6},{518,7},{5... | collective-permute-start | bytes 884744 | tf_op jit(solution)/shard_map/ppermute | solution.py:173
  31.9 7.2 %collective-permute-done.4.x = bf16[320,768]{1,0:T(8,128)(2,1)S(1)} collective-permute-done((bf16[320,768]{1,0:T(8,128)(2,1)S(1)}, bf16[320,768]{1,0:T(8,128)(2,1)S(1)}, u32[]{:S(2)}, u32[]{:S(2)}) %collective-permute-start.4) | collective-permute-done | bytes 491552 | tf_op jit(solution)/shard_map/ppermute | solution.py:173
  39.1 0.0 copy-start
  39.1 0.8 %copy-done = bf16[320,768]{1,0:T(8,128)(2,1)} copy-done((bf16[320,768]{1,0:T(8,128)(2,1)}, bf16[320,768]{1,0:T(8,128)(2,1)S(1)}, u32[]{:S(2)}) %copy-start) | copy-done | bytes 491544
  39.9 1.9 %collective-permute-start.7 = (bf16[320,768]{1,0:T(8,128)(2,1)}, bf16[320,768]{1,0:T(8,128)(2,1)S(1)}, u32[]{:S(2)}, u32[]{:S(2)}) collective-permute-start(bf16[320,768]{1,0:T(8,128)(2,1)} %shard_map.69.refs_2_.r1), channel_id=1, source_target_pairs={{1016,0},{1017,1},{1018,2},{1019,3},{12,4},{13,5},{14,6},{15,7},{0... | collective-permute-start | bytes 1474568 | tf_op jit(solution)/shard_map/ppermute | solution.py:173
  41.8 0.0 collective-permute-done.5.refs_3_.r2
  41.9 0.0 copy-done.4
  41.9 0.0 copy-start.1
  41.9 1.0 %copy-done.1 = bf16[320,768]{1,0:T(8,128)(2,1)S(1)} copy-done((bf16[320,768]{1,0:T(8,128)(2,1)S(1)}, bf16[320,768]{1,0:T(8,128)(2,1)}, u32[]{:S(2)}) %copy-start.1) | copy-done | bytes 491544
  42.9 0.1 shard_map.70
  43.0 0.0 copy-start.2
  43.0 2.3 %collective-permute-start.6 = (bf16[960,768]{1,0:T(8,128)(2,1)S(1)}, bf16[960,768]{1,0:T(8,128)(2,1)S(1)}, u32[]{:S(2)}, u32[]{:S(2)}) collective-permute-start(bf16[960,768]{1,0:T(8,128)(2,1)S(1)} %shard_map.70), channel_id=1, source_target_pairs={{4,0},{5,1},{6,2},{7,3},{0,4},{1,5},{2,6},{3,7},{12,8},{13,9},{14,... | collective-permute-start | bytes 4423688 | tf_op jit(solution)/shard_map/ppermute | solution.py:173
  45.3 0.0 collective-permute-done.refs_0_.refs_1_.w1
  45.3 0.0 collective-permute-done.2.refs_3_.w3
  45.3 0.1 shard_map.68
  45.4 2.2 %collective-permute-start.3 = (bf16[576,768]{1,0:T(8,128)(2,1)S(1)}, bf16[576,768]{1,0:T(8,128)(2,1)S(1)}, u32[]{:S(2)}, u32[]{:S(2)}) collective-permute-start(bf16[576,768]{1,0:T(8,128)(2,1)S(1)} %shard_map.68), channel_id=1, source_target_pairs={{4,0},{5,1},{6,2},{7,3},{0,4},{1,5},{2,6},{3,7},{12,8},{13,9},{14,... | collective-permute-start | bytes 2654216 | tf_op jit(solution)/shard_map/ppermute | solution.py:173
  47.6 6.3 %collective-permute-done.7.r3 = bf16[320,768]{1,0:T(8,128)(2,1)S(1)} collective-permute-done((bf16[320,768]{1,0:T(8,128)(2,1)}, bf16[320,768]{1,0:T(8,128)(2,1)S(1)}, u32[]{:S(2)}, u32[]{:S(2)}) %collective-permute-start.7) | collective-permute-done | bytes 491552 | tf_op jit(solution)/shard_map/ppermute | solution.py:173
  53.9 0.0 copy-done.2
  53.9 3.7 %shard_map.71 = (bf16[1280,768]{1,0:T(8,128)(2,1)}, f32[320,768]{1,0:T(8,128)S(1)}, f32[320,1]{1,0:T(8,128)S(1)}, bf16[768,256]{1,0:T(8,128)(2,1)S(1)}) custom-call(s32[2]{0:T(128)S(1)} %pad_add_fusion.group.place, bf16[192,768]{1,0:T(8,128)(2,1)S(1)} %get-tuple-element.19.w0, bf16[192,768]{1,0:T(8,128)(2,1)S(1)} %collective-permute-done.refs_0_.refs_1_.w1, ...), custom_call_target="tpu_custom_call" | custom-call | flops 15099494400 | bytes 8000000 | tf_op jit(solution)/shard_map/pallas_call | solution.py:198
  57.6 0.0 collective-permute-done.3.w123
  57.6 0.0 collective-permute-done.6.s123
  57.7 8.6 %shard_map.72 = (bf16[192,320]{1,0:T(8,128)(2,1)}, bf16[192,320]{1,0:T(8,128)(2,1)}, f32[1,80]{1,0:T(1,128)}) custom-call(s32[2]{0:T(128)S(1)} %pad_add_fusion.group.place, bf16[192,768]{1,0:T(8,128)(2,1)S(1)} %get-tuple-element.20.w0, bf16[576,768]{1,0:T(8,128)(2,1)S(1)} %collective-permute-done.3.w123, bf16[320,768]{1,0:T(8,128)(2,1)S(1)} %get-tuple-element.18.own, ...), custom_call_target="tpu_custom_call" | custom-call | flops 4529848320 | bytes 8000000 | tf_op jit(solution)/shard_map/pallas_call | solution.py:214
  (2 shorter events, 0.0 us)
Async XLA Ops:
  0.6 20.2 %copy-start.5 = (bf16[320,768]{1,0:T(8,128)(2,1)S(1)}, bf16[320,768]{1,0:T(8,128)(2,1)}, u32[]{:S(2)}) copy-start(bf16[320,768]{1,0:T(8,128)(2,1)} %param.4) | copy-start | bytes 1474564
  0.6 20.2 %copy-start.6 = (bf16[320,768]{1,0:T(8,128)(2,1)S(1)}, bf16[320,768]{1,0:T(8,128)(2,1)}, u32[]{:S(2)}) copy-start(bf16[320,768]{1,0:T(8,128)(2,1)} %param.5) | copy-start | bytes 1474564
  1.8 25.3 %collective-permute-start.1 = (bf16[192,768]{1,0:T(8,128)(2,1)S(1)}, bf16[192,768]{1,0:T(8,128)(2,1)S(1)}, u32[]{:S(2)}, u32[]{:S(2)}) collective-permute-start(bf16[192,768]{1,0:T(8,128)(2,1)S(1)} %get-tuple-element.19.w0), channel_id=1, source_target_pairs={{1,0},{2,1},{3,2},{0,3},{5,4},{6,5},{7,6},{4,7},{9,8},{10,9},{11,1... | collective-permute-start | bytes 884744 | tf_op jit(solution)/shard_map/ppermute | solution.py:173
  18.0 27.3 %collective-permute-start = (bf16[192,768]{1,0:T(8,128)(2,1)S(1)}, bf16[192,768]{1,0:T(8,128)(2,1)S(1)}, u32[]{:S(2)}, u32[]{:S(2)}) collective-permute-start(bf16[192,768]{1,0:T(8,128)(2,1)S(1)} %get-tuple-element.19.w0), channel_id=1, source_target_pairs={{515,0},{512,1},{513,2},{514,3},{519,4},{516,5},{517,6},{518,7},{5... | collective-permute-start | bytes 884744 | tf_op jit(solution)/shard_map/ppermute | solution.py:173
  20.9 18.2 %collective-permute-start.4 = (bf16[320,768]{1,0:T(8,128)(2,1)S(1)}, bf16[320,768]{1,0:T(8,128)(2,1)S(1)}, u32[]{:S(2)}, u32[]{:S(2)}) collective-permute-start(bf16[320,768]{1,0:T(8,128)(2,1)S(1)} %get-tuple-element.18.own), channel_id=1, source_target_pairs={{1020,0},{1021,1},{1022,2},{1023,3},{8,4},{9,5},{10,6},{11,7},{4,8... | collective-permute-start | bytes 1474568 | tf_op jit(solution)/shard_map/ppermute | solution.py:173
  22.8 19.0 %collective-permute-start.5 = (bf16[320,768]{1,0:T(8,128)(2,1)S(1)}, bf16[320,768]{1,0:T(8,128)(2,1)S(1)}, u32[]{:S(2)}, u32[]{:S(2)}) collective-permute-start(bf16[320,768]{1,0:T(8,128)(2,1)S(1)} %get-tuple-element.17.refs_1_.own), channel_id=1, source_target_pairs={{1016,0},{1017,1},{1018,2},{1019,3},{12,4},{13,5},{14,6},{15,7},{0... | collective-permute-start | bytes 1474568 | tf_op jit(solution)/shard_map/ppermute | solution.py:173
  27.1 0.7 %copy-start.3 = (bf16[192,768]{1,0:T(8,128)(2,1)}, bf16[192,768]{1,0:T(8,128)(2,1)S(1)}, u32[]{:S(2)}) copy-start(bf16[192,768]{1,0:T(8,128)(2,1)S(1)} %collective-permute-done.1.x) | copy-start | bytes 884740
  27.8 14.0 %copy-start.4 = (bf16[192,768]{1,0:T(8,128)(2,1)S(1)}, bf16[192,768]{1,0:T(8,128)(2,1)}, u32[]{:S(2)}) copy-start(bf16[192,768]{1,0:T(8,128)(2,1)} %shard_map.67.refs_2_.refs_0_.w2) | copy-start | bytes 884740
  27.8 17.5 %collective-permute-start.2 = (bf16[192,768]{1,0:T(8,128)(2,1)}, bf16[192,768]{1,0:T(8,128)(2,1)S(1)}, u32[]{:S(2)}, u32[]{:S(2)}) collective-permute-start(bf16[192,768]{1,0:T(8,128)(2,1)} %shard_map.67.refs_2_.refs_0_.w2), channel_id=1, source_target_pairs={{515,0},{512,1},{513,2},{514,3},{519,4},{516,5},{517,6},{518,7},{5... | collective-permute-start | bytes 884744 | tf_op jit(solution)/shard_map/ppermute | solution.py:173
  39.1 0.8 %copy-start = (bf16[320,768]{1,0:T(8,128)(2,1)}, bf16[320,768]{1,0:T(8,128)(2,1)S(1)}, u32[]{:S(2)}) copy-start(bf16[320,768]{1,0:T(8,128)(2,1)S(1)} %collective-permute-done.4.x) | copy-start | bytes 1474564
  39.9 14.0 %collective-permute-start.7 = (bf16[320,768]{1,0:T(8,128)(2,1)}, bf16[320,768]{1,0:T(8,128)(2,1)S(1)}, u32[]{:S(2)}, u32[]{:S(2)}) collective-permute-start(bf16[320,768]{1,0:T(8,128)(2,1)} %shard_map.69.refs_2_.r1), channel_id=1, source_target_pairs={{1016,0},{1017,1},{1018,2},{1019,3},{12,4},{13,5},{14,6},{15,7},{0... | collective-permute-start | bytes 1474568 | tf_op jit(solution)/shard_map/ppermute | solution.py:173
  41.9 1.1 %copy-start.1 = (bf16[320,768]{1,0:T(8,128)(2,1)S(1)}, bf16[320,768]{1,0:T(8,128)(2,1)}, u32[]{:S(2)}) copy-start(bf16[320,768]{1,0:T(8,128)(2,1)} %shard_map.69.refs_2_.r1) | copy-start | bytes 1474564
  43.0 10.9 %copy-start.2 = (bf16[320,768]{1,0:T(8,128)(2,1)S(1)}, bf16[320,768]{1,0:T(8,128)(2,1)}, u32[]{:S(2)}) copy-start(bf16[320,768]{1,0:T(8,128)(2,1)} %shard_map.69.refs_2_.r1) | copy-start | bytes 1474564
  43.0 14.6 %collective-permute-start.6 = (bf16[960,768]{1,0:T(8,128)(2,1)S(1)}, bf16[960,768]{1,0:T(8,128)(2,1)S(1)}, u32[]{:S(2)}, u32[]{:S(2)}) collective-permute-start(bf16[960,768]{1,0:T(8,128)(2,1)S(1)} %shard_map.70), channel_id=1, source_target_pairs={{4,0},{5,1},{6,2},{7,3},{0,4},{1,5},{2,6},{3,7},{12,8},{13,9},{14,... | collective-permute-start | bytes 4423688 | tf_op jit(solution)/shard_map/ppermute | solution.py:173
  45.4 12.3 %collective-permute-start.3 = (bf16[576,768]{1,0:T(8,128)(2,1)S(1)}, bf16[576,768]{1,0:T(8,128)(2,1)S(1)}, u32[]{:S(2)}, u32[]{:S(2)}) collective-permute-start(bf16[576,768]{1,0:T(8,128)(2,1)S(1)} %shard_map.68), channel_id=1, source_target_pairs={{4,0},{5,1},{6,2},{7,3},{0,4},{1,5},{2,6},{3,7},{12,8},{13,9},{14,... | collective-permute-start | bytes 2654216 | tf_op jit(solution)/shard_map/ppermute | solution.py:173

commit v5 on v3

v5 whole, which is shorter than its diff:
```python
import jax
import jax.numpy as jnp
from jax import lax
from jax.experimental import pallas as pl
from jax.experimental.pallas import tpu as pltpu
from jax.sharding import PartitionSpec as P

LOGIT_SCALE = 10.0
LOGIT_BIAS = -2.0
EPSILON = 1e-06
PACK = 20_000_000_000
AXES = ("blk", "head")
LANES = 128


class Grid:
    def __init__(self, n_blk, n_head):
        self.n_blk, self.n_head = n_blk, n_head
        self.half = n_blk // 2
        self.depth = 2 * n_head

    def route(self, source):
        return [(source(d), d) for d in range(self.n_blk * self.n_head)]

    def along_blk(self, even, odd):
        def source(d):
            blk, head = divmod(d, self.n_head)
            step = odd if blk % 2 else even
            return (blk + step) % self.n_blk * self.n_head + head

        return self.route(source)

    def along_z(self, even, odd):
        def source(d):
            blk, head = divmod(d, self.n_head)
            z = 2 * head + blk // self.half
            z = (z + (odd if z % 2 else even)) % self.depth
            return (blk % self.half + self.half * (z % 2)) * self.n_head + z // 2

        return self.route(source)


def dot(left, right, left_dim=1, right_dim=0):
    return lax.dot_general(
        left, right, (((left_dim,), (right_dim,)), ((), ())), preferred_element_type=jnp.float32
    )


def project(feats, whole):
    z = dot(feats, whole[...], 1, 1)
    back = 1.0 / jnp.sqrt(jnp.sum(z * z, axis=1, keepdims=True) + EPSILON)
    return z, back, (z * back).astype(jnp.bfloat16)


def window(group, width):
    start = group * width // LANES * LANES
    return pl.multiple_of(start, LANES), pl.multiple_of(group * width - start, 64)


def pack_kernel(*refs):
    _, *blocks, out = refs
    at = 0
    for block in blocks:
        out[at : at + block.shape[0], :] = block[...]
        at += block.shape[0]


def gate_kernel(*refs):
    pass


def primary_kernel(whole, own_r1_r2, r3, u_out, z_out, back_out):
    rows = r3.shape[0]
    for k in range(4):
        block = r3[...] if k == 3 else own_r1_r2[k * rows : (k + 1) * rows, :]
        z, back, u = project(block, whole)
        u_out[k * rows : (k + 1) * rows, :] = u
        if k == 0:
            z_out[...] = z
            back_out[...] = back


def side(u_own, u_others, z, back, cut, logits_ref, at):
    rows = u_own.shape[0]
    logits = LOGIT_SCALE * dot(u_own, u_others[...], 1, 1) + LOGIT_BIAS
    logits_ref[at] = logits
    own = logits[:, :rows]
    turn = jnp.where(
        lax.broadcasted_iota(jnp.int32, own.shape, 0) == lax.broadcasted_iota(jnp.int32, own.shape, 1),
        -1.0,
        1.0,
    )
    w_own = (turn * LOGIT_SCALE / (1.0 + jnp.exp(-turn * own))).astype(jnp.bfloat16)
    w = (LOGIT_SCALE / (1.0 + jnp.exp(-logits[:, rows:]))).astype(jnp.bfloat16)
    g = dot(w_own, u_others[:rows, :]) + dot(w, u_others[rows:, :])
    inner = jnp.sum(g * z, axis=1, keepdims=True)
    dz = (g * back - z * (inner * back * back * back)).astype(jnp.bfloat16)
    return jnp.transpose(dot(dz, cut))


def main_kernel(
    place, whole_q, own, others, whole_p, u_p, z_p, back_p, image_out, text_out, loss_out,
    u_q, logits_ref, grads,
):
    group, swapped = place[0], place[1]
    rows, width = image_out.shape[1], image_out.shape[0]
    start, offset = window(group, width)
    columns = pl.ds(start, grads.shape[1])
    z_q, back_q, u = project(own[...], whole_q)
    u_q[:rows, :] = u
    for k in range(3):
        _, _, u = project(others[k * rows : (k + 1) * rows, :], whole_q)
        u_q[(k + 1) * rows : (k + 2) * rows, :] = u
    grads[0] = side(u_p[:rows, :], u_q, z_p[...], back_p[...], whole_p[:, columns], logits_ref, 0)
    grads[1] = side(u_q[:rows, :], u_p, z_q, back_q, whole_q[:, columns], logits_ref, 1)
    image_out[...] = grads[swapped, pl.ds(offset, width), :].astype(image_out.dtype)
    text_out[...] = grads[1 - swapped, pl.ds(offset, width), :].astype(text_out.dtype)
    quarter = loss_out.shape[1]
    first = pl.multiple_of(group * quarter, 8)
    x = logits_ref[swapped, pl.ds(first, quarter), :]
    on = first + lax.broadcasted_iota(jnp.int32, x.shape, 0) == lax.broadcasted_iota(
        jnp.int32, x.shape, 1
    )
    x = jnp.where(on, -x, x)
    loss = jnp.sum(jnp.maximum(x, 0.0) + jnp.log1p(jnp.exp(-jnp.abs(x))), axis=1, keepdims=True)
    loss_out[...] = jnp.transpose(jnp.broadcast_to(loss, (quarter, LANES)))[:1, :]


ANY = pl.BlockSpec(memory_space=pl.ANY)
VMEM = pl.BlockSpec(memory_space=pltpu.VMEM)
SMEM = pl.BlockSpec(memory_space=pltpu.SMEM)
PARAMS = pltpu.CompilerParams(vmem_limit_bytes=16 * 1024 * 1024)


def cost(flops):
    return pl.CostEstimate(flops=flops, bytes_accessed=1_000_000, transcendentals=0)


def gate(x, after=None):
    operands = (x,) if after is None else (x, after)
    return pl.pallas_call(
        gate_kernel,
        out_shape=jax.ShapeDtypeStruct(x.shape, x.dtype),
        in_specs=[ANY] * len(operands),
        out_specs=ANY,
        input_output_aliases={0: 0},
        cost_estimate=cost(PACK),
    )(*operands)


def pack(*blocks, after):
    rows = sum(block.shape[0] for block in blocks)
    return pl.pallas_call(
        pack_kernel,
        out_shape=jax.ShapeDtypeStruct((rows, blocks[0].shape[1]), blocks[0].dtype),
        in_specs=[ANY] + [VMEM] * len(blocks),
        out_specs=VMEM,
        compiler_params=PARAMS,
        cost_estimate=cost(PACK),
    )(after, *blocks)


def body(image_feats, text_feats, image_head, text_head):
    rows, depth = image_feats.shape
    groups = lax.axis_size("head")
    grid = Grid(lax.axis_size("blk"), groups)
    width = image_head.shape[1]
    features = width * groups
    place = jnp.stack([lax.axis_index("head"), lax.axis_index("blk") % 2]).astype(jnp.int32)

    def permute(block, route):
        return lax.ppermute(block, AXES, route)

    even = place[1] == 0
    image_head, text_head = image_head.T, text_head.T
    own_p = jnp.where(even, image_feats, text_feats)
    own_q = jnp.where(even, text_feats, image_feats)
    head_p = jnp.where(even, image_head, text_head)

    swap = grid.along_blk(1, -1)
    near = grid.along_z(-1, 1)
    two_on = grid.along_blk(-2, 2)
    r1 = permute(own_q, grid.along_blk(-1, 1))
    w2 = permute(head_p, grid.along_z(2, -2))
    w1 = permute(head_p, near)
    r2 = permute(own_p, two_on)
    r1 = gate(r1)
    r3 = permute(r1, two_on)
    w2 = gate(w2, after=r1)
    w3 = permute(w2, near)
    own_r1_r2 = pack(own_p, r1, r2, after=w2)
    others = permute(own_r1_r2, swap)
    whole_p = pack(head_p, w1, w2, w3, after=r1)
    whole_q = permute(whole_p, swap)

    u_p, z_p, back_p = pl.pallas_call(
        primary_kernel,
        out_shape=(
            jax.ShapeDtypeStruct((4 * rows, features), jnp.bfloat16),
            jax.ShapeDtypeStruct((rows, features), jnp.float32),
            jax.ShapeDtypeStruct((rows, 1), jnp.float32),
        ),
        in_specs=[VMEM] * 3,
        out_specs=(VMEM,) * 3,
        compiler_params=PARAMS,
        cost_estimate=cost(80 * rows * depth * features),
    )(whole_p, own_r1_r2, r3)
    image_grad, text_grad, loss = pl.pallas_call(
        main_kernel,
        out_shape=(
            jax.ShapeDtypeStruct((width, rows), jnp.bfloat16),
            jax.ShapeDtypeStruct((width, rows), jnp.bfloat16),
            jax.ShapeDtypeStruct((1, rows // groups), jnp.float32),
        ),
        in_specs=[SMEM] + [VMEM] * 7,
        out_specs=(VMEM,) * 3,
        scratch_shapes=[
            pltpu.VMEM((4 * rows, features), jnp.bfloat16),
            pltpu.VMEM((2, rows, 4 * rows), jnp.float32),
            pltpu.VMEM((2, 2 * LANES, rows), jnp.float32),
        ],
        compiler_params=PARAMS,
        cost_estimate=cost(24 * rows * depth * features),
    )(place, whole_q, own_q, others, whole_p, u_p, z_p, back_p)
    return image_grad.T, text_grad.T, loss.reshape(rows // groups)


def solution(mesh):
    in_specs = (P("blk", None), P("blk", None), P(None, "head"), P(None, "head"))
    out_specs = (P("blk", "head"), P("blk", "head"), P(("blk", "head")))
    return jax.shard_map(body, mesh=mesh, in_specs=in_specs, out_specs=out_specs, check_vma=False)
```

time: 75 us -> 64.7 us (0.86)
  the two profiles are of different devices: /device:TPU:127 before, /device:TPU:1 now
where the time goes in v5:
time: 64.7 us; the launch traced here: 64.3 us
  starting transfers between devices  47.8 us (74%)
  Pallas kernels  9.64 us (15%)
  local copies, waits for them, and re-layouts  2.48 us (4%)
  waiting for transfers between devices  2.19 us (3%)
  other arithmetic  1.41 us (2%)
  between operations  0.84 us (1%)
    ppermute x8, starting transfers between devices, permute(): return lax.ppermute(block, AXES, route)  47.8 us
    pallas_call x1, Pallas kernels, body(): pl.pallas_call(main_kernel, out_shape=(jax.ShapeDtypeStruct((width, rows)...  7.6 us
    unnamed x14, local copies, waits for them, and re-layouts  2.48 us
    ppermute x8, waiting for transfers between devices, permute(): return lax.ppermute(block, AXES, route)  2.19 us
    pallas_call x1, Pallas kernels, body(): pl.pallas_call(primary_kernel, out_shape=(jax.ShapeDtypeStruct((4 * rows,...  1.86 us
    select_n x1, other arithmetic, body(): own_p = jnp.where(even, image_feats, text_feats)  1.3 us
  transfers between devices with their start and end apart: 8, of which 2 were waited for; matrix products, arithmetic and copies ran while one was open for 0% of the time, Pallas kernels for 3%

profile of v5, /device:TPU:1, one launch (start us, length us, event | category | flops | bytes accessed | tf_op | source)
XLA Modules:
  0.0 64.3 jit_solution(15982026798485659714)
XLA Ops:
  0.6 0.0 copy-start.5
  0.6 0.0 copy-start.6
  0.7 1.3 %broadcast_select_fusion = (bf16[320,768]{1,0:T(8,128)(2,1)S(1)}, bf16[320,768]{1,0:T(8,128)(2,1)S(1)}) fusion(bf16[320,768]{1,0:T(8,128)(2,1)} %param.4, bf16[320,768]{1,0:T(8,128)(2,1)} %param.5, pred[]{:T(512)S(6)} %eq.5), kind=kLoop, calls=%fused_computation | loop fusion | flops 491520 | bytes 1966081 | tf_op jit(solution)/shard_map/jit(_where)/select_n | solution.py:176
  2.0 4.5 %collective-permute-start = (bf16[320,768]{1,0:T(8,128)(2,1)S(1)}, bf16[320,768]{1,0:T(8,128)(2,1)S(1)}, u32[]{:S(2)}, u32[]{:S(2)}) collective-permute-start(bf16[320,768]{1,0:T(8,128)(2,1)S(1)} %get-tuple-element.16.own), channel_id=1, source_target_pairs={{1020,0},{1021,1},{1022,2},{1023,3},{8,4},{9,5},{10,6},{11,7},{4,8... | collective-permute-start | bytes 1474568 | tf_op jit(solution)/shard_map/ppermute | solution.py:172
  6.5 0.0 copy-done.5
  6.5 0.0 copy-done.6
  6.6 16.2 %collective-permute-start.2 = (bf16[192,768]{1,0:T(8,128)(2,1)S(1)}, bf16[192,768]{1,0:T(8,128)(2,1)S(1)}, u32[]{:S(2)}, u32[]{:S(2)}) collective-permute-start(bf16[192,768]{1,0:T(8,128)(2,1)S(1)} %select_bitcast_fusion.refs_1_), channel_id=1, source_target_pairs={{1,0},{2,1},{3,2},{0,3},{5,4},{6,5},{7,6},{4,7},{9,8},{10,9},{11,1... | collective-permute-start | bytes 884744 | tf_op jit(solution)/shard_map/ppermute | solution.py:172
  22.7 2.8 %collective-permute-start.1 = (bf16[192,768]{1,0:T(8,128)(2,1)S(1)}, bf16[192,768]{1,0:T(8,128)(2,1)S(1)}, u32[]{:S(2)}, u32[]{:S(2)}) collective-permute-start(bf16[192,768]{1,0:T(8,128)(2,1)S(1)} %select_bitcast_fusion.refs_1_), channel_id=1, source_target_pairs={{515,0},{512,1},{513,2},{514,3},{519,4},{516,5},{517,6},{518,7},{5... | collective-permute-start | bytes 884744 | tf_op jit(solution)/shard_map/ppermute | solution.py:172
  25.6 3.8 %collective-permute-start.5 = (bf16[320,768]{1,0:T(8,128)(2,1)S(1)}, bf16[320,768]{1,0:T(8,128)(2,1)S(1)}, u32[]{:S(2)}, u32[]{:S(2)}) collective-permute-start(bf16[320,768]{1,0:T(8,128)(2,1)S(1)} %get-tuple-element.15.refs_1_), channel_id=1, source_target_pairs={{1016,0},{1017,1},{1018,2},{1019,3},{12,4},{13,5},{14,6},{15,7},{0... | collective-permute-start | bytes 1474568 | tf_op jit(solution)/shard_map/ppermute | solution.py:172
  29.5 0.1 pad_add_fusion.place
  29.5 0.0 collective-permute-done.refs_0_
  29.5 0.0 copy-start
  29.5 0.8 %copy-done = bf16[320,768]{1,0:T(8,128)(2,1)} copy-done((bf16[320,768]{1,0:T(8,128)(2,1)}, bf16[320,768]{1,0:T(8,128)(2,1)S(1)}, u32[]{:S(2)}) %copy-start) | copy-done | bytes 491544
  30.3 0.0 copy-start.1
  30.3 2.6 %collective-permute-start.7 = (bf16[320,768]{1,0:T(8,128)(2,1)}, bf16[320,768]{1,0:T(8,128)(2,1)S(1)}, u32[]{:S(2)}, u32[]{:S(2)}) collective-permute-start(bf16[320,768]{1,0:T(8,128)(2,1)} %shard_map.67.refs_1_.refs_0_.refs_2_), channel_id=1, source_target_pairs={{1016,0},{1017,1},{1018,2},{1019,3},{12,4},{13,5},{14,6},{15,7},{0... | collective-permute-start | bytes 1474568 | tf_op jit(solution)/shard_map/ppermute | solution.py:172
  32.9 0.0 collective-permute-done.2.refs_0_
  33.0 0.0 copy-start.2
  33.0 0.7 %copy-done.2 = bf16[192,768]{1,0:T(8,128)(2,1)} copy-done((bf16[192,768]{1,0:T(8,128)(2,1)}, bf16[192,768]{1,0:T(8,128)(2,1)S(1)}, u32[]{:S(2)}) %copy-start.2) | copy-done | bytes 294936
  33.7 13.9 %collective-permute-start.3 = (bf16[192,768]{1,0:T(8,128)(2,1)}, bf16[192,768]{1,0:T(8,128)(2,1)S(1)}, u32[]{:S(2)}, u32[]{:S(2)}) collective-permute-start(bf16[192,768]{1,0:T(8,128)(2,1)} %shard_map.68.refs_3_.refs_0_), channel_id=1, source_target_pairs={{515,0},{512,1},{513,2},{514,3},{519,4},{516,5},{517,6},{518,7},{5... | collective-permute-start | bytes 884744 | tf_op jit(solution)/shard_map/ppermute | solution.py:172
  47.6 0.0 collective-permute-done.5.refs_3_
  47.6 0.0 copy-done.1
  47.6 0.0 copy-start.3
  47.6 1.0 %copy-done.3 = bf16[192,768]{1,0:T(8,128)(2,1)S(1)} copy-done((bf16[192,768]{1,0:T(8,128)(2,1)S(1)}, bf16[192,768]{1,0:T(8,128)(2,1)}, u32[]{:S(2)}) %copy-start.3) | copy-done | bytes 294936
  48.6 0.0 copy-start.4
  48.6 0.1 shard_map.70.own_r1_r2
  48.7 1.9 %collective-permute-start.6 = (bf16[960,768]{1,0:T(8,128)(2,1)S(1)}, bf16[960,768]{1,0:T(8,128)(2,1)S(1)}, u32[]{:S(2)}, u32[]{:S(2)}) collective-permute-start(bf16[960,768]{1,0:T(8,128)(2,1)S(1)} %shard_map.70.own_r1_r2), channel_id=1, source_target_pairs={{4,0},{5,1},{6,2},{7,3},{0,4},{1,5},{2,6},{3,7},{12,8},{13,9},{14,... | collective-permute-start | bytes 4423688 | tf_op jit(solution)/shard_map/ppermute | solution.py:172
  50.6 0.0 collective-permute-done.1.refs_2_
  50.6 1.3 %collective-permute-done.3.refs_4_ = bf16[192,768]{1,0:T(8,128)(2,1)S(1)} collective-permute-done((bf16[192,768]{1,0:T(8,128)(2,1)}, bf16[192,768]{1,0:T(8,128)(2,1)S(1)}, u32[]{:S(2)}, u32[]{:S(2)}) %collective-permute-start.3) | collective-permute-done | bytes 294944 | tf_op jit(solution)/shard_map/ppermute | solution.py:172
  51.9 0.0 copy-done.4
  51.9 0.1 shard_map.69.whole.whole_p
  52.0 1.9 %collective-permute-start.4 = (bf16[768,768]{1,0:T(8,128)(2,1)S(1)}, bf16[768,768]{1,0:T(8,128)(2,1)S(1)}, u32[]{:S(2)}, u32[]{:S(2)}) collective-permute-start(bf16[768,768]{1,0:T(8,128)(2,1)S(1)} %shard_map.69.whole.whole_p), channel_id=1, source_target_pairs={{4,0},{5,1},{6,2},{7,3},{0,4},{1,5},{2,6},{3,7},{12,8},{13,9},{14,... | collective-permute-start | bytes 3538952 | tf_op jit(solution)/shard_map/ppermute | solution.py:172
  53.9 0.0 collective-permute-done.7.r3
  53.9 1.9 %shard_map.71 = (bf16[1280,768]{1,0:T(8,128)(2,1)S(1)}, f32[320,768]{1,0:T(8,128)S(1)}, f32[320,1]{1,0:T(8,128)S(1)}) custom-call(bf16[768,768]{1,0:T(8,128)(2,1)S(1)} %shard_map.69.whole.whole_p, bf16[960,768]{1,0:T(8,128)(2,1)S(1)} %shard_map.70.own_r1_r2, bf16[320,768]{1,0:T(8,128)(2,1)S(1)} %collective-permute-done.7.r3), custom_call_target="tpu_custom_call" | custom-call | flops 15099494400 | bytes 1000000 | tf_op jit(solution)/shard_map/pallas_call | solution.py:196
  55.8 0.0 collective-permute-done.6.others
  55.8 0.9 %collective-permute-done.4.whole_q = bf16[768,768]{1,0:T(8,128)(2,1)S(1)} collective-permute-done((bf16[768,768]{1,0:T(8,128)(2,1)S(1)}, bf16[768,768]{1,0:T(8,128)(2,1)S(1)}, u32[]{:S(2)}, u32[]{:S(2)}) %collective-permute-start.4) | collective-permute-done | bytes 1179680 | tf_op jit(solution)/shard_map/ppermute | solution.py:172
  56.7 7.6 %shard_map.72 = (bf16[192,320]{1,0:T(8,128)(2,1)}, bf16[192,320]{1,0:T(8,128)(2,1)}, f32[1,80]{1,0:T(1,128)}) custom-call(s32[2]{0:T(128)S(1)} %pad_add_fusion.place, bf16[768,768]{1,0:T(8,128)(2,1)S(1)} %collective-permute-done.4.whole_q, bf16[320,768]{1,0:T(8,128)(2,1)S(1)} %get-tuple-element.16.own, bf16[960,768]{1,0:T(8,128)(2,1)S(1)} %collective-permute-done.6.others, ...), custom_call_target="tpu_custom_call" | custom-call | flops 4529848320 | bytes 1000000 | tf_op jit(solution)/shard_map/pallas_call | solution.py:208
  (3 shorter events, 0.0 us)
Async XLA Ops:
  0.6 5.9 %copy-start.5 = (bf16[768,192]{0,1:T(8,128)(2,1)S(1)}, bf16[768,192]{0,1:T(8,128)(2,1)}, u32[]{:S(2)}) copy-start(bf16[768,192]{0,1:T(8,128)(2,1)} %param.6) | copy-start | bytes 884740
  0.6 5.9 %copy-start.6 = (bf16[768,192]{0,1:T(8,128)(2,1)S(1)}, bf16[768,192]{0,1:T(8,128)(2,1)}, u32[]{:S(2)}) copy-start(bf16[768,192]{0,1:T(8,128)(2,1)} %param.7) | copy-start | bytes 884740
  2.0 27.6 %collective-permute-start = (bf16[320,768]{1,0:T(8,128)(2,1)S(1)}, bf16[320,768]{1,0:T(8,128)(2,1)S(1)}, u32[]{:S(2)}, u32[]{:S(2)}) collective-permute-start(bf16[320,768]{1,0:T(8,128)(2,1)S(1)} %get-tuple-element.16.own), channel_id=1, source_target_pairs={{1020,0},{1021,1},{1022,2},{1023,3},{8,4},{9,5},{10,6},{11,7},{4,8... | collective-permute-start | bytes 1474568 | tf_op jit(solution)/shard_map/ppermute | solution.py:172
  6.6 26.4 %collective-permute-start.2 = (bf16[192,768]{1,0:T(8,128)(2,1)S(1)}, bf16[192,768]{1,0:T(8,128)(2,1)S(1)}, u32[]{:S(2)}, u32[]{:S(2)}) collective-permute-start(bf16[192,768]{1,0:T(8,128)(2,1)S(1)} %select_bitcast_fusion.refs_1_), channel_id=1, source_target_pairs={{1,0},{2,1},{3,2},{0,3},{5,4},{6,5},{7,6},{4,7},{9,8},{10,9},{11,1... | collective-permute-start | bytes 884744 | tf_op jit(solution)/shard_map/ppermute | solution.py:172
  22.7 27.9 %collective-permute-start.1 = (bf16[192,768]{1,0:T(8,128)(2,1)S(1)}, bf16[192,768]{1,0:T(8,128)(2,1)S(1)}, u32[]{:S(2)}, u32[]{:S(2)}) collective-permute-start(bf16[192,768]{1,0:T(8,128)(2,1)S(1)} %select_bitcast_fusion.refs_1_), channel_id=1, source_target_pairs={{515,0},{512,1},{513,2},{514,3},{519,4},{516,5},{517,6},{518,7},{5... | collective-permute-start | bytes 884744 | tf_op jit(solution)/shard_map/ppermute | solution.py:172
  25.6 22.0 %collective-permute-start.5 = (bf16[320,768]{1,0:T(8,128)(2,1)S(1)}, bf16[320,768]{1,0:T(8,128)(2,1)S(1)}, u32[]{:S(2)}, u32[]{:S(2)}) collective-permute-start(bf16[320,768]{1,0:T(8,128)(2,1)S(1)} %get-tuple-element.15.refs_1_), channel_id=1, source_target_pairs={{1016,0},{1017,1},{1018,2},{1019,3},{12,4},{13,5},{14,6},{15,7},{0... | collective-permute-start | bytes 1474568 | tf_op jit(solution)/shard_map/ppermute | solution.py:172
  29.5 0.8 %copy-start = (bf16[320,768]{1,0:T(8,128)(2,1)}, bf16[320,768]{1,0:T(8,128)(2,1)S(1)}, u32[]{:S(2)}) copy-start(bf16[320,768]{1,0:T(8,128)(2,1)S(1)} %collective-permute-done.refs_0_) | copy-start | bytes 1474564
  30.3 17.3 %copy-start.1 = (bf16[320,768]{1,0:T(8,128)(2,1)S(1)}, bf16[320,768]{1,0:T(8,128)(2,1)}, u32[]{:S(2)}) copy-start(bf16[320,768]{1,0:T(8,128)(2,1)} %shard_map.67.refs_1_.refs_0_.refs_2_) | copy-start | bytes 1474564
  30.3 23.6 %collective-permute-start.7 = (bf16[320,768]{1,0:T(8,128)(2,1)}, bf16[320,768]{1,0:T(8,128)(2,1)S(1)}, u32[]{:S(2)}, u32[]{:S(2)}) collective-permute-start(bf16[320,768]{1,0:T(8,128)(2,1)} %shard_map.67.refs_1_.refs_0_.refs_2_), channel_id=1, source_target_pairs={{1016,0},{1017,1},{1018,2},{1019,3},{12,4},{13,5},{14,6},{15,7},{0... | collective-permute-start | bytes 1474568 | tf_op jit(solution)/shard_map/ppermute | solution.py:172
  33.0 0.7 %copy-start.2 = (bf16[192,768]{1,0:T(8,128)(2,1)}, bf16[192,768]{1,0:T(8,128)(2,1)S(1)}, u32[]{:S(2)}) copy-start(bf16[192,768]{1,0:T(8,128)(2,1)S(1)} %collective-permute-done.2.refs_0_) | copy-start | bytes 884740
  33.7 18.2 %collective-permute-start.3 = (bf16[192,768]{1,0:T(8,128)(2,1)}, bf16[192,768]{1,0:T(8,128)(2,1)S(1)}, u32[]{:S(2)}, u32[]{:S(2)}) collective-permute-start(bf16[192,768]{1,0:T(8,128)(2,1)} %shard_map.68.refs_3_.refs_0_), channel_id=1, source_target_pairs={{515,0},{512,1},{513,2},{514,3},{519,4},{516,5},{517,6},{518,7},{5... | collective-permute-start | bytes 884744 | tf_op jit(solution)/shard_map/ppermute | solution.py:172
  47.6 1.0 %copy-start.3 = (bf16[192,768]{1,0:T(8,128)(2,1)S(1)}, bf16[192,768]{1,0:T(8,128)(2,1)}, u32[]{:S(2)}) copy-start(bf16[192,768]{1,0:T(8,128)(2,1)} %shard_map.68.refs_3_.refs_0_) | copy-start | bytes 884740
  48.6 3.3 %copy-start.4 = (bf16[192,768]{1,0:T(8,128)(2,1)S(1)}, bf16[192,768]{1,0:T(8,128)(2,1)}, u32[]{:S(2)}) copy-start(bf16[192,768]{1,0:T(8,128)(2,1)} %shard_map.68.refs_3_.refs_0_) | copy-start | bytes 884740
  48.7 7.1 %collective-permute-start.6 = (bf16[960,768]{1,0:T(8,128)(2,1)S(1)}, bf16[960,768]{1,0:T(8,128)(2,1)S(1)}, u32[]{:S(2)}, u32[]{:S(2)}) collective-permute-start(bf16[960,768]{1,0:T(8,128)(2,1)S(1)} %shard_map.70.own_r1_r2), channel_id=1, source_target_pairs={{4,0},{5,1},{6,2},{7,3},{0,4},{1,5},{2,6},{3,7},{12,8},{13,9},{14,... | collective-permute-start | bytes 4423688 | tf_op jit(solution)/shard_map/ppermute | solution.py:172
  52.0 4.7 %collective-permute-start.4 = (bf16[768,768]{1,0:T(8,128)(2,1)S(1)}, bf16[768,768]{1,0:T(8,128)(2,1)S(1)}, u32[]{:S(2)}, u32[]{:S(2)}) collective-permute-start(bf16[768,768]{1,0:T(8,128)(2,1)S(1)} %shard_map.69.whole.whole_p), channel_id=1, source_target_pairs={{4,0},{5,1},{6,2},{7,3},{0,4},{1,5},{2,6},{3,7},{12,8},{13,9},{14,... | collective-permute-start | bytes 3538952 | tf_op jit(solution)/shard_map/ppermute | solution.py:172

commit v6 on v5

--- a/solution.py
+++ b/solution.py
@@ -1,3 +1,5 @@
+import functools
+
 import jax
 import jax.numpy as jnp
 from jax import lax
@@ -57,16 +59,12 @@
     return pl.multiple_of(start, LANES), pl.multiple_of(group * width - start, 64)
 
 
-def pack_kernel(*refs):
-    _, *blocks, out = refs
+def pack_kernel(skipped, *refs):
+    *blocks, out = refs[skipped:]
     at = 0
     for block in blocks:
         out[at : at + block.shape[0], :] = block[...]
         at += block.shape[0]
-
-
-def gate_kernel(*refs):
-    pass
 
 
 def primary_kernel(whole, own_r1_r2, r3, u_out, z_out, back_out):
@@ -136,28 +134,16 @@
     return pl.CostEstimate(flops=flops, bytes_accessed=1_000_000, transcendentals=0)
 
 
-def gate(x, after=None):
-    operands = (x,) if after is None else (x, after)
-    return pl.pallas_call(
-        gate_kernel,
-        out_shape=jax.ShapeDtypeStruct(x.shape, x.dtype),
-        in_specs=[ANY] * len(operands),
-        out_specs=ANY,
-        input_output_aliases={0: 0},
-        cost_estimate=cost(PACK),
-    )(*operands)
-
-
-def pack(*blocks, after):
+def pack(*blocks, after=()):
     rows = sum(block.shape[0] for block in blocks)
     return pl.pallas_call(
-        pack_kernel,
+        functools.partial(pack_kernel, len(after)),
         out_shape=jax.ShapeDtypeStruct((rows, blocks[0].shape[1]), blocks[0].dtype),
-        in_specs=[ANY] + [VMEM] * len(blocks),
+        in_specs=[ANY] * len(after) + [VMEM] * len(blocks),
         out_specs=VMEM,
         compiler_params=PARAMS,
         cost_estimate=cost(PACK),
-    )(after, *blocks)
+    )(*after, *blocks)
 
 
 def body(image_feats, text_feats, image_head, text_head):
@@ -180,17 +166,17 @@
     swap = grid.along_blk(1, -1)
     near = grid.along_z(-1, 1)
     two_on = grid.along_blk(-2, 2)
-    r1 = permute(own_q, grid.along_blk(-1, 1))
     w2 = permute(head_p, grid.along_z(2, -2))
     w1 = permute(head_p, near)
+    r1 = permute(own_q, grid.along_blk(-1, 1))
     r2 = permute(own_p, two_on)
-    r1 = gate(r1)
+    w2 = pack(w2)
+    w3 = permute(w2, near)
+    r1 = pack(r1, after=(w2,))
     r3 = permute(r1, two_on)
-    w2 = gate(w2, after=r1)
-    w3 = permute(w2, near)
-    own_r1_r2 = pack(own_p, r1, r2, after=w2)
+    own_r1_r2 = pack(own_p, r1, r2)
     others = permute(own_r1_r2, swap)
-    whole_p = pack(head_p, w1, w2, w3, after=r1)
+    whole_p = pack(head_p, w1, w2, w3)
     whole_q = permute(whole_p, swap)
 
     u_p, z_p, back_p = pl.pallas_call(

time: 64.7 us -> 64 us (0.989)
  the two profiles are of different devices: /device:TPU:1 before, /device:TPU:127 now
where the time goes in v6:
time: 64 us; the launch traced here: 63.6 us
  starting transfers between devices  35.3 us (55%)
  waiting for transfers between devices  15.4 us (24%)
  Pallas kernels  9.83 us (15%)
  other arithmetic  2.33 us (4%)
  between operations  0.79 us (1%)
    ppermute x8, starting transfers between devices, permute(): return lax.ppermute(block, AXES, route)  35.3 us
    ppermute x8, waiting for transfers between devices, permute(): return lax.ppermute(block, AXES, route)  15.4 us
    pallas_call x1, Pallas kernels, body(): pl.pallas_call(main_kernel, out_shape=(jax.ShapeDtypeStruct((width, rows)...  7.72 us
    pallas_call x1, Pallas kernels, body(): pl.pallas_call(primary_kernel, out_shape=(jax.ShapeDtypeStruct((4 * rows,...  1.88 us
  transfers between devices with their start and end apart: 8, of which 2 were waited for; matrix products, arithmetic and copies ran while one was open for 2% of the time, Pallas kernels for 3%

profile of v6, /device:TPU:127, one launch (start us, length us, event | category | flops | bytes accessed | tf_op | source)
XLA Modules:
  0.0 63.6 jit_solution(17045112805551984984)
XLA Ops:
  0.6 1.0 %select_bitcast_fusion.refs_0_ = bf16[192,768]{1,0:T(8,128)(2,1)S(1)} fusion(bf16[768,192]{0,1:T(8,128)(2,1)} %param.6, bf16[768,192]{0,1:T(8,128)(2,1)} %param.7, pred[]{:T(512)S(6)} %eq.5), kind=kLoop, calls=%fused_computation.2 | loop fusion | flops 147456 | bytes 884737 | tf_op jit(solution)/shard_map/jit(_where)/select_n | solution.py:164
  1.7 16.1 %collective-permute-start.1 = (bf16[192,768]{1,0:T(8,128)(2,1)S(1)}, bf16[192,768]{1,0:T(8,128)(2,1)S(1)}, u32[]{:S(2)}, u32[]{:S(2)}) collective-permute-start(bf16[192,768]{1,0:T(8,128)(2,1)S(1)} %select_bitcast_fusion.refs_0_), channel_id=1, source_target_pairs={{1,0},{2,1},{3,2},{0,3},{5,4},{6,5},{7,6},{4,7},{9,8},{10,9},{11,1... | collective-permute-start | bytes 884744 | tf_op jit(solution)/shard_map/ppermute | solution.py:158
  17.8 2.8 %collective-permute-start = (bf16[192,768]{1,0:T(8,128)(2,1)S(1)}, bf16[192,768]{1,0:T(8,128)(2,1)S(1)}, u32[]{:S(2)}, u32[]{:S(2)}) collective-permute-start(bf16[192,768]{1,0:T(8,128)(2,1)S(1)} %select_bitcast_fusion.refs_0_), channel_id=1, source_target_pairs={{515,0},{512,1},{513,2},{514,3},{519,4},{516,5},{517,6},{518,7},{5... | collective-permute-start | bytes 884744 | tf_op jit(solution)/shard_map/ppermute | solution.py:158
  20.6 1.2 %broadcast_select_fusion = (bf16[320,768]{1,0:T(8,128)(2,1)S(1)}, bf16[320,768]{1,0:T(8,128)(2,1)S(1)}) fusion(bf16[320,768]{1,0:T(8,128)(2,1)} %param.4, bf16[320,768]{1,0:T(8,128)(2,1)} %param.5, pred[]{:T(512)S(6)} %eq.5), kind=kLoop, calls=%fused_computation | loop fusion | flops 491520 | bytes 1966081 | tf_op jit(solution)/shard_map/jit(_where)/select_n | solution.py:162
  21.9 1.9 %collective-permute-start.4 = (bf16[320,768]{1,0:T(8,128)(2,1)S(1)}, bf16[320,768]{1,0:T(8,128)(2,1)S(1)}, u32[]{:S(2)}, u32[]{:S(2)}) collective-permute-start(bf16[320,768]{1,0:T(8,128)(2,1)S(1)} %get-tuple-element.16.own), channel_id=1, source_target_pairs={{1020,0},{1021,1},{1022,2},{1023,3},{8,4},{9,5},{10,6},{11,7},{4,8... | collective-permute-start | bytes 1474568 | tf_op jit(solution)/shard_map/ppermute | solution.py:158
  23.8 4.2 %collective-permute-start.5 = (bf16[320,768]{1,0:T(8,128)(2,1)S(1)}, bf16[320,768]{1,0:T(8,128)(2,1)S(1)}, u32[]{:S(2)}, u32[]{:S(2)}) collective-permute-start(bf16[320,768]{1,0:T(8,128)(2,1)S(1)} %get-tuple-element.15.refs_0_), channel_id=1, source_target_pairs={{1016,0},{1017,1},{1018,2},{1019,3},{12,4},{13,5},{14,6},{15,7},{0... | collective-permute-start | bytes 1474568 | tf_op jit(solution)/shard_map/ppermute | solution.py:158
  28.0 0.1 pad_add_fusion.place
  28.1 0.0 collective-permute-done.1.refs_0_
  28.1 3.9 %collective-permute-start.2 = (bf16[192,768]{1,0:T(8,128)(2,1)S(1)}, bf16[192,768]{1,0:T(8,128)(2,1)S(1)}, u32[]{:S(2)}, u32[]{:S(2)}) collective-permute-start(bf16[192,768]{1,0:T(8,128)(2,1)S(1)} %shard_map.67.refs_2_.refs_0_), channel_id=1, source_target_pairs={{515,0},{512,1},{513,2},{514,3},{519,4},{516,5},{517,6},{518,7},{5... | collective-permute-start | bytes 884744 | tf_op jit(solution)/shard_map/ppermute | solution.py:158
  32.1 8.0 %collective-permute-done.4.refs_1_ = bf16[320,768]{1,0:T(8,128)(2,1)S(1)} collective-permute-done((bf16[320,768]{1,0:T(8,128)(2,1)S(1)}, bf16[320,768]{1,0:T(8,128)(2,1)S(1)}, u32[]{:S(2)}, u32[]{:S(2)}) %collective-permute-start.4) | collective-permute-done | bytes 491552 | tf_op jit(solution)/shard_map/ppermute | solution.py:158
  40.1 1.9 %collective-permute-start.7 = (bf16[320,768]{1,0:T(8,128)(2,1)S(1)}, bf16[320,768]{1,0:T(8,128)(2,1)S(1)}, u32[]{:S(2)}, u32[]{:S(2)}) collective-permute-start(bf16[320,768]{1,0:T(8,128)(2,1)S(1)} %shard_map.69.refs_1_), channel_id=1, source_target_pairs={{1016,0},{1017,1},{1018,2},{1019,3},{12,4},{13,5},{14,6},{15,7},{0... | collective-permute-start | bytes 1474568 | tf_op jit(solution)/shard_map/ppermute | solution.py:158
  42.1 0.0 collective-permute-done.5.refs_2_
  42.1 0.1 shard_map.70.own_r1_r2
  42.2 2.1 %collective-permute-start.6 = (bf16[960,768]{1,0:T(8,128)(2,1)S(1)}, bf16[960,768]{1,0:T(8,128)(2,1)S(1)}, u32[]{:S(2)}, u32[]{:S(2)}) collective-permute-start(bf16[960,768]{1,0:T(8,128)(2,1)S(1)} %shard_map.70.own_r1_r2), channel_id=1, source_target_pairs={{4,0},{5,1},{6,2},{7,3},{0,4},{1,5},{2,6},{3,7},{12,8},{13,9},{14,... | collective-permute-start | bytes 4423688 | tf_op jit(solution)/shard_map/ppermute | solution.py:158
  44.3 0.0 collective-permute-done.refs_1_
  44.3 0.0 collective-permute-done.2.refs_3_
  44.3 0.1 shard_map.68.whole.whole_p
  44.4 2.2 %collective-permute-start.3 = (bf16[768,768]{1,0:T(8,128)(2,1)S(1)}, bf16[768,768]{1,0:T(8,128)(2,1)S(1)}, u32[]{:S(2)}, u32[]{:S(2)}) collective-permute-start(bf16[768,768]{1,0:T(8,128)(2,1)S(1)} %shard_map.68.whole.whole_p), channel_id=1, source_target_pairs={{4,0},{5,1},{6,2},{7,3},{0,4},{1,5},{2,6},{3,7},{12,8},{13,9},{14,... | collective-permute-start | bytes 3538952 | tf_op jit(solution)/shard_map/ppermute | solution.py:158
  46.6 7.3 %collective-permute-done.7.r3 = bf16[320,768]{1,0:T(8,128)(2,1)S(1)} collective-permute-done((bf16[320,768]{1,0:T(8,128)(2,1)S(1)}, bf16[320,768]{1,0:T(8,128)(2,1)S(1)}, u32[]{:S(2)}, u32[]{:S(2)}) %collective-permute-start.7) | collective-permute-done | bytes 491552 | tf_op jit(solution)/shard_map/ppermute | solution.py:158
  53.9 1.9 %shard_map.71 = (bf16[1280,768]{1,0:T(8,128)(2,1)S(1)}, f32[320,768]{1,0:T(8,128)S(1)}, f32[320,1]{1,0:T(8,128)S(1)}) custom-call(bf16[768,768]{1,0:T(8,128)(2,1)S(1)} %shard_map.68.whole.whole_p, bf16[960,768]{1,0:T(8,128)(2,1)S(1)} %shard_map.70.own_r1_r2, bf16[320,768]{1,0:T(8,128)(2,1)S(1)} %collective-permute-done.7.r3), custom_call_target="tpu_custom_call" | custom-call | flops 15099494400 | bytes 1000000 | tf_op jit(solution)/shard_map/pallas_call | solution.py:182
  55.8 0.0 collective-permute-done.3.whole_q
  55.8 0.0 collective-permute-done.6.others
  55.8 7.7 %shard_map.72 = (bf16[192,320]{1,0:T(8,128)(2,1)}, bf16[192,320]{1,0:T(8,128)(2,1)}, f32[1,80]{1,0:T(1,128)}) custom-call(s32[2]{0:T(128)S(1)} %pad_add_fusion.place, bf16[768,768]{1,0:T(8,128)(2,1)S(1)} %collective-permute-done.3.whole_q, bf16[320,768]{1,0:T(8,128)(2,1)S(1)} %get-tuple-element.16.own, bf16[960,768]{1,0:T(8,128)(2,1)S(1)} %collective-permute-done.6.others, ...), custom_call_target="tpu_custom_call" | custom-call | flops 4529848320 | bytes 1000000 | tf_op jit(solution)/shard_map/pallas_call | solution.py:194
  (2 shorter events, 0.1 us)
Async XLA Ops:
  1.7 26.4 %collective-permute-start.1 = (bf16[192,768]{1,0:T(8,128)(2,1)S(1)}, bf16[192,768]{1,0:T(8,128)(2,1)S(1)}, u32[]{:S(2)}, u32[]{:S(2)}) collective-permute-start(bf16[192,768]{1,0:T(8,128)(2,1)S(1)} %select_bitcast_fusion.refs_0_), channel_id=1, source_target_pairs={{1,0},{2,1},{3,2},{0,3},{5,4},{6,5},{7,6},{4,7},{9,8},{10,9},{11,1... | collective-permute-start | bytes 884744 | tf_op jit(solution)/shard_map/ppermute | solution.py:158
  17.8 26.6 %collective-permute-start = (bf16[192,768]{1,0:T(8,128)(2,1)S(1)}, bf16[192,768]{1,0:T(8,128)(2,1)S(1)}, u32[]{:S(2)}, u32[]{:S(2)}) collective-permute-start(bf16[192,768]{1,0:T(8,128)(2,1)S(1)} %select_bitcast_fusion.refs_0_), channel_id=1, source_target_pairs={{515,0},{512,1},{513,2},{514,3},{519,4},{516,5},{517,6},{518,7},{5... | collective-permute-start | bytes 884744 | tf_op jit(solution)/shard_map/ppermute | solution.py:158
  21.9 18.2 %collective-permute-start.4 = (bf16[320,768]{1,0:T(8,128)(2,1)S(1)}, bf16[320,768]{1,0:T(8,128)(2,1)S(1)}, u32[]{:S(2)}, u32[]{:S(2)}) collective-permute-start(bf16[320,768]{1,0:T(8,128)(2,1)S(1)} %get-tuple-element.16.own), channel_id=1, source_target_pairs={{1020,0},{1021,1},{1022,2},{1023,3},{8,4},{9,5},{10,6},{11,7},{4,8... | collective-permute-start | bytes 1474568 | tf_op jit(solution)/shard_map/ppermute | solution.py:158
  23.8 18.3 %collective-permute-start.5 = (bf16[320,768]{1,0:T(8,128)(2,1)S(1)}, bf16[320,768]{1,0:T(8,128)(2,1)S(1)}, u32[]{:S(2)}, u32[]{:S(2)}) collective-permute-start(bf16[320,768]{1,0:T(8,128)(2,1)S(1)} %get-tuple-element.15.refs_0_), channel_id=1, source_target_pairs={{1016,0},{1017,1},{1018,2},{1019,3},{12,4},{13,5},{14,6},{15,7},{0... | collective-permute-start | bytes 1474568 | tf_op jit(solution)/shard_map/ppermute | solution.py:158
  28.1 16.2 %collective-permute-start.2 = (bf16[192,768]{1,0:T(8,128)(2,1)S(1)}, bf16[192,768]{1,0:T(8,128)(2,1)S(1)}, u32[]{:S(2)}, u32[]{:S(2)}) collective-permute-start(bf16[192,768]{1,0:T(8,128)(2,1)S(1)} %shard_map.67.refs_2_.refs_0_), channel_id=1, source_target_pairs={{515,0},{512,1},{513,2},{514,3},{519,4},{516,5},{517,6},{518,7},{5... | collective-permute-start | bytes 884744 | tf_op jit(solution)/shard_map/ppermute | solution.py:158
  40.1 13.8 %collective-permute-start.7 = (bf16[320,768]{1,0:T(8,128)(2,1)S(1)}, bf16[320,768]{1,0:T(8,128)(2,1)S(1)}, u32[]{:S(2)}, u32[]{:S(2)}) collective-permute-start(bf16[320,768]{1,0:T(8,128)(2,1)S(1)} %shard_map.69.refs_1_), channel_id=1, source_target_pairs={{1016,0},{1017,1},{1018,2},{1019,3},{12,4},{13,5},{14,6},{15,7},{0... | collective-permute-start | bytes 1474568 | tf_op jit(solution)/shard_map/ppermute | solution.py:158
  42.2 13.7 %collective-permute-start.6 = (bf16[960,768]{1,0:T(8,128)(2,1)S(1)}, bf16[960,768]{1,0:T(8,128)(2,1)S(1)}, u32[]{:S(2)}, u32[]{:S(2)}) collective-permute-start(bf16[960,768]{1,0:T(8,128)(2,1)S(1)} %shard_map.70.own_r1_r2), channel_id=1, source_target_pairs={{4,0},{5,1},{6,2},{7,3},{0,4},{1,5},{2,6},{3,7},{12,8},{13,9},{14,... | collective-permute-start | bytes 4423688 | tf_op jit(solution)/shard_map/ppermute | solution.py:158
  44.4 11.4 %collective-permute-start.3 = (bf16[768,768]{1,0:T(8,128)(2,1)S(1)}, bf16[768,768]{1,0:T(8,128)(2,1)S(1)}, u32[]{:S(2)}, u32[]{:S(2)}) collective-permute-start(bf16[768,768]{1,0:T(8,128)(2,1)S(1)} %shard_map.68.whole.whole_p), channel_id=1, source_target_pairs={{4,0},{5,1},{6,2},{7,3},{0,4},{1,5},{2,6},{3,7},{12,8},{13,9},{14,... | collective-permute-start | bytes 3538952 | tf_op jit(solution)/shard_map/ppermute | solution.py:158

commit v7 on v6

--- a/solution.py
+++ b/solution.py
@@ -166,11 +166,11 @@
     swap = grid.along_blk(1, -1)
     near = grid.along_z(-1, 1)
     two_on = grid.along_blk(-2, 2)
+    r1 = permute(own_q, grid.along_blk(-1, 1))
     w2 = permute(head_p, grid.along_z(2, -2))
     w1 = permute(head_p, near)
-    r1 = permute(own_q, grid.along_blk(-1, 1))
     r2 = permute(own_p, two_on)
-    w2 = pack(w2)
+    w2 = pack(w2, after=(r1,))
     w3 = permute(w2, near)
     r1 = pack(r1, after=(w2,))
     r3 = permute(r1, two_on)

time: 64 us -> 63.3 us (0.989)
  the two profiles are of different devices: /device:TPU:127 before, /device:TPU:128 now
where the time goes in v7:
time: 63.3 us; the launch traced here: 63 us
  starting transfers between devices  33.7 us (53%)
  waiting for transfers between devices  17.2 us (27%)
  Pallas kernels  9.83 us (16%)
  other arithmetic  1.41 us (2%)
  between operations  0.82 us (1%)
    ppermute x8, starting transfers between devices, permute(): return lax.ppermute(block, AXES, route)  33.7 us
    ppermute x8, waiting for transfers between devices, permute(): return lax.ppermute(block, AXES, route)  17.2 us
    pallas_call x1, Pallas kernels, body(): pl.pallas_call(main_kernel, out_shape=(jax.ShapeDtypeStruct((width, rows)...  7.72 us
    pallas_call x1, Pallas kernels, body(): pl.pallas_call(primary_kernel, out_shape=(jax.ShapeDtypeStruct((4 * rows,...  1.88 us
    select_n x1, other arithmetic, body(): own_p = jnp.where(even, image_feats, text_feats)  1.3 us
  transfers between devices with their start and end apart: 8, of which 3 were waited for; matrix products, arithmetic and copies ran while one was open for 0% of the time, Pallas kernels for 3%

profile of v7, /device:TPU:128, one launch (start us, length us, event | category | flops | bytes accessed | tf_op | source)
XLA Modules:
  0.0 63.0 jit_solution(220219929730666735)
XLA Ops:
  0.6 0.0 copy-start
  0.6 0.0 copy-start.1
  0.7 1.3 %broadcast_select_fusion = (bf16[320,768]{1,0:T(8,128)(2,1)S(1)}, bf16[320,768]{1,0:T(8,128)(2,1)S(1)}) fusion(bf16[320,768]{1,0:T(8,128)(2,1)} %param.4, bf16[320,768]{1,0:T(8,128)(2,1)} %param.5, pred[]{:T(512)S(6)} %eq.5), kind=kLoop, calls=%fused_computation | loop fusion | flops 491520 | bytes 1966081 | tf_op jit(solution)/shard_map/jit(_where)/select_n | solution.py:162
  2.0 6.1 %collective-permute-start.1 = (bf16[320,768]{1,0:T(8,128)(2,1)S(1)}, bf16[320,768]{1,0:T(8,128)(2,1)S(1)}, u32[]{:S(2)}, u32[]{:S(2)}) collective-permute-start(bf16[320,768]{1,0:T(8,128)(2,1)S(1)} %get-tuple-element.16.own), channel_id=1, source_target_pairs={{1020,0},{1021,1},{1022,2},{1023,3},{8,4},{9,5},{10,6},{11,7},{4,8... | collective-permute-start | bytes 1474568 | tf_op jit(solution)/shard_map/ppermute | solution.py:158
  8.1 0.0 copy-done
  8.1 0.0 copy-done.1
  8.1 7.9 %collective-permute-start.2 = (bf16[192,768]{1,0:T(8,128)(2,1)S(1)}, bf16[192,768]{1,0:T(8,128)(2,1)S(1)}, u32[]{:S(2)}, u32[]{:S(2)}) collective-permute-start(bf16[192,768]{1,0:T(8,128)(2,1)S(1)} %select_bitcast_fusion.refs_0_), channel_id=1, source_target_pairs={{1,0},{2,1},{3,2},{0,3},{5,4},{6,5},{7,6},{4,7},{9,8},{10,9},{11,1... | collective-permute-start | bytes 884744 | tf_op jit(solution)/shard_map/ppermute | solution.py:158
  16.1 4.6 %collective-permute-start = (bf16[192,768]{1,0:T(8,128)(2,1)S(1)}, bf16[192,768]{1,0:T(8,128)(2,1)S(1)}, u32[]{:S(2)}, u32[]{:S(2)}) collective-permute-start(bf16[192,768]{1,0:T(8,128)(2,1)S(1)} %select_bitcast_fusion.refs_0_), channel_id=1, source_target_pairs={{515,0},{512,1},{513,2},{514,3},{519,4},{516,5},{517,6},{518,7},{5... | collective-permute-start | bytes 884744 | tf_op jit(solution)/shard_map/ppermute | solution.py:158
  20.7 1.9 %collective-permute-start.5 = (bf16[320,768]{1,0:T(8,128)(2,1)S(1)}, bf16[320,768]{1,0:T(8,128)(2,1)S(1)}, u32[]{:S(2)}, u32[]{:S(2)}) collective-permute-start(bf16[320,768]{1,0:T(8,128)(2,1)S(1)} %get-tuple-element.15.refs_0_), channel_id=1, source_target_pairs={{1016,0},{1017,1},{1018,2},{1019,3},{12,4},{13,5},{14,6},{15,7},{0... | collective-permute-start | bytes 1474568 | tf_op jit(solution)/shard_map/ppermute | solution.py:158
  22.6 0.1 pad_add_fusion.place
  22.7 9.3 %collective-permute-done.2.refs_1_ = bf16[192,768]{1,0:T(8,128)(2,1)S(1)} collective-permute-done((bf16[192,768]{1,0:T(8,128)(2,1)S(1)}, bf16[192,768]{1,0:T(8,128)(2,1)S(1)}, u32[]{:S(2)}, u32[]{:S(2)}) %collective-permute-start.2) | collective-permute-done | bytes 294944 | tf_op jit(solution)/shard_map/ppermute | solution.py:158
  31.9 0.0 collective-permute-done.1.refs_0_.refs_1_
  32.0 2.0 %collective-permute-start.3 = (bf16[192,768]{1,0:T(8,128)(2,1)S(1)}, bf16[192,768]{1,0:T(8,128)(2,1)S(1)}, u32[]{:S(2)}, u32[]{:S(2)}) collective-permute-start(bf16[192,768]{1,0:T(8,128)(2,1)S(1)} %shard_map.67.refs_2_.refs_0_), channel_id=1, source_target_pairs={{515,0},{512,1},{513,2},{514,3},{519,4},{516,5},{517,6},{518,7},{5... | collective-permute-start | bytes 884744 | tf_op jit(solution)/shard_map/ppermute | solution.py:158
  34.0 1.9 %collective-permute-start.7 = (bf16[320,768]{1,0:T(8,128)(2,1)S(1)}, bf16[320,768]{1,0:T(8,128)(2,1)S(1)}, u32[]{:S(2)}, u32[]{:S(2)}) collective-permute-start(bf16[320,768]{1,0:T(8,128)(2,1)S(1)} %shard_map.69.refs_1_), channel_id=1, source_target_pairs={{1016,0},{1017,1},{1018,2},{1019,3},{12,4},{13,5},{14,6},{15,7},{0... | collective-permute-start | bytes 1474568 | tf_op jit(solution)/shard_map/ppermute | solution.py:158
  35.9 1.6 %collective-permute-done.5.refs_2_ = bf16[320,768]{1,0:T(8,128)(2,1)S(1)} collective-permute-done((bf16[320,768]{1,0:T(8,128)(2,1)S(1)}, bf16[320,768]{1,0:T(8,128)(2,1)S(1)}, u32[]{:S(2)}, u32[]{:S(2)}) %collective-permute-start.5) | collective-permute-done | bytes 491552 | tf_op jit(solution)/shard_map/ppermute | solution.py:158
  37.5 0.1 shard_map.70.own_r1_r2
  37.6 7.4 %collective-permute-start.6 = (bf16[960,768]{1,0:T(8,128)(2,1)S(1)}, bf16[960,768]{1,0:T(8,128)(2,1)S(1)}, u32[]{:S(2)}, u32[]{:S(2)}) collective-permute-start(bf16[960,768]{1,0:T(8,128)(2,1)S(1)} %shard_map.70.own_r1_r2), channel_id=1, source_target_pairs={{4,0},{5,1},{6,2},{7,3},{0,4},{1,5},{2,6},{3,7},{12,8},{13,9},{14,... | collective-permute-start | bytes 4423688 | tf_op jit(solution)/shard_map/ppermute | solution.py:158
  45.0 0.0 collective-permute-done.refs_1_
  45.0 0.0 collective-permute-done.3.refs_3_
  45.0 0.1 shard_map.68.whole.whole_p
  45.1 1.9 %collective-permute-start.4 = (bf16[768,768]{1,0:T(8,128)(2,1)S(1)}, bf16[768,768]{1,0:T(8,128)(2,1)S(1)}, u32[]{:S(2)}, u32[]{:S(2)}) collective-permute-start(bf16[768,768]{1,0:T(8,128)(2,1)S(1)} %shard_map.68.whole.whole_p), channel_id=1, source_target_pairs={{4,0},{5,1},{6,2},{7,3},{0,4},{1,5},{2,6},{3,7},{12,8},{13,9},{14,... | collective-permute-start | bytes 3538952 | tf_op jit(solution)/shard_map/ppermute | solution.py:158
  47.0 6.3 %collective-permute-done.7.r3 = bf16[320,768]{1,0:T(8,128)(2,1)S(1)} collective-permute-done((bf16[320,768]{1,0:T(8,128)(2,1)S(1)}, bf16[320,768]{1,0:T(8,128)(2,1)S(1)}, u32[]{:S(2)}, u32[]{:S(2)}) %collective-permute-start.7) | collective-permute-done | bytes 491552 | tf_op jit(solution)/shard_map/ppermute | solution.py:158
  53.3 1.9 %shard_map.71 = (bf16[1280,768]{1,0:T(8,128)(2,1)S(1)}, f32[320,768]{1,0:T(8,128)S(1)}, f32[320,1]{1,0:T(8,128)S(1)}) custom-call(bf16[768,768]{1,0:T(8,128)(2,1)S(1)} %shard_map.68.whole.whole_p, bf16[960,768]{1,0:T(8,128)(2,1)S(1)} %shard_map.70.own_r1_r2, bf16[320,768]{1,0:T(8,128)(2,1)S(1)} %collective-permute-done.7.r3), custom_call_target="tpu_custom_call" | custom-call | flops 15099494400 | bytes 1000000 | tf_op jit(solution)/shard_map/pallas_call | solution.py:182
  55.2 0.0 collective-permute-done.6.others
  55.2 0.0 collective-permute-done.4.whole_q
  55.3 7.7 %shard_map.72 = (bf16[192,320]{1,0:T(8,128)(2,1)}, bf16[192,320]{1,0:T(8,128)(2,1)}, f32[1,80]{1,0:T(1,128)}) custom-call(s32[2]{0:T(128)S(1)} %pad_add_fusion.place, bf16[768,768]{1,0:T(8,128)(2,1)S(1)} %collective-permute-done.4.whole_q, bf16[320,768]{1,0:T(8,128)(2,1)S(1)} %get-tuple-element.16.own, bf16[960,768]{1,0:T(8,128)(2,1)S(1)} %collective-permute-done.6.others, ...), custom_call_target="tpu_custom_call" | custom-call | flops 4529848320 | bytes 1000000 | tf_op jit(solution)/shard_map/pallas_call | solution.py:194
  (3 shorter events, 0.1 us)
Async XLA Ops:
  0.6 7.5 %copy-start = (bf16[768,192]{0,1:T(8,128)(2,1)S(1)}, bf16[768,192]{0,1:T(8,128)(2,1)}, u32[]{:S(2)}) copy-start(bf16[768,192]{0,1:T(8,128)(2,1)} %param.6) | copy-start | bytes 884740
  0.6 7.5 %copy-start.1 = (bf16[768,192]{0,1:T(8,128)(2,1)S(1)}, bf16[768,192]{0,1:T(8,128)(2,1)}, u32[]{:S(2)}) copy-start(bf16[768,192]{0,1:T(8,128)(2,1)} %param.7) | copy-start | bytes 884740
  2.0 30.0 %collective-permute-start.1 = (bf16[320,768]{1,0:T(8,128)(2,1)S(1)}, bf16[320,768]{1,0:T(8,128)(2,1)S(1)}, u32[]{:S(2)}, u32[]{:S(2)}) collective-permute-start(bf16[320,768]{1,0:T(8,128)(2,1)S(1)} %get-tuple-element.16.own), channel_id=1, source_target_pairs={{1020,0},{1021,1},{1022,2},{1023,3},{8,4},{9,5},{10,6},{11,7},{4,8... | collective-permute-start | bytes 1474568 | tf_op jit(solution)/shard_map/ppermute | solution.py:158
  8.1 23.8 %collective-permute-start.2 = (bf16[192,768]{1,0:T(8,128)(2,1)S(1)}, bf16[192,768]{1,0:T(8,128)(2,1)S(1)}, u32[]{:S(2)}, u32[]{:S(2)}) collective-permute-start(bf16[192,768]{1,0:T(8,128)(2,1)S(1)} %select_bitcast_fusion.refs_0_), channel_id=1, source_target_pairs={{1,0},{2,1},{3,2},{0,3},{5,4},{6,5},{7,6},{4,7},{9,8},{10,9},{11,1... | collective-permute-start | bytes 884744 | tf_op jit(solution)/shard_map/ppermute | solution.py:158
  16.1 28.9 %collective-permute-start = (bf16[192,768]{1,0:T(8,128)(2,1)S(1)}, bf16[192,768]{1,0:T(8,128)(2,1)S(1)}, u32[]{:S(2)}, u32[]{:S(2)}) collective-permute-start(bf16[192,768]{1,0:T(8,128)(2,1)S(1)} %select_bitcast_fusion.refs_0_), channel_id=1, source_target_pairs={{515,0},{512,1},{513,2},{514,3},{519,4},{516,5},{517,6},{518,7},{5... | collective-permute-start | bytes 884744 | tf_op jit(solution)/shard_map/ppermute | solution.py:158
  20.7 16.9 %collective-permute-start.5 = (bf16[320,768]{1,0:T(8,128)(2,1)S(1)}, bf16[320,768]{1,0:T(8,128)(2,1)S(1)}, u32[]{:S(2)}, u32[]{:S(2)}) collective-permute-start(bf16[320,768]{1,0:T(8,128)(2,1)S(1)} %get-tuple-element.15.refs_0_), channel_id=1, source_target_pairs={{1016,0},{1017,1},{1018,2},{1019,3},{12,4},{13,5},{14,6},{15,7},{0... | collective-permute-start | bytes 1474568 | tf_op jit(solution)/shard_map/ppermute | solution.py:158
  32.0 13.0 %collective-permute-start.3 = (bf16[192,768]{1,0:T(8,128)(2,1)S(1)}, bf16[192,768]{1,0:T(8,128)(2,1)S(1)}, u32[]{:S(2)}, u32[]{:S(2)}) collective-permute-start(bf16[192,768]{1,0:T(8,128)(2,1)S(1)} %shard_map.67.refs_2_.refs_0_), channel_id=1, source_target_pairs={{515,0},{512,1},{513,2},{514,3},{519,4},{516,5},{517,6},{518,7},{5... | collective-permute-start | bytes 884744 | tf_op jit(solution)/shard_map/ppermute | solution.py:158
  34.0 19.3 %collective-permute-start.7 = (bf16[320,768]{1,0:T(8,128)(2,1)S(1)}, bf16[320,768]{1,0:T(8,128)(2,1)S(1)}, u32[]{:S(2)}, u32[]{:S(2)}) collective-permute-start(bf16[320,768]{1,0:T(8,128)(2,1)S(1)} %shard_map.69.refs_1_), channel_id=1, source_target_pairs={{1016,0},{1017,1},{1018,2},{1019,3},{12,4},{13,5},{14,6},{15,7},{0... | collective-permute-start | bytes 1474568 | tf_op jit(solution)/shard_map/ppermute | solution.py:158
  37.6 17.6 %collective-permute-start.6 = (bf16[960,768]{1,0:T(8,128)(2,1)S(1)}, bf16[960,768]{1,0:T(8,128)(2,1)S(1)}, u32[]{:S(2)}, u32[]{:S(2)}) collective-permute-start(bf16[960,768]{1,0:T(8,128)(2,1)S(1)} %shard_map.70.own_r1_r2), channel_id=1, source_target_pairs={{4,0},{5,1},{6,2},{7,3},{0,4},{1,5},{2,6},{3,7},{12,8},{13,9},{14,... | collective-permute-start | bytes 4423688 | tf_op jit(solution)/shard_map/ppermute | solution.py:158
  45.1 10.1 %collective-permute-start.4 = (bf16[768,768]{1,0:T(8,128)(2,1)S(1)}, bf16[768,768]{1,0:T(8,128)(2,1)S(1)}, u32[]{:S(2)}, u32[]{:S(2)}) collective-permute-start(bf16[768,768]{1,0:T(8,128)(2,1)S(1)} %shard_map.68.whole.whole_p), channel_id=1, source_target_pairs={{4,0},{5,1},{6,2},{7,3},{0,4},{1,5},{2,6},{3,7},{12,8},{13,9},{14,... | collective-permute-start | bytes 3538952 | tf_op jit(solution)/shard_map/ppermute | solution.py:158

commit v8 on v7

v8 whole, which is shorter than its diff:
```python
import functools

import jax
import jax.numpy as jnp
from jax import lax
from jax.experimental import pallas as pl
from jax.experimental.pallas import tpu as pltpu
from jax.sharding import PartitionSpec as P

LOGIT_SCALE = 10.0
LOGIT_BIAS = -2.0
EPSILON = 1e-06
PACK = 20_000_000_000
AXES = ("blk", "head")
LANES = 128


class Grid:
    def __init__(self, n_blk, n_head):
        self.n_blk, self.n_head = n_blk, n_head
        self.half = n_blk // 2
        self.depth = 2 * n_head

    def route(self, source, heads=None):
        heads = heads or range(self.n_head)
        return [(source(d), d) for d in range(self.n_blk * self.n_head) if d % self.n_head in heads]

    def along_blk(self, even, odd, heads=None):
        def source(d):
            blk, head = divmod(d, self.n_head)
            step = odd if blk % 2 else even
            return (blk + step) % self.n_blk * self.n_head + head

        return self.route(source, heads)

    def along_z(self, even, odd):
        def source(d):
            blk, head = divmod(d, self.n_head)
            z = 2 * head + blk // self.half
            z = (z + (odd if z % 2 else even)) % self.depth
            return (blk % self.half + self.half * (z % 2)) * self.n_head + z // 2

        return self.route(source)


def dot(left, right, left_dim=1, right_dim=0):
    return lax.dot_general(
        left, right, (((left_dim,), (right_dim,)), ((), ())), preferred_element_type=jnp.float32
    )


def project(feats, whole):
    z = dot(feats, whole[...], 1, 1)
    back = 1.0 / jnp.sqrt(jnp.sum(z * z, axis=1, keepdims=True) + EPSILON)
    return z, back, (z * back).astype(jnp.bfloat16)


def window(group, width):
    start = group * width // LANES * LANES
    return pl.multiple_of(start, LANES), pl.multiple_of(group * width - start, 64)


def pack_kernel(skipped, *refs):
    *blocks, out = refs[skipped:]
    at = 0
    for block in blocks:
        out[at : at + block.shape[0], :] = block[...]
        at += block.shape[0]


def either_kernel(place, early, late, _, out):
    @pl.when(place[2] != 0)
    def _():
        out[...] = early[...]

    @pl.when(place[2] == 0)
    def _():
        out[...] = late[...]


def project_all(blocks, whole, u_out, z_out, back_out):
    rows = z_out.shape[0]
    for k, block in enumerate(blocks):
        z, back, u = project(block, whole)
        u_out[k * rows : (k + 1) * rows, :] = u
        if k == 0:
            z_out[...] = z
            back_out[...] = back


def primary_kernel(whole, blocks, u_out, z_out, back_out):
    rows = z_out.shape[0]
    project_all([blocks[k * rows : (k + 1) * rows, :] for k in range(3)], whole, u_out, z_out, back_out)


def weights_of(logits, turned):
    if turned:
        on = lax.broadcasted_iota(jnp.int32, logits.shape, 0) == lax.broadcasted_iota(
            jnp.int32, logits.shape, 1
        )
        turn = jnp.where(on, -1.0, 1.0)
        return (turn * LOGIT_SCALE / (1.0 + jnp.exp(-turn * logits))).astype(jnp.bfloat16)
    return (LOGIT_SCALE / (1.0 + jnp.exp(-logits))).astype(jnp.bfloat16)


def side(place, u_own, met, z, back, whole, logits_ref, grad_ref, grad_out, loss_out):
    group, width = place[0], grad_out.shape[0]
    rows = u_own.shape[0]
    at, g = 0, None
    for u in met:
        logits = LOGIT_SCALE * dot(u_own, u, 1, 1) + LOGIT_BIAS
        logits_ref[:, at : at + u.shape[0]] = logits
        if at == 0:
            g = dot(weights_of(logits[:, :rows], True), u[:rows, :])
            if u.shape[0] > rows:
                g = g + dot(weights_of(logits[:, rows:], False), u[rows:, :])
        else:
            g = g + dot(weights_of(logits, False), u)
        at += u.shape[0]
    inner = jnp.sum(g * z, axis=1, keepdims=True)
    dz = (g * back - z * (inner * back * back * back)).astype(jnp.bfloat16)
    start, offset = window(group, width)
    grad_ref[...] = jnp.transpose(dot(dz, whole[:, pl.ds(start, grad_ref.shape[0])]))
    grad_out[...] = grad_ref[pl.ds(offset, width), :].astype(grad_out.dtype)
    quarter = loss_out.shape[1]
    first = pl.multiple_of(group * quarter, 8)
    x = logits_ref[pl.ds(first, quarter), :]
    on = first + lax.broadcasted_iota(jnp.int32, x.shape, 0) == lax.broadcasted_iota(
        jnp.int32, x.shape, 1
    )
    x = jnp.where(on, -x, x)
    loss = jnp.sum(jnp.maximum(x, 0.0) + jnp.log1p(jnp.exp(-jnp.abs(x))), axis=1, keepdims=True)
    loss_out[...] = jnp.transpose(jnp.broadcast_to(loss, (quarter, LANES)))[:1, :]


def primary_side_kernel(
    place, whole_q, own_q, others, whole_p, u_p, z_p, back_p,
    grad_out, loss_out, u_out, z_out, back_out, u_q, logits_ref, grad_ref,
):
    rows = own_q.shape[0]
    blocks = [own_q[...]] + [others[k * rows : (k + 1) * rows, :] for k in range(3)]
    project_all(blocks, whole_q, u_q, z_out, back_out)
    u_out[...] = u_q[:rows, :]
    side(
        place, u_p[:rows, :], [u_q[...]], z_p[...], back_p[...], whole_p, logits_ref, grad_ref,
        grad_out, loss_out,
    )


def secondary_side_kernel(
    place, whole_p, r3, u_p, whole_q, u_q, z_q, back_q, grad_p, loss_p,
    image_out, text_out, loss_out, logits_ref, grad_ref, grad_q,
):
    _, _, u_3 = project(r3[...], whole_p)
    side(
        place, u_q[...], [u_p[...], u_3], z_q[...], back_q[...], whole_q, logits_ref, grad_ref,
        grad_q, loss_out,
    )

    @pl.when(place[1] == 0)
    def _():
        image_out[...] = grad_p[...]
        text_out[...] = grad_q[...]
        loss_out[...] = loss_p[...]

    @pl.when(place[1] != 0)
    def _():
        image_out[...] = grad_q[...]
        text_out[...] = grad_p[...]


ANY = pl.BlockSpec(memory_space=pl.ANY)
VMEM = pl.BlockSpec(memory_space=pltpu.VMEM)
SMEM = pl.BlockSpec(memory_space=pltpu.SMEM)
PARAMS = pltpu.CompilerParams(vmem_limit_bytes=16 * 1024 * 1024)


def cost(flops):
    return pl.CostEstimate(flops=flops, bytes_accessed=1_000_000, transcendentals=0)


def pack(*blocks, after=()):
    rows = sum(block.shape[0] for block in blocks)
    return pl.pallas_call(
        functools.partial(pack_kernel, len(after)),
        out_shape=jax.ShapeDtypeStruct((rows, blocks[0].shape[1]), blocks[0].dtype),
        in_specs=[ANY] * len(after) + [VMEM] * len(blocks),
        out_specs=VMEM,
        compiler_params=PARAMS,
        cost_estimate=cost(PACK),
    )(*after, *blocks)


def body(image_feats, text_feats, image_head, text_head):
    rows, depth = image_feats.shape
    groups = lax.axis_size("head")
    grid = Grid(lax.axis_size("blk"), groups)
    width = image_head.shape[1]
    features = width * groups
    group = lax.axis_index("head")
    place = jnp.stack([group, lax.axis_index("blk") % 2, group < groups // 2]).astype(jnp.int32)

    def permute(block, route):
        return lax.ppermute(block, AXES, route)

    even = place[1] == 0
    image_head, text_head = image_head.T, text_head.T
    own_p = jnp.where(even, image_feats, text_feats)
    own_q = jnp.where(even, text_feats, image_feats)
    head_p = jnp.where(even, image_head, text_head)

    swap = grid.along_blk(1, -1)
    near = grid.along_z(-1, 1)
    two_on = grid.along_blk(-2, 2)
    early, late = range(groups // 2), range(groups // 2, groups)
    early_1 = permute(own_q, grid.along_blk(-1, 1, early))
    w2 = permute(head_p, grid.along_z(2, -2))
    w1 = permute(head_p, near)
    late_1 = permute(own_q, grid.along_blk(-1, 1, late))
    r2 = permute(own_p, two_on)
    w2 = pack(w2, after=(early_1,))
    w3 = permute(w2, near)
    r1 = pl.pallas_call(
        either_kernel,
        out_shape=jax.ShapeDtypeStruct((rows, depth), own_q.dtype),
        in_specs=[SMEM, VMEM, VMEM, ANY],
        out_specs=VMEM,
        compiler_params=PARAMS,
        cost_estimate=cost(PACK),
    )(place, early_1, late_1, w2)
    r3 = permute(r1, two_on)
    own_r1_r2 = pack(own_p, r1, r2)
    others = permute(own_r1_r2, swap)
    whole_p = pack(head_p, w1, w2, w3)
    whole_q = permute(whole_p, swap)

    own_z = jax.ShapeDtypeStruct((rows, features), jnp.float32)
    own_back = jax.ShapeDtypeStruct((rows, 1), jnp.float32)
    grad = jax.ShapeDtypeStruct((width, rows), jnp.bfloat16)
    loss = jax.ShapeDtypeStruct((1, rows // groups), jnp.float32)
    scratch = [
        pltpu.VMEM((rows, 4 * rows), jnp.float32),
        pltpu.VMEM((2 * LANES, rows), jnp.float32),
    ]
    u_p, z_p, back_p = pl.pallas_call(
        primary_kernel,
        out_shape=(jax.ShapeDtypeStruct((3 * rows, features), jnp.bfloat16), own_z, own_back),
        in_specs=[VMEM] * 2,
        out_specs=(VMEM,) * 3,
        compiler_params=PARAMS,
        cost_estimate=cost(80 * rows * depth * features),
    )(whole_p, own_r1_r2)
    grad_p, loss_p, u_q, z_q, back_q = pl.pallas_call(
        primary_side_kernel,
        out_shape=(
            grad, loss, jax.ShapeDtypeStruct((rows, features), jnp.bfloat16), own_z, own_back,
        ),
        in_specs=[SMEM] + [VMEM] * 7,
        out_specs=(VMEM,) * 5,
        scratch_shapes=[pltpu.VMEM((4 * rows, features), jnp.bfloat16)] + scratch,
        compiler_params=PARAMS,
        cost_estimate=cost(24 * rows * depth * features),
    )(place, whole_q, own_q, others, whole_p, u_p, z_p, back_p)
    image_grad, text_grad, loss = pl.pallas_call(
        secondary_side_kernel,
        out_shape=(grad, grad, loss),
        in_specs=[SMEM] + [VMEM] * 9,
        out_specs=(VMEM,) * 3,
        scratch_shapes=scratch + [pltpu.VMEM(grad.shape, grad.dtype)],
        compiler_params=PARAMS,
        cost_estimate=cost(12 * rows * depth * features),
    )(place, whole_p, r3, u_p, whole_q, u_q, z_q, back_q, grad_p, loss_p)
    return image_grad.T, text_grad.T, loss.reshape(rows // groups)


def solution(mesh):
    in_specs = (P("blk", None), P("blk", None), P(None, "head"), P(None, "head"))
    out_specs = (P("blk", "head"), P("blk", "head"), P(("blk", "head")))
    return jax.shard_map(body, mesh=mesh, in_specs=in_specs, out_specs=out_specs, check_vma=False)
```

time: 63.3 us -> 59.6 us (0.942)
  the two profiles are of different devices: /device:TPU:128 before, /device:TPU:1 now
where the time goes in v8:
time: 59.6 us; the launch traced here: 59.3 us
  starting transfers between devices  44 us (74%)
  Pallas kernels  12.2 us (20%)
  other arithmetic  1.41 us (2%)
  waiting for transfers between devices  0.89 us (1%)
  between operations  0.85 us (1%)
    ppermute x9, starting transfers between devices, permute(): return lax.ppermute(block, AXES, route)  44 us
    pallas_call x1, Pallas kernels, body(): pl.pallas_call(secondary_side_kernel, out_shape=(grad, grad, loss), in_sp...  4.92 us
    pallas_call x1, Pallas kernels, body(): pl.pallas_call(primary_side_kernel, out_shape=(grad, loss, jax.ShapeDtype...  4.87 us
    pallas_call x1, Pallas kernels, body(): pl.pallas_call(primary_kernel, out_shape=(jax.ShapeDtypeStruct((3 * rows,...  1.58 us
    select_n x1, other arithmetic, body(): own_p = jnp.where(even, image_feats, text_feats)  1.3 us
  transfers between devices with their start and end apart: 9, of which 1 were waited for; matrix products, arithmetic and copies ran while one was open for 0% of the time, Pallas kernels for 12%

profile of v8, /device:TPU:1, one launch (start us, length us, event | category | flops | bytes accessed | tf_op | source)
XLA Modules:
  0.0 59.3 jit_solution(2838102488412501512)
XLA Ops:
  0.6 0.0 copy-start.1
  0.6 0.0 copy-start
  0.7 1.3 %broadcast_select_fusion = (bf16[320,768]{1,0:T(8,128)(2,1)S(1)}, bf16[320,768]{1,0:T(8,128)(2,1)S(1)}) fusion(bf16[320,768]{1,0:T(8,128)(2,1)} %param.4, bf16[320,768]{1,0:T(8,128)(2,1)} %param.5, pred[]{:T(512)S(6)} %eq.5), kind=kLoop, calls=%fused_computation | loop fusion | flops 491520 | bytes 1966081 | tf_op jit(solution)/shard_map/jit(_where)/select_n | solution.py:208
  2.0 4.5 %collective-permute-start.1 = (bf16[320,768]{1,0:T(8,128)(2,1)S(1)}, bf16[320,768]{1,0:T(8,128)(2,1)S(1)}, u32[]{:S(2)}, u32[]{:S(2)}) collective-permute-start(bf16[320,768]{1,0:T(8,128)(2,1)S(1)} %get-tuple-element.26.own_q), channel_id=1, source_target_pairs={{1020,0},{1021,1},{8,4},{9,5},{4,8},{5,9},{16,12},{17,13},{12,16},... | collective-permute-start | bytes 1474568 | tf_op jit(solution)/shard_map/ppermute | solution.py:204
  6.5 0.0 copy-done.1
  6.5 0.0 copy-done
  6.6 13.1 %collective-permute-start.2 = (bf16[192,768]{1,0:T(8,128)(2,1)S(1)}, bf16[192,768]{1,0:T(8,128)(2,1)S(1)}, u32[]{:S(2)}, u32[]{:S(2)}) collective-permute-start(bf16[192,768]{1,0:T(8,128)(2,1)S(1)} %select_bitcast_fusion.refs_0_), channel_id=1, source_target_pairs={{1,0},{2,1},{3,2},{0,3},{5,4},{6,5},{7,6},{4,7},{9,8},{10,9},{11,1... | collective-permute-start | bytes 884744 | tf_op jit(solution)/shard_map/ppermute | solution.py:204
  19.7 2.8 %collective-permute-start = (bf16[192,768]{1,0:T(8,128)(2,1)S(1)}, bf16[192,768]{1,0:T(8,128)(2,1)S(1)}, u32[]{:S(2)}, u32[]{:S(2)}) collective-permute-start(bf16[192,768]{1,0:T(8,128)(2,1)S(1)} %select_bitcast_fusion.refs_0_), channel_id=1, source_target_pairs={{515,0},{512,1},{513,2},{514,3},{519,4},{516,5},{517,6},{518,7},{5... | collective-permute-start | bytes 884744 | tf_op jit(solution)/shard_map/ppermute | solution.py:204
  22.5 0.7 %collective-permute-start.4 = (bf16[320,768]{1,0:T(8,128)(2,1)S(1)}, bf16[320,768]{1,0:T(8,128)(2,1)S(1)}, u32[]{:S(2)}, u32[]{:S(2)}) collective-permute-start(bf16[320,768]{1,0:T(8,128)(2,1)S(1)} %get-tuple-element.26.own_q), channel_id=1, source_target_pairs={{1022,2},{1023,3},{10,6},{11,7},{6,10},{7,11},{18,14},{19,15},{14,... | collective-permute-start | bytes 1474568 | tf_op jit(solution)/shard_map/ppermute | solution.py:204
  23.2 6.9 %collective-permute-start.6 = (bf16[320,768]{1,0:T(8,128)(2,1)S(1)}, bf16[320,768]{1,0:T(8,128)(2,1)S(1)}, u32[]{:S(2)}, u32[]{:S(2)}) collective-permute-start(bf16[320,768]{1,0:T(8,128)(2,1)S(1)} %get-tuple-element.25.refs_0_), channel_id=1, source_target_pairs={{1016,0},{1017,1},{1018,2},{1019,3},{12,4},{13,5},{14,6},{15,7},{0... | collective-permute-start | bytes 1474568 | tf_op jit(solution)/shard_map/ppermute | solution.py:204
  30.2 0.1 pad_add_fusion.place
  30.2 0.0 collective-permute-done.2.refs_1_
  30.2 0.0 collective-permute-done.1.refs_0_.early
  30.3 6.8 %collective-permute-start.3 = (bf16[192,768]{1,0:T(8,128)(2,1)S(1)}, bf16[192,768]{1,0:T(8,128)(2,1)S(1)}, u32[]{:S(2)}, u32[]{:S(2)}) collective-permute-start(bf16[192,768]{1,0:T(8,128)(2,1)S(1)} %shard_map.67.refs_2_._), channel_id=1, source_target_pairs={{515,0},{512,1},{513,2},{514,3},{519,4},{516,5},{517,6},{518,7},{5... | collective-permute-start | bytes 884744 | tf_op jit(solution)/shard_map/ppermute | solution.py:204
  37.1 0.0 collective-permute-done.4.late
  37.1 0.6 shard_map.69.refs_1_
  37.7 3.8 %collective-permute-start.5 = (bf16[320,768]{1,0:T(8,128)(2,1)S(1)}, bf16[320,768]{1,0:T(8,128)(2,1)S(1)}, u32[]{:S(2)}, u32[]{:S(2)}) collective-permute-start(bf16[320,768]{1,0:T(8,128)(2,1)S(1)} %shard_map.69.refs_1_), channel_id=1, source_target_pairs={{1016,0},{1017,1},{1018,2},{1019,3},{12,4},{13,5},{14,6},{15,7},{0... | collective-permute-start | bytes 1474568 | tf_op jit(solution)/shard_map/ppermute | solution.py:204
  41.5 0.0 collective-permute-done.6.refs_2_
  41.5 0.1 shard_map.70.blocks
  41.6 1.9 %collective-permute-start.8 = (bf16[960,768]{1,0:T(8,128)(2,1)S(1)}, bf16[960,768]{1,0:T(8,128)(2,1)S(1)}, u32[]{:S(2)}, u32[]{:S(2)}) collective-permute-start(bf16[960,768]{1,0:T(8,128)(2,1)S(1)} %shard_map.70.blocks), channel_id=1, source_target_pairs={{4,0},{5,1},{6,2},{7,3},{0,4},{1,5},{2,6},{3,7},{12,8},{13,9},{14,... | collective-permute-start | bytes 4423688 | tf_op jit(solution)/shard_map/ppermute | solution.py:204
  43.5 0.0 collective-permute-done.refs_1_
  43.5 0.0 collective-permute-done.3.refs_3_
  43.6 0.1 shard_map.68.whole.whole_p
  43.6 3.4 %collective-permute-start.7 = (bf16[768,768]{1,0:T(8,128)(2,1)S(1)}, bf16[768,768]{1,0:T(8,128)(2,1)S(1)}, u32[]{:S(2)}, u32[]{:S(2)}) collective-permute-start(bf16[768,768]{1,0:T(8,128)(2,1)S(1)} %shard_map.68.whole.whole_p), channel_id=1, source_target_pairs={{4,0},{5,1},{6,2},{7,3},{0,4},{1,5},{2,6},{3,7},{12,8},{13,9},{14,... | collective-permute-start | bytes 3538952 | tf_op jit(solution)/shard_map/ppermute | solution.py:204
  47.0 1.6 %shard_map.71 = (bf16[960,768]{1,0:T(8,128)(2,1)S(1)}, f32[320,768]{1,0:T(8,128)S(1)}, f32[320,1]{1,0:T(8,128)S(1)}) custom-call(bf16[768,768]{1,0:T(8,128)(2,1)S(1)} %shard_map.68.whole.whole_p, bf16[960,768]{1,0:T(8,128)(2,1)S(1)} %shard_map.70.blocks), custom_call_target="tpu_custom_call" | custom-call | flops 15099494400 | bytes 1000000 | tf_op jit(solution)/shard_map/pallas_call | solution.py:245
  48.6 0.9 %collective-permute-done.7.whole_q = bf16[768,768]{1,0:T(8,128)(2,1)S(1)} collective-permute-done((bf16[768,768]{1,0:T(8,128)(2,1)S(1)}, bf16[768,768]{1,0:T(8,128)(2,1)S(1)}, u32[]{:S(2)}, u32[]{:S(2)}) %collective-permute-start.7) | collective-permute-done | bytes 1179680 | tf_op jit(solution)/shard_map/ppermute | solution.py:204
  49.5 0.0 collective-permute-done.8.others
  49.5 4.9 %shard_map.72 = (bf16[192,320]{1,0:T(8,128)(2,1)S(1)}, f32[1,80]{1,0:T(1,128)S(1)}, bf16[320,768]{1,0:T(8,128)(2,1)S(1)}, f32[320,768]{1,0:T(8,128)S(1)}, f32[320,1]{1,0:T(8,128)S(1)}) custom-call(s32[3]{0:T(128)S(1)} %pad_add_fusion.place, bf16[768,768]{1,0:T(8,128)(2,1)S(1)} %collective-permute-done.7.whole_q, ...), custom_call_target="tpu_custom_call" | custom-call | flops 4529848320 | bytes 1000000 | tf_op jit(solution)/shard_map/pallas_call | solution.py:253
  54.3 0.0 collective-permute-done.5.r3
  54.3 4.9 %shard_map.73 = (bf16[192,320]{1,0:T(8,128)(2,1)}, bf16[192,320]{1,0:T(8,128)(2,1)}, f32[1,80]{1,0:T(1,128)}) custom-call(s32[3]{0:T(128)S(1)} %pad_add_fusion.place, bf16[768,768]{1,0:T(8,128)(2,1)S(1)} %shard_map.68.whole.whole_p, bf16[320,768]{1,0:T(8,128)(2,1)S(1)} %collective-permute-done.5.r3, bf16[960,768]{1,0:T(8,128)(2,1)S(1)} %get-tuple-element.14.u_p, ...), custom_call_target="tpu_custom_call" | custom-call | flops 2264924160 | bytes 1000000 | tf_op jit(solution)/shard_map/pallas_call | solution.py:264
  (2 shorter events, 0.1 us)
Async XLA Ops:
  0.6 5.9 %copy-start.1 = (bf16[768,192]{0,1:T(8,128)(2,1)S(1)}, bf16[768,192]{0,1:T(8,128)(2,1)}, u32[]{:S(2)}) copy-start(bf16[768,192]{0,1:T(8,128)(2,1)} %param.7) | copy-start | bytes 884740
  0.6 5.9 %copy-start = (bf16[768,192]{0,1:T(8,128)(2,1)S(1)}, bf16[768,192]{0,1:T(8,128)(2,1)}, u32[]{:S(2)}) copy-start(bf16[768,192]{0,1:T(8,128)(2,1)} %param.6) | copy-start | bytes 884740
  2.0 28.3 %collective-permute-start.1 = (bf16[320,768]{1,0:T(8,128)(2,1)S(1)}, bf16[320,768]{1,0:T(8,128)(2,1)S(1)}, u32[]{:S(2)}, u32[]{:S(2)}) collective-permute-start(bf16[320,768]{1,0:T(8,128)(2,1)S(1)} %get-tuple-element.26.own_q), channel_id=1, source_target_pairs={{1020,0},{1021,1},{8,4},{9,5},{4,8},{5,9},{16,12},{17,13},{12,16},... | collective-permute-start | bytes 1474568 | tf_op jit(solution)/shard_map/ppermute | solution.py:204
  6.6 23.7 %collective-permute-start.2 = (bf16[192,768]{1,0:T(8,128)(2,1)S(1)}, bf16[192,768]{1,0:T(8,128)(2,1)S(1)}, u32[]{:S(2)}, u32[]{:S(2)}) collective-permute-start(bf16[192,768]{1,0:T(8,128)(2,1)S(1)} %select_bitcast_fusion.refs_0_), channel_id=1, source_target_pairs={{1,0},{2,1},{3,2},{0,3},{5,4},{6,5},{7,6},{4,7},{9,8},{10,9},{11,1... | collective-permute-start | bytes 884744 | tf_op jit(solution)/shard_map/ppermute | solution.py:204
  19.7 23.9 %collective-permute-start = (bf16[192,768]{1,0:T(8,128)(2,1)S(1)}, bf16[192,768]{1,0:T(8,128)(2,1)S(1)}, u32[]{:S(2)}, u32[]{:S(2)}) collective-permute-start(bf16[192,768]{1,0:T(8,128)(2,1)S(1)} %select_bitcast_fusion.refs_0_), channel_id=1, source_target_pairs={{515,0},{512,1},{513,2},{514,3},{519,4},{516,5},{517,6},{518,7},{5... | collective-permute-start | bytes 884744 | tf_op jit(solution)/shard_map/ppermute | solution.py:204
  22.5 14.5 %collective-permute-start.4 = (bf16[320,768]{1,0:T(8,128)(2,1)S(1)}, bf16[320,768]{1,0:T(8,128)(2,1)S(1)}, u32[]{:S(2)}, u32[]{:S(2)}) collective-permute-start(bf16[320,768]{1,0:T(8,128)(2,1)S(1)} %get-tuple-element.26.own_q), channel_id=1, source_target_pairs={{1022,2},{1023,3},{10,6},{11,7},{6,10},{7,11},{18,14},{19,15},{14,... | collective-permute-start | bytes 1474568 | tf_op jit(solution)/shard_map/ppermute | solution.py:204
  23.2 18.3 %collective-permute-start.6 = (bf16[320,768]{1,0:T(8,128)(2,1)S(1)}, bf16[320,768]{1,0:T(8,128)(2,1)S(1)}, u32[]{:S(2)}, u32[]{:S(2)}) collective-permute-start(bf16[320,768]{1,0:T(8,128)(2,1)S(1)} %get-tuple-element.25.refs_0_), channel_id=1, source_target_pairs={{1016,0},{1017,1},{1018,2},{1019,3},{12,4},{13,5},{14,6},{15,7},{0... | collective-permute-start | bytes 1474568 | tf_op jit(solution)/shard_map/ppermute | solution.py:204
  30.3 13.3 %collective-permute-start.3 = (bf16[192,768]{1,0:T(8,128)(2,1)S(1)}, bf16[192,768]{1,0:T(8,128)(2,1)S(1)}, u32[]{:S(2)}, u32[]{:S(2)}) collective-permute-start(bf16[192,768]{1,0:T(8,128)(2,1)S(1)} %shard_map.67.refs_2_._), channel_id=1, source_target_pairs={{515,0},{512,1},{513,2},{514,3},{519,4},{516,5},{517,6},{518,7},{5... | collective-permute-start | bytes 884744 | tf_op jit(solution)/shard_map/ppermute | solution.py:204
  37.7 16.7 %collective-permute-start.5 = (bf16[320,768]{1,0:T(8,128)(2,1)S(1)}, bf16[320,768]{1,0:T(8,128)(2,1)S(1)}, u32[]{:S(2)}, u32[]{:S(2)}) collective-permute-start(bf16[320,768]{1,0:T(8,128)(2,1)S(1)} %shard_map.69.refs_1_), channel_id=1, source_target_pairs={{1016,0},{1017,1},{1018,2},{1019,3},{12,4},{13,5},{14,6},{15,7},{0... | collective-permute-start | bytes 1474568 | tf_op jit(solution)/shard_map/ppermute | solution.py:204
  41.6 7.9 %collective-permute-start.8 = (bf16[960,768]{1,0:T(8,128)(2,1)S(1)}, bf16[960,768]{1,0:T(8,128)(2,1)S(1)}, u32[]{:S(2)}, u32[]{:S(2)}) collective-permute-start(bf16[960,768]{1,0:T(8,128)(2,1)S(1)} %shard_map.70.blocks), channel_id=1, source_target_pairs={{4,0},{5,1},{6,2},{7,3},{0,4},{1,5},{2,6},{3,7},{12,8},{13,9},{14,... | collective-permute-start | bytes 4423688 | tf_op jit(solution)/shard_map/ppermute | solution.py:204
  43.6 5.8 %collective-permute-start.7 = (bf16[768,768]{1,0:T(8,128)(2,1)S(1)}, bf16[768,768]{1,0:T(8,128)(2,1)S(1)}, u32[]{:S(2)}, u32[]{:S(2)}) collective-permute-start(bf16[768,768]{1,0:T(8,128)(2,1)S(1)} %shard_map.68.whole.whole_p), channel_id=1, source_target_pairs={{4,0},{5,1},{6,2},{7,3},{0,4},{1,5},{2,6},{3,7},{12,8},{13,9},{14,... | collective-permute-start | bytes 3538952 | tf_op jit(solution)/shard_map/ppermute | solution.py:204

commit v9 on v7

--- a/solution.py
+++ b/solution.py
@@ -21,16 +21,17 @@
         self.half = n_blk // 2
         self.depth = 2 * n_head
 
-    def route(self, source):
-        return [(source(d), d) for d in range(self.n_blk * self.n_head)]
-
-    def along_blk(self, even, odd):
+    def route(self, source, heads=None):
+        heads = heads or range(self.n_head)
+        return [(source(d), d) for d in range(self.n_blk * self.n_head) if d % self.n_head in heads]
+
+    def along_blk(self, even, odd, heads=None):
         def source(d):
             blk, head = divmod(d, self.n_head)
             step = odd if blk % 2 else even
             return (blk + step) % self.n_blk * self.n_head + head
 
-        return self.route(source)
+        return self.route(source, heads)
 
     def along_z(self, even, odd):
         def source(d):
@@ -67,15 +68,29 @@
         at += block.shape[0]
 
 
-def primary_kernel(whole, own_r1_r2, r3, u_out, z_out, back_out):
-    rows = r3.shape[0]
-    for k in range(4):
-        block = r3[...] if k == 3 else own_r1_r2[k * rows : (k + 1) * rows, :]
+def either_kernel(place, early, late, _, out):
+    @pl.when(place[2] != 0)
+    def _():
+        out[...] = early[...]
+
+    @pl.when(place[2] == 0)
+    def _():
+        out[...] = late[...]
+
+
+def project_all(blocks, whole, u_out, z_out, back_out):
+    rows = z_out.shape[0]
+    for k, block in enumerate(blocks):
         z, back, u = project(block, whole)
         u_out[k * rows : (k + 1) * rows, :] = u
         if k == 0:
             z_out[...] = z
             back_out[...] = back
+
+
+def primary_kernel(whole, blocks, u_out, z_out, back_out):
+    rows = z_out.shape[0]
+    project_all([blocks[k * rows : (k + 1) * rows, :] for k in range(3)], whole, u_out, z_out, back_out)
 
 
 def side(u_own, u_others, z, back, cut, logits_ref, at):
@@ -96,21 +111,25 @@
     return jnp.transpose(dot(dz, cut))
 
 
-def main_kernel(
-    place, whole_q, own, others, whole_p, u_p, z_p, back_p, image_out, text_out, loss_out,
-    u_q, logits_ref, grads,
+def secondary_kernel(whole, own, others, u_out, z_out, back_out):
+    rows = z_out.shape[0]
+    blocks = [own[...]] + [others[k * rows : (k + 1) * rows, :] for k in range(3)]
+    project_all(blocks, whole, u_out, z_out, back_out)
+
+
+def sides_kernel(
+    place, whole_p, r3, u_p3, z_p, back_p, whole_q, u_q, z_q, back_q, image_out, text_out, loss_out,
+    u_p, logits_ref, grads,
 ):
     group, swapped = place[0], place[1]
     rows, width = image_out.shape[1], image_out.shape[0]
     start, offset = window(group, width)
     columns = pl.ds(start, grads.shape[1])
-    z_q, back_q, u = project(own[...], whole_q)
-    u_q[:rows, :] = u
-    for k in range(3):
-        _, _, u = project(others[k * rows : (k + 1) * rows, :], whole_q)
-        u_q[(k + 1) * rows : (k + 2) * rows, :] = u
+    _, _, u = project(r3[...], whole_p)
+    u_p[3 * rows :, :] = u
+    u_p[: 3 * rows, :] = u_p3[...]
     grads[0] = side(u_p[:rows, :], u_q, z_p[...], back_p[...], whole_p[:, columns], logits_ref, 0)
-    grads[1] = side(u_q[:rows, :], u_p, z_q, back_q, whole_q[:, columns], logits_ref, 1)
+    grads[1] = side(u_q[:rows, :], u_p, z_q[...], back_q[...], whole_q[:, columns], logits_ref, 1)
     image_out[...] = grads[swapped, pl.ds(offset, width), :].astype(image_out.dtype)
     text_out[...] = grads[1 - swapped, pl.ds(offset, width), :].astype(text_out.dtype)
     quarter = loss_out.shape[1]
@@ -152,7 +171,8 @@
     grid = Grid(lax.axis_size("blk"), groups)
     width = image_head.shape[1]
     features = width * groups
-    place = jnp.stack([lax.axis_index("head"), lax.axis_index("blk") % 2]).astype(jnp.int32)
+    group = lax.axis_index("head")
+    place = jnp.stack([group, lax.axis_index("blk") % 2, group < groups // 2]).astype(jnp.int32)
 
     def permute(block, route):
         return lax.ppermute(block, AXES, route)
@@ -166,39 +186,52 @@
     swap = grid.along_blk(1, -1)
     near = grid.along_z(-1, 1)
     two_on = grid.along_blk(-2, 2)
-    r1 = permute(own_q, grid.along_blk(-1, 1))
+    early, late = range(groups // 2), range(groups // 2, groups)
+    early_1 = permute(own_q, grid.along_blk(-1, 1, early))
     w2 = permute(head_p, grid.along_z(2, -2))
     w1 = permute(head_p, near)
+    late_1 = permute(own_q, grid.along_blk(-1, 1, late))
     r2 = permute(own_p, two_on)
-    w2 = pack(w2, after=(r1,))
+    w2 = pack(w2, after=(early_1,))
     w3 = permute(w2, near)
-    r1 = pack(r1, after=(w2,))
+    r1 = pl.pallas_call(
+        either_kernel,
+        out_shape=jax.ShapeDtypeStruct((rows, depth), own_q.dtype),
+        in_specs=[SMEM, VMEM, VMEM, ANY],
+        out_specs=VMEM,
+        compiler_params=PARAMS,
+        cost_estimate=cost(PACK),
+    )(place, early_1, late_1, w2)
     r3 = permute(r1, two_on)
     own_r1_r2 = pack(own_p, r1, r2)
     others = permute(own_r1_r2, swap)
     whole_p = pack(head_p, w1, w2, w3)
     whole_q = permute(whole_p, swap)
 
+    own_z = jax.ShapeDtypeStruct((rows, features), jnp.float32)
+    own_back = jax.ShapeDtypeStruct((rows, 1), jnp.float32)
+    grad = jax.ShapeDtypeStruct((width, rows), jnp.bfloat16)
+    loss = jax.ShapeDtypeStruct((1, rows // groups), jnp.float32)
     u_p, z_p, back_p = pl.pallas_call(
         primary_kernel,
-        out_shape=(
-            jax.ShapeDtypeStruct((4 * rows, features), jnp.bfloat16),
-            jax.ShapeDtypeStruct((rows, features), jnp.float32),
-            jax.ShapeDtypeStruct((rows, 1), jnp.float32),
-        ),
+        out_shape=(jax.ShapeDtypeStruct((3 * rows, features), jnp.bfloat16), own_z, own_back),
+        in_specs=[VMEM] * 2,
+        out_specs=(VMEM,) * 3,
+        compiler_params=PARAMS,
+        cost_estimate=cost(80 * rows * depth * features),
+    )(whole_p, own_r1_r2)
+    u_q, z_q, back_q = pl.pallas_call(
+        secondary_kernel,
+        out_shape=(jax.ShapeDtypeStruct((4 * rows, features), jnp.bfloat16), own_z, own_back),
         in_specs=[VMEM] * 3,
         out_specs=(VMEM,) * 3,
         compiler_params=PARAMS,
-        cost_estimate=cost(80 * rows * depth * features),
-    )(whole_p, own_r1_r2, r3)
+        cost_estimate=cost(24 * rows * depth * features),
+    )(whole_q, own_q, others)
     image_grad, text_grad, loss = pl.pallas_call(
-        main_kernel,
-        out_shape=(
-            jax.ShapeDtypeStruct((width, rows), jnp.bfloat16),
-            jax.ShapeDtypeStruct((width, rows), jnp.bfloat16),
-            jax.ShapeDtypeStruct((1, rows // groups), jnp.float32),
-        ),
-        in_specs=[SMEM] + [VMEM] * 7,
+        sides_kernel,
+        out_shape=(grad, grad, loss),
+        in_specs=[SMEM] + [VMEM] * 9,
         out_specs=(VMEM,) * 3,
         scratch_shapes=[
             pltpu.VMEM((4 * rows, features), jnp.bfloat16),
@@ -206,8 +239,8 @@
             pltpu.VMEM((2, 2 * LANES, rows), jnp.float32),
         ],
         compiler_params=PARAMS,
-        cost_estimate=cost(24 * rows * depth * features),
-    )(place, whole_q, own_q, others, whole_p, u_p, z_p, back_p)
+        cost_estimate=cost(12 * rows * depth * features),
+    )(place, whole_p, r3, u_p, z_p, back_p, whole_q, u_q, z_q, back_q)
     return image_grad.T, text_grad.T, loss.reshape(rows // groups)
 
 

time: 63.3 us -> 58.3 us (0.921)
  the two profiles are of different devices: /device:TPU:128 before, /device:TPU:1 now
where the time goes in v9:
time: 58.3 us; the launch traced here: 57.9 us
  starting transfers between devices  44 us (75%)
  Pallas kernels  10.8 us (19%)
  other arithmetic  1.41 us (2%)
  waiting for transfers between devices  0.9 us (2%)
  between operations  0.85 us (1%)
    ppermute x9, starting transfers between devices, permute(): return lax.ppermute(block, AXES, route)  44 us
    pallas_call x1, Pallas kernels, body(): pl.pallas_call(sides_kernel, out_shape=(grad, grad, loss), in_specs=[SMEM...  6.52 us
    pallas_call x1, Pallas kernels, body(): pl.pallas_call(secondary_kernel, out_shape=(jax.ShapeDtypeStruct((4 * row...  1.89 us
    pallas_call x1, Pallas kernels, body(): pl.pallas_call(primary_kernel, out_shape=(jax.ShapeDtypeStruct((3 * rows,...  1.56 us
    select_n x1, other arithmetic, body(): own_p = jnp.where(even, image_feats, text_feats)  1.3 us
  transfers between devices with their start and end apart: 9, of which 1 were waited for; matrix products, arithmetic and copies ran while one was open for 0% of the time, Pallas kernels for 7%

profile of v9, /device:TPU:1, one launch (start us, length us, event | category | flops | bytes accessed | tf_op | source)
XLA Modules:
  0.0 57.9 jit_solution(14510074855224959421)
XLA Ops:
  0.6 0.0 copy-start.1
  0.6 0.0 copy-start
  0.7 1.3 %broadcast_select_fusion = (bf16[320,768]{1,0:T(8,128)(2,1)S(1)}, bf16[320,768]{1,0:T(8,128)(2,1)S(1)}) fusion(bf16[320,768]{1,0:T(8,128)(2,1)} %param.4, bf16[320,768]{1,0:T(8,128)(2,1)} %param.5, pred[]{:T(512)S(6)} %eq.5), kind=kLoop, calls=%fused_computation | loop fusion | flops 491520 | bytes 1966081 | tf_op jit(solution)/shard_map/jit(_where)/select_n | solution.py:182
  2.0 4.5 %collective-permute-start.1 = (bf16[320,768]{1,0:T(8,128)(2,1)S(1)}, bf16[320,768]{1,0:T(8,128)(2,1)S(1)}, u32[]{:S(2)}, u32[]{:S(2)}) collective-permute-start(bf16[320,768]{1,0:T(8,128)(2,1)S(1)} %get-tuple-element.22.own), channel_id=1, source_target_pairs={{1020,0},{1021,1},{8,4},{9,5},{4,8},{5,9},{16,12},{17,13},{12,16},... | collective-permute-start | bytes 1474568 | tf_op jit(solution)/shard_map/ppermute | solution.py:178
  6.5 0.0 copy-done.1
  6.5 0.0 copy-done
  6.6 13.1 %collective-permute-start.2 = (bf16[192,768]{1,0:T(8,128)(2,1)S(1)}, bf16[192,768]{1,0:T(8,128)(2,1)S(1)}, u32[]{:S(2)}, u32[]{:S(2)}) collective-permute-start(bf16[192,768]{1,0:T(8,128)(2,1)S(1)} %select_bitcast_fusion.refs_0_), channel_id=1, source_target_pairs={{1,0},{2,1},{3,2},{0,3},{5,4},{6,5},{7,6},{4,7},{9,8},{10,9},{11,1... | collective-permute-start | bytes 884744 | tf_op jit(solution)/shard_map/ppermute | solution.py:178
  19.7 2.8 %collective-permute-start = (bf16[192,768]{1,0:T(8,128)(2,1)S(1)}, bf16[192,768]{1,0:T(8,128)(2,1)S(1)}, u32[]{:S(2)}, u32[]{:S(2)}) collective-permute-start(bf16[192,768]{1,0:T(8,128)(2,1)S(1)} %select_bitcast_fusion.refs_0_), channel_id=1, source_target_pairs={{515,0},{512,1},{513,2},{514,3},{519,4},{516,5},{517,6},{518,7},{5... | collective-permute-start | bytes 884744 | tf_op jit(solution)/shard_map/ppermute | solution.py:178
  22.5 0.7 %collective-permute-start.4 = (bf16[320,768]{1,0:T(8,128)(2,1)S(1)}, bf16[320,768]{1,0:T(8,128)(2,1)S(1)}, u32[]{:S(2)}, u32[]{:S(2)}) collective-permute-start(bf16[320,768]{1,0:T(8,128)(2,1)S(1)} %get-tuple-element.22.own), channel_id=1, source_target_pairs={{1022,2},{1023,3},{10,6},{11,7},{6,10},{7,11},{18,14},{19,15},{14,... | collective-permute-start | bytes 1474568 | tf_op jit(solution)/shard_map/ppermute | solution.py:178
  23.2 6.9 %collective-permute-start.6 = (bf16[320,768]{1,0:T(8,128)(2,1)S(1)}, bf16[320,768]{1,0:T(8,128)(2,1)S(1)}, u32[]{:S(2)}, u32[]{:S(2)}) collective-permute-start(bf16[320,768]{1,0:T(8,128)(2,1)S(1)} %get-tuple-element.21.refs_0_), channel_id=1, source_target_pairs={{1016,0},{1017,1},{1018,2},{1019,3},{12,4},{13,5},{14,6},{15,7},{0... | collective-permute-start | bytes 1474568 | tf_op jit(solution)/shard_map/ppermute | solution.py:178
  30.2 0.1 pad_add_fusion.place
  30.2 0.0 collective-permute-done.2.refs_1_
  30.2 0.0 collective-permute-done.1.refs_0_.early
  30.3 6.8 %collective-permute-start.3 = (bf16[192,768]{1,0:T(8,128)(2,1)S(1)}, bf16[192,768]{1,0:T(8,128)(2,1)S(1)}, u32[]{:S(2)}, u32[]{:S(2)}) collective-permute-start(bf16[192,768]{1,0:T(8,128)(2,1)S(1)} %shard_map.67.refs_2_._), channel_id=1, source_target_pairs={{515,0},{512,1},{513,2},{514,3},{519,4},{516,5},{517,6},{518,7},{5... | collective-permute-start | bytes 884744 | tf_op jit(solution)/shard_map/ppermute | solution.py:178
  37.1 0.0 collective-permute-done.4.late
  37.1 0.6 %shard_map.69.refs_1_ = bf16[320,768]{1,0:T(8,128)(2,1)S(1)} custom-call(s32[3]{0:T(128)S(1)} %pad_add_fusion.place, bf16[320,768]{1,0:T(8,128)(2,1)S(1)} %collective-permute-done.1.refs_0_.early, bf16[320,768]{1,0:T(8,128)(2,1)S(1)} %collective-permute-done.4.late, bf16[192,768]{1,0:T(8,128)(2,1)S(1)} %shard_map.67.refs_2_._), custom_call_target="tpu_custom_call" | custom-call | flops 20000000000 | bytes 1000000 | tf_op jit(solution)/shard_map/pallas_call | solution.py:197
  37.7 3.8 %collective-permute-start.5 = (bf16[320,768]{1,0:T(8,128)(2,1)S(1)}, bf16[320,768]{1,0:T(8,128)(2,1)S(1)}, u32[]{:S(2)}, u32[]{:S(2)}) collective-permute-start(bf16[320,768]{1,0:T(8,128)(2,1)S(1)} %shard_map.69.refs_1_), channel_id=1, source_target_pairs={{1016,0},{1017,1},{1018,2},{1019,3},{12,4},{13,5},{14,6},{15,7},{0... | collective-permute-start | bytes 1474568 | tf_op jit(solution)/shard_map/ppermute | solution.py:178
  41.5 0.0 collective-permute-done.6.refs_2_
  41.5 0.1 shard_map.70.blocks
  41.6 1.9 %collective-permute-start.8 = (bf16[960,768]{1,0:T(8,128)(2,1)S(1)}, bf16[960,768]{1,0:T(8,128)(2,1)S(1)}, u32[]{:S(2)}, u32[]{:S(2)}) collective-permute-start(bf16[960,768]{1,0:T(8,128)(2,1)S(1)} %shard_map.70.blocks), channel_id=1, source_target_pairs={{4,0},{5,1},{6,2},{7,3},{0,4},{1,5},{2,6},{3,7},{12,8},{13,9},{14,... | collective-permute-start | bytes 4423688 | tf_op jit(solution)/shard_map/ppermute | solution.py:178
  43.5 0.0 collective-permute-done.refs_1_
  43.5 0.0 collective-permute-done.3.refs_3_
  43.6 0.1 shard_map.68.whole.whole_p
  43.6 3.4 %collective-permute-start.7 = (bf16[768,768]{1,0:T(8,128)(2,1)S(1)}, bf16[768,768]{1,0:T(8,128)(2,1)S(1)}, u32[]{:S(2)}, u32[]{:S(2)}) collective-permute-start(bf16[768,768]{1,0:T(8,128)(2,1)S(1)} %shard_map.68.whole.whole_p), channel_id=1, source_target_pairs={{4,0},{5,1},{6,2},{7,3},{0,4},{1,5},{2,6},{3,7},{12,8},{13,9},{14,... | collective-permute-start | bytes 3538952 | tf_op jit(solution)/shard_map/ppermute | solution.py:178
  47.0 1.6 %shard_map.71 = (bf16[960,768]{1,0:T(8,128)(2,1)S(1)}, f32[320,768]{1,0:T(8,128)S(1)}, f32[320,1]{1,0:T(8,128)S(1)}) custom-call(bf16[768,768]{1,0:T(8,128)(2,1)S(1)} %shard_map.68.whole.whole_p, bf16[960,768]{1,0:T(8,128)(2,1)S(1)} %shard_map.70.blocks), custom_call_target="tpu_custom_call" | custom-call | flops 15099494400 | bytes 1000000 | tf_op jit(solution)/shard_map/pallas_call | solution.py:215
  48.6 0.9 %collective-permute-done.7.whole.whole_q = bf16[768,768]{1,0:T(8,128)(2,1)S(1)} collective-permute-done((bf16[768,768]{1,0:T(8,128)(2,1)S(1)}, bf16[768,768]{1,0:T(8,128)(2,1)S(1)}, u32[]{:S(2)}, u32[]{:S(2)}) %collective-permute-start.7) | collective-permute-done | bytes 1179680 | tf_op jit(solution)/shard_map/ppermute | solution.py:178
  49.5 0.0 collective-permute-done.8.others
  49.5 1.9 %shard_map.72 = (bf16[1280,768]{1,0:T(8,128)(2,1)S(1)}, f32[320,768]{1,0:T(8,128)S(1)}, f32[320,1]{1,0:T(8,128)S(1)}) custom-call(bf16[768,768]{1,0:T(8,128)(2,1)S(1)} %collective-permute-done.7.whole.whole_q, bf16[320,768]{1,0:T(8,128)(2,1)S(1)} %get-tuple-element.22.own, bf16[960,768]{1,0:T(8,128)(2,1)S(1)} %collective-permute-done.8.others), custom_call_target="tpu_custom_call" | custom-call | flops 4529848320 | bytes 1000000 | tf_op jit(solution)/shard_map/pallas_call | solution.py:223
  51.4 0.0 collective-permute-done.5.r3
  51.4 6.5 %shard_map.73 = (bf16[192,320]{1,0:T(8,128)(2,1)}, bf16[192,320]{1,0:T(8,128)(2,1)}, f32[1,80]{1,0:T(1,128)}) custom-call(s32[3]{0:T(128)S(1)} %pad_add_fusion.place, bf16[768,768]{1,0:T(8,128)(2,1)S(1)} %shard_map.68.whole.whole_p, bf16[320,768]{1,0:T(8,128)(2,1)S(1)} %collective-permute-done.5.r3, bf16[960,768]{1,0:T(8,128)(2,1)S(1)} %get-tuple-element.12.u_p3, ...), custom_call_target="tpu_custom_call" | custom-call | flops 2264924160 | bytes 1000000 | tf_op jit(solution)/shard_map/pallas_call | solution.py:231
  (2 shorter events, 0.1 us)
Async XLA Ops:
  0.6 5.9 %copy-start.1 = (bf16[768,192]{0,1:T(8,128)(2,1)S(1)}, bf16[768,192]{0,1:T(8,128)(2,1)}, u32[]{:S(2)}) copy-start(bf16[768,192]{0,1:T(8,128)(2,1)} %param.7) | copy-start | bytes 884740
  0.6 5.9 %copy-start = (bf16[768,192]{0,1:T(8,128)(2,1)S(1)}, bf16[768,192]{0,1:T(8,128)(2,1)}, u32[]{:S(2)}) copy-start(bf16[768,192]{0,1:T(8,128)(2,1)} %param.6) | copy-start | bytes 884740
  2.0 28.3 %collective-permute-start.1 = (bf16[320,768]{1,0:T(8,128)(2,1)S(1)}, bf16[320,768]{1,0:T(8,128)(2,1)S(1)}, u32[]{:S(2)}, u32[]{:S(2)}) collective-permute-start(bf16[320,768]{1,0:T(8,128)(2,1)S(1)} %get-tuple-element.22.own), channel_id=1, source_target_pairs={{1020,0},{1021,1},{8,4},{9,5},{4,8},{5,9},{16,12},{17,13},{12,16},... | collective-permute-start | bytes 1474568 | tf_op jit(solution)/shard_map/ppermute | solution.py:178
  6.6 23.7 %collective-permute-start.2 = (bf16[192,768]{1,0:T(8,128)(2,1)S(1)}, bf16[192,768]{1,0:T(8,128)(2,1)S(1)}, u32[]{:S(2)}, u32[]{:S(2)}) collective-permute-start(bf16[192,768]{1,0:T(8,128)(2,1)S(1)} %select_bitcast_fusion.refs_0_), channel_id=1, source_target_pairs={{1,0},{2,1},{3,2},{0,3},{5,4},{6,5},{7,6},{4,7},{9,8},{10,9},{11,1... | collective-permute-start | bytes 884744 | tf_op jit(solution)/shard_map/ppermute | solution.py:178
  19.7 23.9 %collective-permute-start = (bf16[192,768]{1,0:T(8,128)(2,1)S(1)}, bf16[192,768]{1,0:T(8,128)(2,1)S(1)}, u32[]{:S(2)}, u32[]{:S(2)}) collective-permute-start(bf16[192,768]{1,0:T(8,128)(2,1)S(1)} %select_bitcast_fusion.refs_0_), channel_id=1, source_target_pairs={{515,0},{512,1},{513,2},{514,3},{519,4},{516,5},{517,6},{518,7},{5... | collective-permute-start | bytes 884744 | tf_op jit(solution)/shard_map/ppermute | solution.py:178
  22.5 14.5 %collective-permute-start.4 = (bf16[320,768]{1,0:T(8,128)(2,1)S(1)}, bf16[320,768]{1,0:T(8,128)(2,1)S(1)}, u32[]{:S(2)}, u32[]{:S(2)}) collective-permute-start(bf16[320,768]{1,0:T(8,128)(2,1)S(1)} %get-tuple-element.22.own), channel_id=1, source_target_pairs={{1022,2},{1023,3},{10,6},{11,7},{6,10},{7,11},{18,14},{19,15},{14,... | collective-permute-start | bytes 1474568 | tf_op jit(solution)/shard_map/ppermute | solution.py:178
  23.2 18.3 %collective-permute-start.6 = (bf16[320,768]{1,0:T(8,128)(2,1)S(1)}, bf16[320,768]{1,0:T(8,128)(2,1)S(1)}, u32[]{:S(2)}, u32[]{:S(2)}) collective-permute-start(bf16[320,768]{1,0:T(8,128)(2,1)S(1)} %get-tuple-element.21.refs_0_), channel_id=1, source_target_pairs={{1016,0},{1017,1},{1018,2},{1019,3},{12,4},{13,5},{14,6},{15,7},{0... | collective-permute-start | bytes 1474568 | tf_op jit(solution)/shard_map/ppermute | solution.py:178
  30.3 13.3 %collective-permute-start.3 = (bf16[192,768]{1,0:T(8,128)(2,1)S(1)}, bf16[192,768]{1,0:T(8,128)(2,1)S(1)}, u32[]{:S(2)}, u32[]{:S(2)}) collective-permute-start(bf16[192,768]{1,0:T(8,128)(2,1)S(1)} %shard_map.67.refs_2_._), channel_id=1, source_target_pairs={{515,0},{512,1},{513,2},{514,3},{519,4},{516,5},{517,6},{518,7},{5... | collective-permute-start | bytes 884744 | tf_op jit(solution)/shard_map/ppermute | solution.py:178
  37.7 13.7 %collective-permute-start.5 = (bf16[320,768]{1,0:T(8,128)(2,1)S(1)}, bf16[320,768]{1,0:T(8,128)(2,1)S(1)}, u32[]{:S(2)}, u32[]{:S(2)}) collective-permute-start(bf16[320,768]{1,0:T(8,128)(2,1)S(1)} %shard_map.69.refs_1_), channel_id=1, source_target_pairs={{1016,0},{1017,1},{1018,2},{1019,3},{12,4},{13,5},{14,6},{15,7},{0... | collective-permute-start | bytes 1474568 | tf_op jit(solution)/shard_map/ppermute | solution.py:178
  41.6 7.9 %collective-permute-start.8 = (bf16[960,768]{1,0:T(8,128)(2,1)S(1)}, bf16[960,768]{1,0:T(8,128)(2,1)S(1)}, u32[]{:S(2)}, u32[]{:S(2)}) collective-permute-start(bf16[960,768]{1,0:T(8,128)(2,1)S(1)} %shard_map.70.blocks), channel_id=1, source_target_pairs={{4,0},{5,1},{6,2},{7,3},{0,4},{1,5},{2,6},{3,7},{12,8},{13,9},{14,... | collective-permute-start | bytes 4423688 | tf_op jit(solution)/shard_map/ppermute | solution.py:178
  43.6 5.8 %collective-permute-start.7 = (bf16[768,768]{1,0:T(8,128)(2,1)S(1)}, bf16[768,768]{1,0:T(8,128)(2,1)S(1)}, u32[]{:S(2)}, u32[]{:S(2)}) collective-permute-start(bf16[768,768]{1,0:T(8,128)(2,1)S(1)} %shard_map.68.whole.whole_p), channel_id=1, source_target_pairs={{4,0},{5,1},{6,2},{7,3},{0,4},{1,5},{2,6},{3,7},{12,8},{13,9},{14,... | collective-permute-start | bytes 3538952 | tf_op jit(solution)/shard_map/ppermute | solution.py:178

commit v10 on v9

--- a/solution.py
+++ b/solution.py
@@ -68,14 +68,8 @@
         at += block.shape[0]
 
 
-def either_kernel(place, early, late, _, out):
-    @pl.when(place[2] != 0)
-    def _():
-        out[...] = early[...]
-
-    @pl.when(place[2] == 0)
-    def _():
-        out[...] = late[...]
+def either_kernel(early, late, _, out):
+    out[...] = early[...] + late[...]
 
 
 def project_all(blocks, whole, u_out, z_out, back_out):
@@ -118,10 +112,10 @@
 
 
 def sides_kernel(
-    place, whole_p, r3, u_p3, z_p, back_p, whole_q, u_q, z_q, back_q, image_out, text_out, loss_out,
+    whole_p, r3, u_p3, z_p, back_p, whole_q, u_q, z_q, back_q, image_out, text_out, loss_out,
     u_p, logits_ref, grads,
 ):
-    group, swapped = place[0], place[1]
+    group, swapped = lax.axis_index("head"), lax.rem(lax.axis_index("blk"), 2)
     rows, width = image_out.shape[1], image_out.shape[0]
     start, offset = window(group, width)
     columns = pl.ds(start, grads.shape[1])
@@ -145,7 +139,6 @@
 
 ANY = pl.BlockSpec(memory_space=pl.ANY)
 VMEM = pl.BlockSpec(memory_space=pltpu.VMEM)
-SMEM = pl.BlockSpec(memory_space=pltpu.SMEM)
 PARAMS = pltpu.CompilerParams(vmem_limit_bytes=16 * 1024 * 1024)
 
 
@@ -171,13 +164,11 @@
     grid = Grid(lax.axis_size("blk"), groups)
     width = image_head.shape[1]
     features = width * groups
-    group = lax.axis_index("head")
-    place = jnp.stack([group, lax.axis_index("blk") % 2, group < groups // 2]).astype(jnp.int32)
 
     def permute(block, route):
         return lax.ppermute(block, AXES, route)
 
-    even = place[1] == 0
+    even = lax.axis_index("blk") % 2 == 0
     image_head, text_head = image_head.T, text_head.T
     own_p = jnp.where(even, image_feats, text_feats)
     own_q = jnp.where(even, text_feats, image_feats)
@@ -197,11 +188,11 @@
     r1 = pl.pallas_call(
         either_kernel,
         out_shape=jax.ShapeDtypeStruct((rows, depth), own_q.dtype),
-        in_specs=[SMEM, VMEM, VMEM, ANY],
+        in_specs=[VMEM, VMEM, ANY],
         out_specs=VMEM,
         compiler_params=PARAMS,
         cost_estimate=cost(PACK),
-    )(place, early_1, late_1, w2)
+    )(early_1, late_1, w2)
     r3 = permute(r1, two_on)
     own_r1_r2 = pack(own_p, r1, r2)
     others = permute(own_r1_r2, swap)
@@ -231,7 +222,7 @@
     image_grad, text_grad, loss = pl.pallas_call(
         sides_kernel,
         out_shape=(grad, grad, loss),
-        in_specs=[SMEM] + [VMEM] * 9,
+        in_specs=[VMEM] * 9,
         out_specs=(VMEM,) * 3,
         scratch_shapes=[
             pltpu.VMEM((4 * rows, features), jnp.bfloat16),
@@ -240,7 +231,7 @@
         ],
         compiler_params=PARAMS,
         cost_estimate=cost(12 * rows * depth * features),
-    )(place, whole_p, r3, u_p, z_p, back_p, whole_q, u_q, z_q, back_q)
+    )(whole_p, r3, u_p, z_p, back_p, whole_q, u_q, z_q, back_q)
     return image_grad.T, text_grad.T, loss.reshape(rows // groups)
 
 

time: 58.3 us -> 57.5 us (0.986)
  Pallas kernels: 10.8 us -> 9.51 us
    pallas_call x1, Pallas kernels: 6.52 us -> 5.87 us  [body(): pl.pallas_call(sides_kernel, out_shape=(grad, grad, loss), in_specs=[VMEM...]
  transfers between devices with their start and end apart: 9 -> 9, of which waited for: 1 -> 2; matrix products, arithmetic and copies ran while one was open for 0% -> 0% of each run, Pallas kernels for 7% -> 6%
where the time goes in v10:
time: 57.5 us; the launch traced here: 57.1 us
  starting transfers between devices  44.4 us (77%)
  Pallas kernels  9.51 us (17%)
  other arithmetic  1.34 us (2%)
  waiting for transfers between devices  1.03 us (2%)
  between operations  0.85 us (1%)
    ppermute x9, starting transfers between devices, permute(): return lax.ppermute(block, AXES, route)  44.4 us
    pallas_call x1, Pallas kernels, body(): pl.pallas_call(sides_kernel, out_shape=(grad, grad, loss), in_specs=[VMEM...  5.87 us
    pallas_call x1, Pallas kernels, body(): pl.pallas_call(secondary_kernel, out_shape=(jax.ShapeDtypeStruct((4 * row...  1.86 us
    pallas_call x1, Pallas kernels, body(): pl.pallas_call(primary_kernel, out_shape=(jax.ShapeDtypeStruct((3 * rows,...  1.53 us
    select_n x1, other arithmetic, body(): own_p = jnp.where(even, image_feats, text_feats)  1.3 us
  transfers between devices with their start and end apart: 9, of which 2 were waited for; matrix products, arithmetic and copies ran while one was open for 0% of the time, Pallas kernels for 6%

profile of v10, /device:TPU:1, one launch (start us, length us, event | category | flops | bytes accessed | tf_op | source)
XLA Modules:
  0.0 57.1 jit_solution(4313308685324813009)
XLA Ops:
  0.6 0.0 copy-start.1
  0.6 0.0 copy-start
  0.7 1.3 %broadcast_select_fusion = (bf16[320,768]{1,0:T(8,128)(2,1)S(1)}, bf16[320,768]{1,0:T(8,128)(2,1)S(1)}) fusion(bf16[320,768]{1,0:T(8,128)(2,1)} %param.4, bf16[320,768]{1,0:T(8,128)(2,1)} %param.5, pred[]{:T(512)S(6)} %eq.5), kind=kLoop, calls=%fused_computation | loop fusion | flops 491520 | bytes 1966081 | tf_op jit(solution)/shard_map/jit(_where)/select_n | solution.py:173
  2.0 4.5 %collective-permute-start.1 = (bf16[320,768]{1,0:T(8,128)(2,1)S(1)}, bf16[320,768]{1,0:T(8,128)(2,1)S(1)}, u32[]{:S(2)}, u32[]{:S(2)}) collective-permute-start(bf16[320,768]{1,0:T(8,128)(2,1)S(1)} %get-tuple-element.22.own), channel_id=1, source_target_pairs={{1020,0},{1021,1},{8,4},{9,5},{4,8},{5,9},{16,12},{17,13},{12,16},... | collective-permute-start | bytes 1474568 | tf_op jit(solution)/shard_map/ppermute | solution.py:169
  6.5 0.0 copy-done.1
  6.5 0.0 copy-done
  6.5 13.1 %collective-permute-start.2 = (bf16[192,768]{1,0:T(8,128)(2,1)S(1)}, bf16[192,768]{1,0:T(8,128)(2,1)S(1)}, u32[]{:S(2)}, u32[]{:S(2)}) collective-permute-start(bf16[192,768]{1,0:T(8,128)(2,1)S(1)} %select_bitcast_fusion.refs_0_), channel_id=1, source_target_pairs={{1,0},{2,1},{3,2},{0,3},{5,4},{6,5},{7,6},{4,7},{9,8},{10,9},{11,1... | collective-permute-start | bytes 884744 | tf_op jit(solution)/shard_map/ppermute | solution.py:169
  19.7 2.8 %collective-permute-start = (bf16[192,768]{1,0:T(8,128)(2,1)S(1)}, bf16[192,768]{1,0:T(8,128)(2,1)S(1)}, u32[]{:S(2)}, u32[]{:S(2)}) collective-permute-start(bf16[192,768]{1,0:T(8,128)(2,1)S(1)} %select_bitcast_fusion.refs_0_), channel_id=1, source_target_pairs={{515,0},{512,1},{513,2},{514,3},{519,4},{516,5},{517,6},{518,7},{5... | collective-permute-start | bytes 884744 | tf_op jit(solution)/shard_map/ppermute | solution.py:169
  22.5 0.7 %collective-permute-start.4 = (bf16[320,768]{1,0:T(8,128)(2,1)S(1)}, bf16[320,768]{1,0:T(8,128)(2,1)S(1)}, u32[]{:S(2)}, u32[]{:S(2)}) collective-permute-start(bf16[320,768]{1,0:T(8,128)(2,1)S(1)} %get-tuple-element.22.own), channel_id=1, source_target_pairs={{1022,2},{1023,3},{10,6},{11,7},{6,10},{7,11},{18,14},{19,15},{14,... | collective-permute-start | bytes 1474568 | tf_op jit(solution)/shard_map/ppermute | solution.py:169
  23.2 6.9 %collective-permute-start.6 = (bf16[320,768]{1,0:T(8,128)(2,1)S(1)}, bf16[320,768]{1,0:T(8,128)(2,1)S(1)}, u32[]{:S(2)}, u32[]{:S(2)}) collective-permute-start(bf16[320,768]{1,0:T(8,128)(2,1)S(1)} %get-tuple-element.21.refs_0_), channel_id=1, source_target_pairs={{1016,0},{1017,1},{1018,2},{1019,3},{12,4},{13,5},{14,6},{15,7},{0... | collective-permute-start | bytes 1474568 | tf_op jit(solution)/shard_map/ppermute | solution.py:169
  30.1 0.0 collective-permute-done.2.refs_1_
  30.2 0.0 collective-permute-done.1.refs_0_.early
  30.2 6.8 %collective-permute-start.3 = (bf16[192,768]{1,0:T(8,128)(2,1)S(1)}, bf16[192,768]{1,0:T(8,128)(2,1)S(1)}, u32[]{:S(2)}, u32[]{:S(2)}) collective-permute-start(bf16[192,768]{1,0:T(8,128)(2,1)S(1)} %shard_map.67.refs_2_._), channel_id=1, source_target_pairs={{515,0},{512,1},{513,2},{514,3},{519,4},{516,5},{517,6},{518,7},{5... | collective-permute-start | bytes 884744 | tf_op jit(solution)/shard_map/ppermute | solution.py:169
  37.0 0.0 collective-permute-done.4.late
  37.0 0.1 shard_map.69.refs_1_
  37.1 3.9 %collective-permute-start.5 = (bf16[320,768]{1,0:T(8,128)(2,1)S(1)}, bf16[320,768]{1,0:T(8,128)(2,1)S(1)}, u32[]{:S(2)}, u32[]{:S(2)}) collective-permute-start(bf16[320,768]{1,0:T(8,128)(2,1)S(1)} %shard_map.69.refs_1_), channel_id=1, source_target_pairs={{1016,0},{1017,1},{1018,2},{1019,3},{12,4},{13,5},{14,6},{15,7},{0... | collective-permute-start | bytes 1474568 | tf_op jit(solution)/shard_map/ppermute | solution.py:169
  41.0 0.0 collective-permute-done.6.refs_2_
  41.0 0.1 shard_map.70.blocks
  41.1 1.9 %collective-permute-start.8 = (bf16[960,768]{1,0:T(8,128)(2,1)S(1)}, bf16[960,768]{1,0:T(8,128)(2,1)S(1)}, u32[]{:S(2)}, u32[]{:S(2)}) collective-permute-start(bf16[960,768]{1,0:T(8,128)(2,1)S(1)} %shard_map.70.blocks), channel_id=1, source_target_pairs={{4,0},{5,1},{6,2},{7,3},{0,4},{1,5},{2,6},{3,7},{12,8},{13,9},{14,... | collective-permute-start | bytes 4423688 | tf_op jit(solution)/shard_map/ppermute | solution.py:169
  43.0 0.0 collective-permute-done.refs_1_
  43.0 0.1 collective-permute-done.3.refs_3_
  43.1 0.1 shard_map.68.whole.whole_p
  43.2 3.7 %collective-permute-start.7 = (bf16[768,768]{1,0:T(8,128)(2,1)S(1)}, bf16[768,768]{1,0:T(8,128)(2,1)S(1)}, u32[]{:S(2)}, u32[]{:S(2)}) collective-permute-start(bf16[768,768]{1,0:T(8,128)(2,1)S(1)} %shard_map.68.whole.whole_p), channel_id=1, source_target_pairs={{4,0},{5,1},{6,2},{7,3},{0,4},{1,5},{2,6},{3,7},{12,8},{13,9},{14,... | collective-permute-start | bytes 3538952 | tf_op jit(solution)/shard_map/ppermute | solution.py:169
  46.9 1.5 %shard_map.71 = (bf16[960,768]{1,0:T(8,128)(2,1)S(1)}, f32[320,768]{1,0:T(8,128)S(1)}, f32[320,1]{1,0:T(8,128)S(1)}) custom-call(bf16[768,768]{1,0:T(8,128)(2,1)S(1)} %shard_map.68.whole.whole_p, bf16[960,768]{1,0:T(8,128)(2,1)S(1)} %shard_map.70.blocks), custom_call_target="tpu_custom_call" | custom-call | flops 15099494400 | bytes 1000000 | tf_op jit(solution)/shard_map/pallas_call | solution.py:206
  48.5 0.9 %collective-permute-done.7.whole.whole_q = bf16[768,768]{1,0:T(8,128)(2,1)S(1)} collective-permute-done((bf16[768,768]{1,0:T(8,128)(2,1)S(1)}, bf16[768,768]{1,0:T(8,128)(2,1)S(1)}, u32[]{:S(2)}, u32[]{:S(2)}) %collective-permute-start.7) | collective-permute-done | bytes 1179680 | tf_op jit(solution)/shard_map/ppermute | solution.py:169
  49.4 0.0 collective-permute-done.8.others
  49.4 1.9 %shard_map.72 = (bf16[1280,768]{1,0:T(8,128)(2,1)S(1)}, f32[320,768]{1,0:T(8,128)S(1)}, f32[320,1]{1,0:T(8,128)S(1)}) custom-call(bf16[768,768]{1,0:T(8,128)(2,1)S(1)} %collective-permute-done.7.whole.whole_q, bf16[320,768]{1,0:T(8,128)(2,1)S(1)} %get-tuple-element.22.own, bf16[960,768]{1,0:T(8,128)(2,1)S(1)} %collective-permute-done.8.others), custom_call_target="tpu_custom_call" | custom-call | flops 4529848320 | bytes 1000000 | tf_op jit(solution)/shard_map/pallas_call | solution.py:214
  51.3 0.0 collective-permute-done.5.r3
  51.3 5.9 %shard_map.73 = (bf16[192,320]{1,0:T(8,128)(2,1)}, bf16[192,320]{1,0:T(8,128)(2,1)}, f32[1,80]{1,0:T(1,128)}) custom-call(bf16[768,768]{1,0:T(8,128)(2,1)S(1)} %shard_map.68.whole.whole_p, bf16[320,768]{1,0:T(8,128)(2,1)S(1)} %collective-permute-done.5.r3, bf16[960,768]{1,0:T(8,128)(2,1)S(1)} %get-tuple-element.12.u_p3, ...), custom_call_target="tpu_custom_call" | custom-call | flops 2264924160 | bytes 1000000 | tf_op jit(solution)/shard_map/pallas_call | solution.py:222
  (2 shorter events, 0.1 us)
Async XLA Ops:
  0.6 5.9 %copy-start.1 = (bf16[768,192]{0,1:T(8,128)(2,1)S(1)}, bf16[768,192]{0,1:T(8,128)(2,1)}, u32[]{:S(2)}) copy-start(bf16[768,192]{0,1:T(8,128)(2,1)} %param.7) | copy-start | bytes 884740
  0.6 5.9 %copy-start = (bf16[768,192]{0,1:T(8,128)(2,1)S(1)}, bf16[768,192]{0,1:T(8,128)(2,1)}, u32[]{:S(2)}) copy-start(bf16[768,192]{0,1:T(8,128)(2,1)} %param.6) | copy-start | bytes 884740
  2.0 28.2 %collective-permute-start.1 = (bf16[320,768]{1,0:T(8,128)(2,1)S(1)}, bf16[320,768]{1,0:T(8,128)(2,1)S(1)}, u32[]{:S(2)}, u32[]{:S(2)}) collective-permute-start(bf16[320,768]{1,0:T(8,128)(2,1)S(1)} %get-tuple-element.22.own), channel_id=1, source_target_pairs={{1020,0},{1021,1},{8,4},{9,5},{4,8},{5,9},{16,12},{17,13},{12,16},... | collective-permute-start | bytes 1474568 | tf_op jit(solution)/shard_map/ppermute | solution.py:169
  6.5 23.6 %collective-permute-start.2 = (bf16[192,768]{1,0:T(8,128)(2,1)S(1)}, bf16[192,768]{1,0:T(8,128)(2,1)S(1)}, u32[]{:S(2)}, u32[]{:S(2)}) collective-permute-start(bf16[192,768]{1,0:T(8,128)(2,1)S(1)} %select_bitcast_fusion.refs_0_), channel_id=1, source_target_pairs={{1,0},{2,1},{3,2},{0,3},{5,4},{6,5},{7,6},{4,7},{9,8},{10,9},{11,1... | collective-permute-start | bytes 884744 | tf_op jit(solution)/shard_map/ppermute | solution.py:169
  19.7 23.3 %collective-permute-start = (bf16[192,768]{1,0:T(8,128)(2,1)S(1)}, bf16[192,768]{1,0:T(8,128)(2,1)S(1)}, u32[]{:S(2)}, u32[]{:S(2)}) collective-permute-start(bf16[192,768]{1,0:T(8,128)(2,1)S(1)} %select_bitcast_fusion.refs_0_), channel_id=1, source_target_pairs={{515,0},{512,1},{513,2},{514,3},{519,4},{516,5},{517,6},{518,7},{5... | collective-permute-start | bytes 884744 | tf_op jit(solution)/shard_map/ppermute | solution.py:169
  22.5 14.5 %collective-permute-start.4 = (bf16[320,768]{1,0:T(8,128)(2,1)S(1)}, bf16[320,768]{1,0:T(8,128)(2,1)S(1)}, u32[]{:S(2)}, u32[]{:S(2)}) collective-permute-start(bf16[320,768]{1,0:T(8,128)(2,1)S(1)} %get-tuple-element.22.own), channel_id=1, source_target_pairs={{1022,2},{1023,3},{10,6},{11,7},{6,10},{7,11},{18,14},{19,15},{14,... | collective-permute-start | bytes 1474568 | tf_op jit(solution)/shard_map/ppermute | solution.py:169
  23.2 17.7 %collective-permute-start.6 = (bf16[320,768]{1,0:T(8,128)(2,1)S(1)}, bf16[320,768]{1,0:T(8,128)(2,1)S(1)}, u32[]{:S(2)}, u32[]{:S(2)}) collective-permute-start(bf16[320,768]{1,0:T(8,128)(2,1)S(1)} %get-tuple-element.21.refs_0_), channel_id=1, source_target_pairs={{1016,0},{1017,1},{1018,2},{1019,3},{12,4},{13,5},{14,6},{15,7},{0... | collective-permute-start | bytes 1474568 | tf_op jit(solution)/shard_map/ppermute | solution.py:169
  30.2 12.9 %collective-permute-start.3 = (bf16[192,768]{1,0:T(8,128)(2,1)S(1)}, bf16[192,768]{1,0:T(8,128)(2,1)S(1)}, u32[]{:S(2)}, u32[]{:S(2)}) collective-permute-start(bf16[192,768]{1,0:T(8,128)(2,1)S(1)} %shard_map.67.refs_2_._), channel_id=1, source_target_pairs={{515,0},{512,1},{513,2},{514,3},{519,4},{516,5},{517,6},{518,7},{5... | collective-permute-start | bytes 884744 | tf_op jit(solution)/shard_map/ppermute | solution.py:169
  37.1 14.2 %collective-permute-start.5 = (bf16[320,768]{1,0:T(8,128)(2,1)S(1)}, bf16[320,768]{1,0:T(8,128)(2,1)S(1)}, u32[]{:S(2)}, u32[]{:S(2)}) collective-permute-start(bf16[320,768]{1,0:T(8,128)(2,1)S(1)} %shard_map.69.refs_1_), channel_id=1, source_target_pairs={{1016,0},{1017,1},{1018,2},{1019,3},{12,4},{13,5},{14,6},{15,7},{0... | collective-permute-start | bytes 1474568 | tf_op jit(solution)/shard_map/ppermute | solution.py:169
  41.1 8.3 %collective-permute-start.8 = (bf16[960,768]{1,0:T(8,128)(2,1)S(1)}, bf16[960,768]{1,0:T(8,128)(2,1)S(1)}, u32[]{:S(2)}, u32[]{:S(2)}) collective-permute-start(bf16[960,768]{1,0:T(8,128)(2,1)S(1)} %shard_map.70.blocks), channel_id=1, source_target_pairs={{4,0},{5,1},{6,2},{7,3},{0,4},{1,5},{2,6},{3,7},{12,8},{13,9},{14,... | collective-permute-start | bytes 4423688 | tf_op jit(solution)/shard_map/ppermute | solution.py:169
  43.2 6.2 %collective-permute-start.7 = (bf16[768,768]{1,0:T(8,128)(2,1)S(1)}, bf16[768,768]{1,0:T(8,128)(2,1)S(1)}, u32[]{:S(2)}, u32[]{:S(2)}) collective-permute-start(bf16[768,768]{1,0:T(8,128)(2,1)S(1)} %shard_map.68.whole.whole_p), channel_id=1, source_target_pairs={{4,0},{5,1},{6,2},{7,3},{0,4},{1,5},{2,6},{3,7},{12,8},{13,9},{14,... | collective-permute-start | bytes 3538952 | tf_op jit(solution)/shard_map/ppermute | solution.py:169
